TPU v7x, 32 devices: a whole 2x2x4 slice. The times are simulated.
32 devices in a mesh: clip: 8 (over z, y), win: 4 (over x, core).
Axes of the slice: x: 2, y: 2, z: 4, core: 2. Of those that a mesh axis runs over, the one named last changes fastest.
Arguments:
- tokens: bfloat16 [16, 5120, 1024], P('clip', 'win'), may hold values from -6 to 6
- cotangent: bfloat16 [16, 5120, 1024], P('clip', 'win'), may hold values from -6 to 6
- modulation: float32 [16, 6, 1024], P('clip'), may hold values from -3 to 3
- text_features: bfloat16 [16, 77, 1024], P('clip'), may hold values from -6 to 6
- null_mask: int32 [16], P('clip'), may hold values 0 or 1
- null_text: bfloat16 [77, 1024], P(None, 'win'), may hold values from -6 to 6
- norm_gain: bfloat16 [1024], P('win'), may hold values from 0.5 to 1.5
- position_bias: float32 [16, 2025], P('win'), may hold values from -5 to 5
- self_input: bfloat16 [1024, 3072], P('clip', 'win'), may hold values from -0.1875 to 0.1875
- self_output: bfloat16 [1024, 1024], P('clip', 'win'), may hold values from -1.5 to 1.5
- cross_query: bfloat16 [1024, 1024], P('clip', 'win'), may hold values from -0.1875 to 0.1875
- cross_memory: bfloat16 [1024, 2048], P('clip', 'win'), may hold values from -0.1875 to 0.1875
- cross_output: bfloat16 [1024, 1024], P('clip', 'win'), may hold values from -1.5 to 1.5
- expand_weight: bfloat16 [1024, 4096], P('clip', 'win'), may hold values from -0.1875 to 0.1875
- reduce_weight: bfloat16 [4096, 1024], P('clip', 'win'), may hold values from -0.09375 to 0.09375
Outputs:
- block_output: bfloat16 [16, 5120, 1024], P('clip', 'win')
- tokens_grad: bfloat16 [16, 5120, 1024], P('clip', 'win')
- self_input_grad: float32 [1024, 3072], P('clip', 'win')
- self_output_grad: float32 [1024, 1024], P('clip', 'win')
- cross_query_grad: float32 [1024, 1024], P('clip', 'win')
- cross_memory_grad: float32 [1024, 2048], P('clip', 'win')
- cross_output_grad: float32 [1024, 1024], P('clip', 'win')
- expand_grad: float32 [1024, 4096], P('clip', 'win')
- reduce_grad: float32 [4096, 1024], P('clip', 'win')
- norm_gain_grad: float32 [1024], P('win')
- null_text_grad: float32 [77, 1024], P(None, 'win')
- position_bias_grad: float32 [16, 2025], P('win')
- modulation_grad: float32 [16, 6, 1024], P('clip', None, 'win')
Inputs may be any that keep to these rules, and one draw needn't show every extreme that they name: `null_mask`: 1 marks a clip whose text features are replaced by the null text.
All inputs are finite; a program needn't handle non-finite values. No bound on the sum of `null_mask` on one device may be relied on, other than what follows from the above.
Results may differ from a plain program's by a relative error of at most 0.02.
Values may be sent and summed in bfloat16 or wider, within the bound.
No kernel may reach another device: no remote copies, remote signals or barrier semaphores. Data moves between devices by JAX's collectives and lax.ppermute only.
A program may use at most 448 MiB of HBM per device.

v0:
```python
import jax
import jax.numpy as jnp
from jax import lax
from jax.sharding import PartitionSpec as P

HEADS = 16
HD = 64
FRAMES = 5
GRID = 32
WS = 8
SEQ = 5120
WIN_TOK = 320
NREL = 2025


epsilon = 1e-06
gelu_coefficient = 0.7978845608028654
group_windows = 4


def normalize(values):
    centered = values - jnp.mean(values, axis=-1, keepdims=True)
    variance = jnp.mean(centered * centered, axis=-1, keepdims=True)
    return centered * lax.rsqrt(variance + epsilon)


def adaptive_norm(values, shift_vector, scaling):
    return normalize(values) * (1.0 + scaling) + shift_vector


def gained_norm(values, gain_vector):
    return normalize(values) * gain_vector


def gelu_tanh(values):
    return (
        0.5
        * values
        * (1.0 + jnp.tanh(gelu_coefficient * (values + 0.044715 * values * values * values)))
    )


def softmax_last(scores):
    top_score = jnp.max(scores, axis=-1, keepdims=True)
    expanded = jnp.exp(scores - top_score)
    return expanded / jnp.sum(expanded, axis=-1, keepdims=True)


def offset_table(count):
    first = lax.broadcasted_iota(jnp.int32, (count, count, 2 * count - 1), 0)
    second = lax.broadcasted_iota(jnp.int32, (count, count, 2 * count - 1), 1)
    offset = lax.broadcasted_iota(jnp.int32, (count, count, 2 * count - 1), 2)
    return (first - second + count - 1 == offset).astype(jnp.float32)


def bias_lookup(position_bias, frame_hot, side_hot):
    heads_local = position_bias.shape[0]
    span_width = 2 * WS - 1
    highest = lax.Precision.HIGHEST
    table = position_bias.reshape(heads_local, 2 * FRAMES - 1, span_width, span_width)
    section_one = jnp.einsum("hfij,tuf->htuij", table, frame_hot, precision=highest)
    section_two = jnp.einsum("htuij,rpi->htrupj", section_one, side_hot, precision=highest)
    section_three = jnp.einsum("htrupj,sqj->htrsupq", section_two, side_hot, precision=highest)
    return section_three.reshape(heads_local, WIN_TOK, WIN_TOK)


def bias_collect(bias_sum, frame_hot, side_hot):
    heads_local = bias_sum.shape[0]
    highest = lax.Precision.HIGHEST
    spread = bias_sum.reshape(heads_local, FRAMES, WS, WS, FRAMES, WS, WS)
    section_one = jnp.einsum("htrsupq,sqj->htrupj", spread, side_hot, precision=highest)
    section_two = jnp.einsum("htrupj,rpi->htuij", section_one, side_hot, precision=highest)
    section_three = jnp.einsum("htuij,tuf->hfij", section_two, frame_hot, precision=highest)
    return section_three.reshape(heads_local, NREL)


def heads_to_windows(heads_array, heads_local):
    clip_count = heads_array.shape[0]
    blocks = GRID // WS
    reshaped = heads_array.reshape(clip_count, FRAMES, blocks, WS, blocks, WS, heads_local, HD)
    arranged = reshaped.transpose(0, 2, 4, 1, 3, 5, 6, 7)
    return arranged.reshape(-1, group_windows, WIN_TOK, heads_local, HD)


def windows_to_heads(grouped, clip_count):
    blocks = GRID // WS
    local_width = grouped.shape[3] * HD
    reshaped = grouped.reshape(clip_count, blocks, blocks, FRAMES, WS, WS, local_width)
    return reshaped.transpose(0, 3, 1, 4, 2, 5, 6).reshape(clip_count, SEQ, local_width)


def local(
    tokens,
    cotangent,
    modulation,
    text_features,
    null_mask,
    null_text,
    norm_gain,
    position_bias,
    self_input,
    self_output,
    cross_query,
    cross_memory,
    cross_output,
    expand_weight,
    reduce_weight,
):
    bfloat = jnp.bfloat16
    single = jnp.float32
    highest = lax.Precision.HIGHEST
    win_count = lax.axis_size("win")
    clip_count = tokens.shape[0]
    model_width = tokens.shape[2]
    heads_local = HEADS // win_count
    scale_factor = HD ** (-0.5)
    columns = (
        lax.all_gather(self_input, "win", axis=1, tiled=True),
        lax.all_gather(self_output, "win", axis=1, tiled=True),
        lax.all_gather(cross_query, "win", axis=1, tiled=True),
        lax.all_gather(cross_memory, "win", axis=1, tiled=True),
        lax.all_gather(cross_output, "win", axis=1, tiled=True),
        lax.all_gather(expand_weight, "win", axis=1, tiled=True),
        lax.all_gather(reduce_weight, "win", axis=1, tiled=True),
        lax.all_gather(norm_gain, "win", axis=0, tiled=True),
        lax.all_gather(null_text, "win", axis=1, tiled=True),
    )
    gathered = (
        lax.all_gather(columns[0], "clip", axis=0, tiled=True),
        lax.all_gather(columns[1], "clip", axis=0, tiled=True),
        lax.all_gather(columns[2], "clip", axis=0, tiled=True),
        lax.all_gather(columns[3], "clip", axis=0, tiled=True),
        lax.all_gather(columns[4], "clip", axis=0, tiled=True),
        lax.all_gather(columns[5], "clip", axis=0, tiled=True),
        lax.all_gather(columns[6], "clip", axis=0, tiled=True),
    )
    gain_full = columns[7]
    null_full = columns[8]
    input_full, output_full, query_full, memory_full, cross_out_full, expand_full, reduce_full = (
        gathered
    )
    shift_first = modulation[:, 0:1]
    scale_first = modulation[:, 1:2]
    gate_first = modulation[:, 2:3]
    shift_second = modulation[:, 3:4]
    scale_second = modulation[:, 4:5]
    gate_second = modulation[:, 5:6]
    tokens_single = tokens.astype(single)
    hidden_first, first_pull = jax.vjp(adaptive_norm, tokens_single, shift_first, scale_first)
    first_low = hidden_first.astype(bfloat)
    projected = jnp.dot(first_low, input_full, preferred_element_type=single).astype(bfloat)
    queries = projected[..., :model_width]
    keys_part = projected[..., model_width : 2 * model_width]
    values_part = projected[..., 2 * model_width :]
    head_queries, head_keys, head_values = (
        lax.all_to_all(queries, "win", split_axis=2, concat_axis=1, tiled=True),
        lax.all_to_all(keys_part, "win", split_axis=2, concat_axis=1, tiled=True),
        lax.all_to_all(values_part, "win", split_axis=2, concat_axis=1, tiled=True),
    )
    group_queries_all = heads_to_windows(head_queries, heads_local)
    group_keys_all = heads_to_windows(head_keys, heads_local)
    group_values_all = heads_to_windows(head_values, heads_local)
    frame_hot = offset_table(FRAMES)
    side_hot = offset_table(WS)
    bias_table = bias_lookup(position_bias, frame_hot, side_hot)

    def attend_group(group_items):
        group_queries, group_keys, group_values = group_items
        scores = (
            jnp.einsum("wqhd,wkhd->whqk", group_queries, group_keys, preferred_element_type=single)
            * scale_factor
            + bias_table[None]
        )
        top_score = jnp.max(scores, axis=-1, keepdims=True)
        expanded_scores = jnp.exp(scores - top_score)
        total_weight = jnp.sum(expanded_scores, axis=-1, keepdims=True)
        weights_low = (expanded_scores / total_weight).astype(bfloat)
        attended = jnp.einsum(
            "whqk,wkhd->wqhd", weights_low, group_values, preferred_element_type=single
        ).astype(bfloat)
        return (attended, top_score + jnp.log(total_weight))

    attended_groups, log_totals = lax.map(
        attend_group, (group_queries_all, group_keys_all, group_values_all)
    )
    attended_heads = windows_to_heads(attended_groups, clip_count)
    attended_tokens = lax.all_to_all(attended_heads, "win", split_axis=1, concat_axis=2, tiled=True)
    branch = jnp.dot(attended_tokens, output_full, preferred_element_type=single)
    first_sum = tokens_single + gate_first * branch
    hidden_second, second_pull = jax.vjp(gained_norm, first_sum, gain_full.astype(single))
    second_low = hidden_second.astype(bfloat)
    cross_queries = (
        jnp.dot(second_low, query_full, preferred_element_type=single)
        .astype(bfloat)
        .reshape(clip_count, -1, HEADS, HD)
    )
    null_flags = null_mask > 0
    used_text = jnp.where(null_flags[:, None, None], null_full[None], text_features)
    memory = jnp.dot(used_text, memory_full, preferred_element_type=single).astype(bfloat)
    cross_keys = memory[..., :model_width].reshape(clip_count, -1, HEADS, HD)
    cross_values = memory[..., model_width:].reshape(clip_count, -1, HEADS, HD)
    cross_scores = (
        jnp.einsum("cqhd,ckhd->chqk", cross_queries, cross_keys, preferred_element_type=single)
        * scale_factor
    )
    cross_probs = softmax_last(cross_scores)
    cross_low = cross_probs.astype(bfloat)
    cross_attended = (
        jnp.einsum("chqk,ckhd->cqhd", cross_low, cross_values, preferred_element_type=single)
        .astype(bfloat)
        .reshape(clip_count, -1, model_width)
    )
    second_sum = first_sum + jnp.dot(cross_attended, cross_out_full, preferred_element_type=single)
    hidden_third, third_pull = jax.vjp(adaptive_norm, second_sum, shift_second, scale_second)
    third_low = hidden_third.astype(bfloat)
    expanded = jnp.dot(third_low, expand_full, preferred_element_type=single)
    activated, gelu_pull = jax.vjp(gelu_tanh, expanded)
    activated_low = activated.astype(bfloat)
    reduced = jnp.dot(activated_low, reduce_full, preferred_element_type=single)
    block_output = (second_sum + gate_second * reduced).astype(bfloat)
    grad_output = cotangent.astype(single)
    grad_gate_second = jnp.sum(grad_output * reduced, axis=1, keepdims=True)
    grad_reduced = (gate_second * grad_output).astype(bfloat)
    reduce_term = jnp.einsum(
        "cnf,cnd->fd", activated_low, grad_reduced, preferred_element_type=single
    )
    grad_activated = jnp.dot(grad_reduced, reduce_full.T, preferred_element_type=single)
    grad_expanded = gelu_pull(grad_activated)[0].astype(bfloat)
    expand_term = jnp.einsum("cnd,cnf->df", third_low, grad_expanded, preferred_element_type=single)
    grad_third = jnp.dot(grad_expanded, expand_full.T, preferred_element_type=single)
    grad_second_norm, grad_shift_second, grad_scale_second = third_pull(grad_third)
    grad_second_sum = grad_output + grad_second_norm
    grad_cross = grad_second_sum.astype(bfloat)
    cross_output_term = jnp.einsum(
        "cnd,cne->de", cross_attended, grad_cross, preferred_element_type=single
    )
    grad_cross_attended = (
        jnp.dot(grad_cross, cross_out_full.T, preferred_element_type=single)
        .astype(bfloat)
        .reshape(clip_count, -1, HEADS, HD)
    )
    grad_cross_probs = jnp.einsum(
        "cqhd,ckhd->chqk", grad_cross_attended, cross_values, preferred_element_type=single
    )
    grad_cross_scores = (
        cross_probs
        * (grad_cross_probs - jnp.sum(cross_probs * grad_cross_probs, axis=-1, keepdims=True))
    ).astype(bfloat)
    grad_cross_queries = (
        (
            jnp.einsum(
                "chqk,ckhd->cqhd", grad_cross_scores, cross_keys, preferred_element_type=single
            )
            * scale_factor
        )
        .astype(bfloat)
        .reshape(clip_count, -1, model_width)
    )
    grad_cross_keys = (
        jnp.einsum(
            "chqk,cqhd->ckhd", grad_cross_scores, cross_queries, preferred_element_type=single
        )
        * scale_factor
    )
    grad_cross_values = jnp.einsum(
        "chqk,cqhd->ckhd", cross_low, grad_cross_attended, preferred_element_type=single
    )
    grad_memory = jnp.concatenate(
        [
            grad_cross_keys.reshape(clip_count, -1, model_width),
            grad_cross_values.reshape(clip_count, -1, model_width),
        ],
        axis=-1,
    )
    memory_term = jnp.einsum(
        "ctd,cte->de", used_text.astype(single), grad_memory, precision=highest
    )
    masked_memory = jnp.sum(jnp.where(null_flags[:, None, None], grad_memory, 0.0), axis=0)
    null_term = jnp.dot(
        masked_memory, memory_full.T, precision=highest, preferred_element_type=single
    )
    query_term = jnp.einsum(
        "cnd,cne->de", second_low, grad_cross_queries, preferred_element_type=single
    )
    grad_second = jnp.dot(grad_cross_queries, query_full.T, preferred_element_type=single)
    grad_first_norm, gain_term = second_pull(grad_second)
    grad_first_sum = grad_second_sum + grad_first_norm
    grad_gate_first = jnp.sum(grad_first_sum * branch, axis=1, keepdims=True)
    grad_branch = (gate_first * grad_first_sum).astype(bfloat)
    output_term = jnp.einsum(
        "cnd,cne->de", attended_tokens, grad_branch, preferred_element_type=single
    )
    grad_attended = jnp.dot(grad_branch, output_full.T, preferred_element_type=single).astype(
        bfloat
    )
    grad_heads = lax.all_to_all(grad_attended, "win", split_axis=2, concat_axis=1, tiled=True)
    grad_groups = heads_to_windows(grad_heads, heads_local)

    def back_group(bias_sum, group_items):
        group_queries, group_keys, group_values, group_totals, group_grad = group_items
        scores = (
            jnp.einsum("wqhd,wkhd->whqk", group_queries, group_keys, preferred_element_type=single)
            * scale_factor
            + bias_table[None]
        )
        probability = jnp.exp(scores - group_totals)
        grad_probability = jnp.einsum(
            "wqhd,wkhd->whqk", group_grad, group_values, preferred_element_type=single
        )
        grad_scores = (
            probability
            * (grad_probability - jnp.sum(probability * grad_probability, axis=-1, keepdims=True))
        ).astype(bfloat)
        query_back = (
            jnp.einsum("whqk,wkhd->wqhd", grad_scores, group_keys, preferred_element_type=single)
            * scale_factor
        ).astype(bfloat)
        key_back = (
            jnp.einsum("whqk,wqhd->wkhd", grad_scores, group_queries, preferred_element_type=single)
            * scale_factor
        ).astype(bfloat)
        value_back = jnp.einsum(
            "whqk,wqhd->wkhd", probability.astype(bfloat), group_grad, preferred_element_type=single
        ).astype(bfloat)
        return (
            bias_sum + jnp.sum(grad_scores.astype(single), axis=0),
            (query_back, key_back, value_back),
        )

    bias_start = jnp.zeros((heads_local, WIN_TOK, WIN_TOK), single)
    bias_sum, back_groups = lax.scan(
        back_group,
        bias_start,
        (group_queries_all, group_keys_all, group_values_all, log_totals, grad_groups),
    )
    position_term = bias_collect(bias_sum, frame_hot, side_hot)
    query_tokens, key_tokens, value_tokens = (
        lax.all_to_all(
            windows_to_heads(back_groups[0], clip_count),
            "win",
            split_axis=1,
            concat_axis=2,
            tiled=True,
        ),
        lax.all_to_all(
            windows_to_heads(back_groups[1], clip_count),
            "win",
            split_axis=1,
            concat_axis=2,
            tiled=True,
        ),
        lax.all_to_all(
            windows_to_heads(back_groups[2], clip_count),
            "win",
            split_axis=1,
            concat_axis=2,
            tiled=True,
        ),
    )
    grad_projected = jnp.concatenate([query_tokens, key_tokens, value_tokens], axis=-1)
    input_term = jnp.einsum("cnd,cne->de", first_low, grad_projected, preferred_element_type=single)
    grad_first = jnp.dot(grad_projected, input_full.T, preferred_element_type=single)
    grad_tokens_norm, grad_shift_first, grad_scale_first = first_pull(grad_first)
    tokens_grad = (grad_first_sum + grad_tokens_norm).astype(bfloat)
    modulation_term = jnp.concatenate(
        [
            grad_shift_first,
            grad_scale_first,
            grad_gate_first,
            grad_shift_second,
            grad_scale_second,
            grad_gate_second,
        ],
        axis=1,
    )
    by_rows = (
        lax.psum_scatter(
            input_term.astype(jnp.bfloat16), "clip", scatter_dimension=0, tiled=True
        ).astype(jnp.float32),
        lax.psum_scatter(
            output_term.astype(jnp.bfloat16), "clip", scatter_dimension=0, tiled=True
        ).astype(jnp.float32),
        lax.psum_scatter(
            query_term.astype(jnp.bfloat16), "clip", scatter_dimension=0, tiled=True
        ).astype(jnp.float32),
        lax.psum_scatter(
            memory_term.astype(jnp.bfloat16), "clip", scatter_dimension=0, tiled=True
        ).astype(jnp.float32),
        lax.psum_scatter(
            cross_output_term.astype(jnp.bfloat16), "clip", scatter_dimension=0, tiled=True
        ).astype(jnp.float32),
        lax.psum_scatter(
            expand_term.astype(jnp.bfloat16), "clip", scatter_dimension=0, tiled=True
        ).astype(jnp.float32),
        lax.psum_scatter(
            reduce_term.astype(jnp.bfloat16), "clip", scatter_dimension=0, tiled=True
        ).astype(jnp.float32),
    )
    by_columns = (
        lax.psum_scatter(
            by_rows[0].astype(jnp.bfloat16), "win", scatter_dimension=1, tiled=True
        ).astype(jnp.float32),
        lax.psum_scatter(
            by_rows[1].astype(jnp.bfloat16), "win", scatter_dimension=1, tiled=True
        ).astype(jnp.float32),
        lax.psum_scatter(
            by_rows[2].astype(jnp.bfloat16), "win", scatter_dimension=1, tiled=True
        ).astype(jnp.float32),
        lax.psum_scatter(
            by_rows[3].astype(jnp.bfloat16), "win", scatter_dimension=1, tiled=True
        ).astype(jnp.float32),
        lax.psum_scatter(
            by_rows[4].astype(jnp.bfloat16), "win", scatter_dimension=1, tiled=True
        ).astype(jnp.float32),
        lax.psum_scatter(
            by_rows[5].astype(jnp.bfloat16), "win", scatter_dimension=1, tiled=True
        ).astype(jnp.float32),
        lax.psum_scatter(
            by_rows[6].astype(jnp.bfloat16), "win", scatter_dimension=1, tiled=True
        ).astype(jnp.float32),
        lax.psum_scatter(
            gain_term.astype(jnp.bfloat16), "win", scatter_dimension=0, tiled=True
        ).astype(jnp.float32),
        lax.psum_scatter(
            null_term.astype(jnp.bfloat16), "win", scatter_dimension=1, tiled=True
        ).astype(jnp.float32),
        lax.psum_scatter(
            modulation_term.astype(jnp.bfloat16), "win", scatter_dimension=2, tiled=True
        ).astype(jnp.float32),
    )
    weight_grads = by_columns[:7]
    gain_local = by_columns[7]
    null_local = by_columns[8]
    modulation_grad = by_columns[9]
    gain_grad, null_grad, position_grad = (
        lax.psum(gain_local.astype(jnp.bfloat16), "clip").astype(jnp.float32),
        lax.psum(null_local.astype(jnp.bfloat16), "clip").astype(jnp.float32),
        lax.psum(position_term.astype(jnp.bfloat16), "clip").astype(jnp.float32),
    )
    return (
        block_output,
        tokens_grad,
        weight_grads[0],
        weight_grads[1],
        weight_grads[2],
        weight_grads[3],
        weight_grads[4],
        weight_grads[5],
        weight_grads[6],
        gain_grad,
        null_grad,
        position_grad,
        modulation_grad,
    )


def solution(mesh):
    in_specs = (
        P("clip", "win", None),
        P("clip", "win", None),
        P("clip", None, None),
        P("clip", None, None),
        P("clip"),
        P(None, "win"),
        P("win"),
        P("win", None),
        P("clip", "win"),
        P("clip", "win"),
        P("clip", "win"),
        P("clip", "win"),
        P("clip", "win"),
        P("clip", "win"),
        P("clip", "win"),
    )
    out_specs = (
        P("clip", "win", None),
        P("clip", "win", None),
        P("clip", "win"),
        P("clip", "win"),
        P("clip", "win"),
        P("clip", "win"),
        P("clip", "win"),
        P("clip", "win"),
        P("clip", "win"),
        P("win"),
        P(None, "win"),
        P("win", None),
        P("clip", None, "win"),
    )
    return jax.shard_map(local, mesh=mesh, in_specs=in_specs, out_specs=out_specs, check_vma=False)
```

profile of v0, /device:TPU:0, one launch (start us, length us, event | category | flops | bytes accessed | tf_op | source)
XLA Modules:
  0.0 2195.5 jit_solution(9009522845391060318)
XLA Ops:
  7.2 11.7 all_gather.48
  42.8 75.6 %all-gather.11.cloned.1.call-done = bf16[1024,3072]{1,0:T(8,128)(2,1)} async-done(((bf16[128,3072]{1,0:T(8,128)(2,1)}), bf16[1024,3072]{1,0:T(8,128)(2,1)}) %all-gather.11.cloned.1.call-update) | async-done | bytes 6291472 | tf_op jit(solution)/shard_map/all_gather | solution.py:129
  118.5 21.7 convolution_convert_fusion
  146.5 13.8 copy.160
  165.6 61.9 %all_gather.50 = bf16[128,1024]{0,1:T(8,128)(2,1)} all-gather(bf16[128,256]{0,1:T(8,128)(2,1)S(1)} %copy.174), channel_id=1, replica_groups=mesh['clip'=8,'win'=4] {'win'}, dimensions={1}, use_global_device_ids=true | all-gather | bytes 327680 | tf_op jit(solution)/shard_map/all_gather | solution.py:119
  227.5 13.9 copy.157
  246.6 61.9 %all_gather.56 = bf16[128,1024]{0,1:T(8,128)(2,1)} all-gather(bf16[128,256]{0,1:T(8,128)(2,1)S(1)} %copy.176), channel_id=1, replica_groups=mesh['clip'=8,'win'=4] {'win'}, dimensions={1}, use_global_device_ids=true | all-gather | bytes 327680 | tf_op jit(solution)/shard_map/all_gather | solution.py:120
  308.5 13.8 copy.154
  327.5 61.9 %all_gather.58 = bf16[128,1024]{0,1:T(8,128)(2,1)} all-gather(bf16[128,256]{0,1:T(8,128)(2,1)S(1)} %copy.180), channel_id=1, replica_groups=mesh['clip'=8,'win'=4] {'win'}, dimensions={1}, use_global_device_ids=true | all-gather | bytes 327680 | tf_op jit(solution)/shard_map/all_gather | solution.py:122
  391.9 31.6 %convolution_bitcast_fusion = f32[4,5,8,8,5,8,8]{5,6,4,2,1,0,3:T(8,128)} fusion(f32[8,8,4,5,5,15]{5,1,4,0,3,2:T(8,128)S(1)} %fusion.134), kind=kOutput, calls=%fused_computation.97 | convolution fusion | flops 73730880 | bytes 2022400 | tf_op jit(solution)/shard_map/htrupj,sqj->htrsupq/dot_general | solution.py:63
  423.4 31.8 %copy.168 = f32[4,5,8,8,5,8,8]{3,2,1,6,5,4,0:T(8,128)} copy(f32[4,5,8,8,5,8,8]{5,6,4,2,1,0,3:T(8,128)} %convolution_bitcast_fusion) | data formatting | bytes 3276800 | tf_op jit(solution)/shard_map/while | solution.py:183
  455.2 15.5 add.330
  470.8 13.7 copy.161
  484.5 16.0 reshape.237
  511.4 12.1 copy.167
  523.5 13.5 copy.158
  537.1 16.1 reshape.235
  564.2 11.8 copy.166
  576.0 13.5 copy.155
  589.6 16.0 reshape.233
  616.5 11.7 copy.165
  631.9 72.6 %while.31 = (s32[]{:T(128)}, bf16[8,4,320,4,64]{2,4,3,1,0:T(8,128)(2,1)}, f32[8,4,4,320,1]{3,2,1,4,0:T(4,128)}, bf16[8,4,320,4,64]{2,4,3,1,0:T(8,128)(2,1)}, bf1...) while((s32[]{:T(128)}, ...), condition=%wide.wide.region_5.6_spmd, body=%wide.wide.region_2.5_spmd.sunk | while | flops 439413760 | bytes 27891816 | solution.py:183
  704.5 18.0 copy.169
  722.5 16.1 reshape.240
  741.7 33.8 %copy.171 = bf16[2,5120,256]{2,0,1:T(2,128)(2,1)} copy(bf16[2,5120,256]{2,1,0:T(8,128)(2,1)S(1)} %bitcast.392) | data formatting | bytes 10485760 | tf_op jit(solution)/shard_map/reshape | solution.py:89
  781.6 59.4 %all-gather = bf16[4,1,256]{2,1,0:T(2,128)(2,1)S(1)} all-gather(bf16[1,1,256]{2,1,0:T(2,128)(2,1)S(1)} %reshape.263), channel_id=1, replica_groups=mesh['clip'=8,'win'=4] {'win'}, dimensions={0}, use_global_device_ids=true | all-gather | bytes 2560 | tf_op jit(solution)/shard_map/all_gather | solution.py:125
  865.3 12.2 fusion.161
  893.5 11.4 fusion.164
  929.5 31.6 %fusion.84 = f32[2,1280,4096]{2,1,0:T(8,128)} fusion(bf16[1024,4096]{1,0:T(8,128)(2,1)} %all-gather.23.cloned.1.call-done, f32[2,1280,1024]{1,2,0:T(8,128)} %copy-done.7, f32[2,1024]{1,0:T(2,128)S(1)} %copy-done.57, f32[2,1024]{1,0:T(2,128)S(1)} %copy-done.49, f32[2,1280]{1,0:T(2,128)S(1)} %fusion.151, f32[2,1280]{1,0:T(2,128)S(1)} %broadcast_multiply_fusion), kind=kOutput, calls=%fused_computation.125 | convolution fusion | flops 21487943680 | bytes 60854272 | tf_op jit(solution)/shard_map/dot_general | solution.py:216
  961.1 62.9 %fusion.58 = bf16[2,1280,4096]{2,1,0:T(8,128)(2,1)} fusion(f32[2,1280,4096]{2,1,0:T(8,128)} %fusion.84, bf16[4096,1024]{1,0:T(8,128)(2,1)} %all-gather.27.cloned.1.call-done, bf16[2,1280,1024]{1,2,0:T(8,128)(2,1)} %copy.184, f32[2,1024]{1,0:T(2,128)S(1)} %copy-done.61), kind=kOutput, calls=%fused_computation.67 | convolution fusion | flops 21734359040 | bytes 76554240 | tf_op jit(solution)/shard_map/dot_general | solution.py:227
  1024.0 27.0 %fusion.167 = (bf16[2,1024]{1,0:T(2,128)(2,1)}, f32[2,1280,1024]{2,1,0:T(8,128)}) fusion(bf16[2,1280,4096]{2,1,0:T(8,128)(2,1)} %fusion.58, bf16[1024,4096]{1,0:T(8,128)(2,1)S(1)} %copy-done.66), kind=kOutput, calls=%fused_computation.236 | convolution fusion | flops 21477455872 | bytes 39849984 | tf_op jit(solution)/shard_map/dot_general | solution.py:230
  1071.7 47.5 %fusion.78 = (bf16[2,1024]{1,0:T(2,128)(2,1)}, bf16[2,1280,1024]{1,2,0:T(8,128)(2,1)}, f32[2,1280]{1,0:T(2,128)S(1)}, f32[2,1280,1024]{1,2,0:T(8,128)}) fusion(bf16[2,1280,1024]{1,2,0:T(8,128)(2,1)S(1)} %bitcast.379, f32[2,1280,1024]{1,2,0:T(8,128)} %copy-done.7, f32[2,1024]{1,0:T(2,128)S(1)} %copy-done.61, f32[2,1280]{1,0:T(2,128)S(1)} %multiply_multiply_fusion.4, ...), kind=kOutput, calls=%fused_computation.104 | convolution fusion | flops 21603282944 | bytes 92336128 | tf_op jit(solution)/shard_map/dot_general | solution.py:219
  1148.8 13.3 multiply_reduce_fusion.1
  1178.5 11.9 multiply_reduce_fusion.6
  1205.9 17.4 multiply_reduce_fusion.4
  1255.7 35.4 %bitcast_convert_fusion = bf16[4096,1024]{1,0:T(8,128)(2,1)} fusion(bf16[2,1280,1024]{1,2,0:T(8,128)(2,1)} %copy.184, f32[2,1024]{1,0:T(2,128)S(1)} %copy-done.61, f32[2,1280,4096]{2,1,0:T(8,128)} %fusion.84), kind=kOutput, calls=%fused_computation.73 | convolution fusion | flops 21581266944 | bytes 55582720 | tf_op jit(solution)/shard_map/cnf,cnd->fd/dot_general | solution.py:224
  1292.7 11.9 convolution_convert_fusion.2
  1304.6 13.7 copy.196
  1323.5 15.9 add.340
  1339.4 29.7 %bitcast_convert_fusion.1 = bf16[1024,4096]{1,0:T(8,128)(2,1)} fusion(bf16[2,1280,4096]{2,1,0:T(8,128)(2,1)} %fusion.58, f32[2,1280,1024]{1,2,0:T(8,128)} %copy-done.7, f32[2,1024]{1,0:T(2,128)S(1)} %copy-done.58, f32[2,1024]{1,0:T(2,128)S(1)} %copy-done.50, f32[2,1280]{1,0:T(2,128)S(1)} %copy-done.45, f32[2,1280]{1,0:T(2,128)S(1)} %copy-done.31), kind=kOutput, calls=%fused_computation.74 | convolution fusion | flops 21492137984 | bytes 39882752 | tf_op jit(solution)/shard_map/cnd,cnf->df/dot_general | solution.py:229
  1369.1 13.7 all-to-all-done.4
  1382.9 13.6 copy.197
  1396.5 16.0 reshape.248
  1423.7 11.8 copy.202
  1446.7 167.9 %while.32 = (s32[]{:T(128)}, f32[4,320,320]{1,2,0:T(8,128)}, bf16[8,4,320,4,64]{2,4,3,1,0:T(8,128)(2,1)}, bf16[8,4,320,4,64]{2,4,3,1,0:T(8,128)(2,1)}, bf16[8,4,...) while((s32[]{:T(128)}, f32[4,320,320]{1,2,0:T(8,128)}, ...), condition=%wide.wide.region_20.21_spmd.clone, body=%wide.wide.region_17.20_spmd.clone.sunk | while | flops 1078471680 | bytes 81741008 | solution.py:331
  1614.6 18.2 copy.214
  1632.8 15.9 reshape.254
  1651.9 34.0 %copy.216 = bf16[2,5120,256]{2,0,1:T(2,128)(2,1)} copy(bf16[2,5120,256]{2,1,0:T(8,128)(2,1)S(1)} %bitcast.394) | data formatting | bytes 10485760 | tf_op jit(solution)/shard_map/reshape | solution.py:89
  1690.9 18.1 copy.204
  1709.0 15.8 reshape.250
  1728.0 33.8 %copy.206 = bf16[2,5120,256]{2,0,1:T(2,128)(2,1)} copy(bf16[2,5120,256]{2,1,0:T(8,128)(2,1)S(1)} %bitcast.395) | data formatting | bytes 10485760 | tf_op jit(solution)/shard_map/reshape | solution.py:89
  1767.1 18.0 copy.209
  1785.1 15.7 reshape.252
  1804.0 33.8 %copy.211 = bf16[2,5120,256]{2,0,1:T(2,128)(2,1)} copy(bf16[2,5120,256]{2,1,0:T(8,128)(2,1)S(1)} %bitcast.396) | data formatting | bytes 10485760 | tf_op jit(solution)/shard_map/reshape | solution.py:89
  1865.6 39.1 %all-to-all-done.6 = bf16[2,5120,256]{2,0,1:T(2,128)(2,1)} async-done(((bf16[2,5120,256]{2,0,1:T(2,128)(2,1)}), bf16[2,5120,256]{2,0,1:T(2,128)(2,1)}, u32[]{:S(2)}, u32[]{:S(2)}) %all-to-all-start.6) | async-done | bytes 5242912 | tf_op jit(solution)/shard_map/all_to_all | solution.py:345
  1915.0 21.1 bitcast_convert_fusion.2
  1936.3 22.7 %fusion.166 = (bf16[2,1024]{1,0:T(2,128)(2,1)S(1)}, f32[2,1280,1024]{2,1,0:T(8,128)}) fusion(bf16[2,1280,3072]{2,1,0:T(8,128)(2,1)} %constant_dynamic-update-slice_fusion, bf16[1024,3072]{1,0:T(8,128)(2,1)} %all-gather.11.cloned.1.call-done), kind=kOutput, calls=%fused_computation.235 | convolution fusion | flops 16108746752 | bytes 32509952 | tf_op jit(solution)/shard_map/dot_general | solution.py:362
  2008.0 12.7 reshape.258
  2021.0 15.5 fusion.115
  2039.5 35.5 %all-reduce.1 = (bf16[256]{0:T(256)(128)(2,1)S(1)}, bf16[77,256]{1,0:T(8,128)(2,1)S(1)}, bf16[4,2025]{1,0:T(4,128)(2,1)S(1)}) all-reduce(bf16[256]{0:T(256)(128)(2,1)S(1)} %dynamic-slice.1, bf16[77,256]{1,0:T(8,128)(2,1)} %reduce-scatter.47.cloned.1.call-done, ...), channel_id=1, replica_groups=mesh['clip'=8,'win'=4] {'clip'}, use_global_device_ids=true, to_apply=%region_39.40 | all-reduce | flops 28068 | bytes 112272 | tf_op jit(solution)/shard_map/psum | solution.py:436
  2081.4 12.5 add_convert_fusion
  2107.9 25.9 %reduce-scatter.45.cloned.1.call-done = bf16[512,256]{1,0:T(8,128)(2,1)} async-done(((bf16[512,1024]{1,0:T(8,128)(2,1)}), bf16[512,256]{1,0:T(8,128)(2,1)}) %reduce-scatter.45.cloned.1.call-update) | async-done | bytes 262160 | tf_op jit(solution)/shard_map/reduce_scatter | solution.py:418
  2135.5 25.7 %reduce-scatter.41.cloned.1.call-done = bf16[128,1024]{1,0:T(8,128)(2,1)} async-done(((bf16[128,4096]{1,0:T(8,128)(2,1)}), bf16[128,1024]{1,0:T(8,128)(2,1)}) %reduce-scatter.41.cloned.1.call-update) | async-done | bytes 262160 | tf_op jit(solution)/shard_map/reduce_scatter | solution.py:415
  2163.1 24.0 %reduce-scatter.21.cloned.1.call-done = bf16[128,768]{1,0:T(8,128)(2,1)} async-done(((bf16[128,3072]{1,0:T(8,128)(2,1)}), bf16[128,768]{1,0:T(8,128)(2,1)}) %reduce-scatter.21.cloned.1.call-update) | async-done | bytes 196624 | tf_op jit(solution)/shard_map/reduce_scatter | solution.py:400
  (498 shorter events, 676.4 us)
Async XLA Ops:
  7.2 29.3 %copy-start.43 = (f32[2,6,1024]{2,0,1:T(2,128)S(1)}, f32[2,6,1024]{2,0,1:T(2,128)}, u32[]{:S(2)}) copy-start(f32[2,6,1024]{2,0,1:T(2,128)} %param.21) | copy-start | bytes 147460
  7.2 111.3 %all-gather.11.cloned.1.call-start = ((), (), s32[]{:S(2)}) async-start(), calls=%async_computation.24 | async-start | bytes 7077888 | tf_op jit(solution)/shard_map/all_gather | solution.py:129
  18.9 451.8 %all-gather.21.cloned.1.call-start = ((), (), s32[]{:S(2)}) async-start(), calls=%async_computation.29 | async-start | bytes 1310720 | tf_op jit(solution)/shard_map/all_gather | solution.py:123
  19.7 761.1 %all-gather.25.cloned.1.call-start = ((), (), s32[]{:S(2)}) async-start(), calls=%async_computation.31 | async-start | bytes 1310720 | tf_op jit(solution)/shard_map/all_gather | solution.py:124
  20.4 834.5 %all-gather.15.cloned.1.call-start = ((), (), s32[]{:S(2)}) async-start(), calls=%async_computation.26 | async-start | bytes 4718592 | tf_op jit(solution)/shard_map/all_gather | solution.py:132
  37.1 103.1 %copy-start.26 = (f32[2,1024]{1,0:T(2,128)}, f32[2,1024]{1,0:T(2,128)S(1)}, u32[]{:S(2)}) copy-start(f32[2,1024]{1,0:T(2,128)S(1)} %get-tuple-element.314) | copy-start | bytes 24580
  37.1 103.1 %copy-start.55 = (f32[2,1024]{1,0:T(2,128)}, f32[2,1024]{1,0:T(2,128)S(1)}, u32[]{:S(2)}) copy-start(f32[2,1024]{1,0:T(2,128)S(1)} %get-tuple-element.313) | copy-start | bytes 24580
  40.8 99.4 %copy-start.20 = (f32[2,1280]{1,0:T(2,128)}, f32[2,1280]{1,0:T(2,128)S(1)}, u32[]{:S(2)}) copy-start(f32[2,1280]{1,0:T(2,128)S(1)} %broadcast_multiply_fusion.2) | copy-start | bytes 30724
  42.8 97.4 %copy-start.38 = (f32[2,1280]{1,0:T(2,128)}, f32[2,1280]{1,0:T(2,128)S(1)}, u32[]{:S(2)}) copy-start(f32[2,1280]{1,0:T(2,128)S(1)} %fusion.149) | copy-start | bytes 30724
  146.5 19.0 copy-start.40
  160.3 81.1 %all-to-all-start.2 = ((bf16[2,1280,1024]{1,0,2:T(2,128)(2,1)}), bf16[2,1280,1024]{1,0,2:T(2,128)(2,1)}, u32[]{:S(2)}, u32[]{:S(2)}) async-start(bf16[2,1280,1024]{1,0,2:T(2,128)(2,1)} %copy.160), calls=%async_computation.2 | async-start | bytes 10485760 | tf_op jit(solution)/shard_map/all_to_all | solution.py:157
  165.4 699.9 %all-gather.13.cloned.1.call-start = ((), (), s32[]{:S(2)}) async-start(), calls=%async_computation.25 | async-start | bytes 2359296 | tf_op jit(solution)/shard_map/all_gather | solution.py:130
  227.5 19.0 copy-start.41
  241.4 80.9 %all-to-all-start.1 = ((bf16[2,1280,1024]{1,0,2:T(2,128)(2,1)}), bf16[2,1280,1024]{1,0,2:T(2,128)(2,1)}, u32[]{:S(2)}, u32[]{:S(2)}) async-start(bf16[2,1280,1024]{1,0,2:T(2,128)(2,1)} %copy.157), calls=%async_computation.1 | async-start | bytes 10485760 | tf_op jit(solution)/shard_map/all_to_all | solution.py:156
  246.4 636.2 %all-gather.17.cloned.1.call-start = ((), (), s32[]{:S(2)}) async-start(), calls=%async_computation.27 | async-start | bytes 2359296 | tf_op jit(solution)/shard_map/all_gather | solution.py:131
  308.5 18.9 copy-start.42
  308.5 81.0 %copy-start.51 = (f32[4,2025]{1,0:T(4,128)S(1)}, f32[4,2025]{1,0:T(4,128)}, u32[]{:S(2)}) copy-start(f32[4,2025]{1,0:T(4,128)} %param.26) | copy-start | bytes 97204
  322.3 253.7 %all-to-all-start = ((bf16[2,1280,1024]{1,0,2:T(2,128)(2,1)}), bf16[2,1280,1024]{1,0,2:T(2,128)(2,1)}, u32[]{:S(2)}, u32[]{:S(2)}) async-start(bf16[2,1280,1024]{1,0,2:T(2,128)(2,1)} %copy.154), calls=%async_computation | async-start | bytes 10485760 | tf_op jit(solution)/shard_map/all_to_all | solution.py:158
  327.3 586.1 %all-gather.19.cloned.1.call-start = ((), (), s32[]{:S(2)}) async-start(), calls=%async_computation.28 | async-start | bytes 2359296 | tf_op jit(solution)/shard_map/all_gather | solution.py:133
  389.4 540.1 %all-gather.23.cloned.1.call-start = ((), (), s32[]{:S(2)}) async-start(), calls=%async_computation.30 | async-start | bytes 9437184 | tf_op jit(solution)/shard_map/all_gather | solution.py:134
  775.6 83.2 %all-to-all-start.3 = ((bf16[2,5120,256]{2,0,1:T(2,128)(2,1)}), bf16[2,5120,256]{2,0,1:T(2,128)(2,1)}, u32[]{:S(2)}, u32[]{:S(2)}) async-start(bf16[2,5120,256]{2,0,1:T(2,128)(2,1)} %copy.171), calls=%async_computation.3 | async-start | bytes 10485760 | tf_op jit(solution)/shard_map/all_to_all | solution.py:187
  780.7 68.2 %copy-start.46 = (bf16[77,256]{1,0:T(8,128)(2,1)S(1)}, bf16[77,256]{1,0:T(8,128)(2,1)}, u32[]{:S(2)}) copy-start(bf16[77,256]{1,0:T(8,128)(2,1)} %param.24) | copy-start | bytes 118276
  780.8 73.7 %copy-start.19 = (bf16[2,77,1024]{2,0,1:T(2,128)(2,1)S(1)}, bf16[2,77,1024]{2,0,1:T(2,128)(2,1)}, u32[]{:S(2)}) copy-start(bf16[2,77,1024]{2,0,1:T(2,128)(2,1)} %param.22) | copy-start | bytes 946180
  780.8 180.3 %all-gather.27.cloned.1.call-start = ((), (), s32[]{:S(2)}) async-start(), calls=%async_computation.32 | async-start | bytes 9437184 | tf_op jit(solution)/shard_map/all_gather | solution.py:135
  781.5 1068.6 %reduce-scatter.35.cloned.1.call-start = ((), (), s32[]{:S(2)}) async-start(), calls=%async_computation.41 | async-start | bytes 2359296 | tf_op jit(solution)/shard_map/reduce_scatter | solution.py:389
  781.6 76.5 %copy-start.64 = (pred[2]{0:T(512)(128)(4,1)}, pred[2]{0:T(512)(128)(4,1)S(1)}, u32[]{:S(2)}) copy-start(pred[2]{0:T(512)(128)(4,1)S(1)} %broadcast_compare_fusion) | copy-start | bytes 10
  841.0 41.6 %copy-start.47 = (f32[4,1,256]{2,1,0:T(1,128)}, f32[4,1,256]{2,1,0:T(1,128)S(1)}, u32[]{:S(2)}) copy-start(f32[4,1,256]{2,1,0:T(1,128)S(1)} %convert_element_type.246) | copy-start | bytes 12292
  858.4 35.1 %copy-start.15 = (bf16[2,77,1024]{1,2,0:T(8,128)(2,1)}, bf16[2,77,1024]{1,2,0:T(8,128)(2,1)S(1)}, u32[]{:S(2)}) copy-start(bf16[2,77,1024]{1,2,0:T(8,128)(2,1)S(1)} %copy.284) | copy-start | bytes 946180
  858.8 46.1 %copy-start.17 = (bf16[2,77,1024]{1,2,0:T(8,128)(2,1)}, bf16[2,77,1024]{1,2,0:T(8,128)(2,1)S(1)}, u32[]{:S(2)}) copy-start(bf16[2,77,1024]{1,2,0:T(8,128)(2,1)S(1)} %copy.283) | copy-start | bytes 946180
  923.9 147.7 %copy-start.30 = (f32[2,1280]{1,0:T(2,128)}, f32[2,1280]{1,0:T(2,128)S(1)}, u32[]{:S(2)}) copy-start(f32[2,1280]{1,0:T(2,128)S(1)} %broadcast_multiply_fusion) | copy-start | bytes 30724
  929.5 142.2 %copy-start.44 = (f32[2,1280]{1,0:T(2,128)}, f32[2,1280]{1,0:T(2,128)S(1)}, u32[]{:S(2)}) copy-start(f32[2,1280]{1,0:T(2,128)S(1)} %fusion.151) | copy-start | bytes 30724
  929.5 31.6 %copy-start.61 = (f32[2,1024]{1,0:T(2,128)S(1)}, f32[2,1024]{1,0:T(2,128)}, u32[]{:S(2)}) copy-start(f32[2,1024]{1,0:T(2,128)} %get-tuple-element.312) | copy-start | bytes 24580
  961.1 62.9 %copy-start.66 = (bf16[1024,4096]{1,0:T(8,128)(2,1)S(1)}, bf16[1024,4096]{1,0:T(8,128)(2,1)}, u32[]{:S(2)}) copy-start(bf16[1024,4096]{1,0:T(8,128)(2,1)} %all-gather.23.cloned.1.call-done) | copy-start | bytes 25165828
  1051.1 20.6 slice-start.7
  1138.3 712.3 %reduce-scatter.27.cloned.1.call-start = ((), (), s32[]{:S(2)}) async-start(), calls=%async_computation.37 | async-start | bytes 2359296 | tf_op jit(solution)/shard_map/reduce_scatter | solution.py:383
  1174.6 15.9 slice-start.4
  1195.8 31.4 %slice-start.11 = ((s8[5242880]{0:T(1024)(128)(4,1)}), s8[1048576]{0:T(1024)(128)(4,1)S(1)}, s32[]{:S(2)}) async-start(s8[5242880]{0:T(1024)(128)(4,1)} %bitcast.413), calls=%async_computation.60 | async-start | bytes 2097152
  1205.8 645.4 %reduce-scatter.23.cloned.1.call-start = ((), (), s32[]{:S(2)}) async-start(), calls=%async_computation.35 | async-start | bytes 2359296 | tf_op jit(solution)/shard_map/reduce_scatter | solution.py:380
  1205.9 21.3 slice-start.12
  1205.9 21.3 copy-start.60
  1234.4 756.9 %reduce-scatter.31.cloned.1.call-start = ((), (), s32[]{:S(2)}) async-start(), calls=%async_computation.39 | async-start | bytes 4718592 | tf_op jit(solution)/shard_map/reduce_scatter | solution.py:386
  1250.2 40.9 %copy-start.11 = (f32[2,77,1024]{2,1,0:T(8,128)}, f32[2,77,1024]{2,1,0:T(8,128)S(1)}, u32[]{:S(2)}) copy-start(f32[2,77,1024]{2,1,0:T(8,128)S(1)} %copy.223) | copy-start | bytes 1892356
  1255.6 736.4 %reduce-scatter.43.cloned.1.call-start = ((), (), s32[]{:S(2)}) async-start(), calls=%async_computation.45 | async-start | bytes 9437184 | tf_op jit(solution)/shard_map/reduce_scatter | solution.py:395
  1318.3 64.5 %all-to-all-start.4 = ((bf16[2,1280,1024]{1,0,2:T(2,128)(2,1)}), bf16[2,1280,1024]{1,0,2:T(2,128)(2,1)}, u32[]{:S(2)}, u32[]{:S(2)}) async-start(bf16[2,1280,1024]{1,0,2:T(2,128)(2,1)} %copy.196), calls=%async_computation.4 | async-start | bytes 10485760 | tf_op jit(solution)/shard_map/all_to_all | solution.py:296
  1323.4 697.3 %reduce-scatter.39.cloned.1.call-start = ((), (), s32[]{:S(2)}) async-start(), calls=%async_computation.43 | async-start | bytes 9437184 | tf_op jit(solution)/shard_map/reduce_scatter | solution.py:392
  1323.5 15.9 copy-start.31
  1685.9 75.9 %all-to-all-start.7 = ((bf16[2,5120,256]{2,0,1:T(2,128)(2,1)}), bf16[2,5120,256]{2,0,1:T(2,128)(2,1)}, u32[]{:S(2)}, u32[]{:S(2)}) async-start(bf16[2,5120,256]{2,0,1:T(2,128)(2,1)} %copy.216), calls=%async_computation.7 | async-start | bytes 10485760 | tf_op jit(solution)/shard_map/all_to_all | solution.py:352
  1761.8 76.0 %all-to-all-start.5 = ((bf16[2,5120,256]{2,0,1:T(2,128)(2,1)}), bf16[2,5120,256]{2,0,1:T(2,128)(2,1)}, u32[]{:S(2)}, u32[]{:S(2)}) async-start(bf16[2,5120,256]{2,0,1:T(2,128)(2,1)} %copy.206), calls=%async_computation.5 | async-start | bytes 10485760 | tf_op jit(solution)/shard_map/all_to_all | solution.py:338
  1803.9 39.0 %copy-start.10 = (f32[2,77,1024]{2,1,0:T(8,128)S(1)}, f32[2,77,1024]{2,1,0:T(8,128)}, u32[]{:S(2)}) copy-start(f32[2,77,1024]{2,1,0:T(8,128)} %copy-done.9) | copy-start | bytes 1892356
  1804.0 39.0 %copy-start.12 = (f32[2,77,1024]{2,1,0:T(8,128)S(1)}, f32[2,77,1024]{2,1,0:T(8,128)}, u32[]{:S(2)}) copy-start(f32[2,77,1024]{2,1,0:T(8,128)} %copy-done.11) | copy-start | bytes 1892356
  1804.0 39.0 %copy-start.65 = (pred[2]{0:T(512)(128)(4,1)S(1)}, pred[2]{0:T(512)(128)(4,1)}, u32[]{:S(2)}) copy-start(pred[2]{0:T(512)(128)(4,1)} %copy-done.64) | copy-start | bytes 10
  1837.8 66.9 %all-to-all-start.6 = ((bf16[2,5120,256]{2,0,1:T(2,128)(2,1)}), bf16[2,5120,256]{2,0,1:T(2,128)(2,1)}, u32[]{:S(2)}, u32[]{:S(2)}) async-start(bf16[2,5120,256]{2,0,1:T(2,128)(2,1)} %copy.211), calls=%async_computation.6 | async-start | bytes 10485760 | tf_op jit(solution)/shard_map/all_to_all | solution.py:345
  1842.9 196.6 %reduce-scatter.47.cloned.1.call-start = ((), (), s32[]{:S(2)}) async-start(), calls=%async_computation.47 | async-start | bytes 204800 | tf_op jit(solution)/shard_map/reduce_scatter | solution.py:424
  1850.0 226.8 %reduce-scatter.37.cloned.1.call-start = ((), (), s32[]{:S(2)}) async-start(), calls=%async_computation.42 | async-start | bytes 327680 | tf_op jit(solution)/shard_map/reduce_scatter | solution.py:412
  1850.6 227.7 %reduce-scatter.29.cloned.1.call-start = ((), (), s32[]{:S(2)}) async-start(), calls=%async_computation.38 | async-start | bytes 327680 | tf_op jit(solution)/shard_map/reduce_scatter | solution.py:406
  1851.2 228.7 %reduce-scatter.25.cloned.1.call-start = ((), (), s32[]{:S(2)}) async-start(), calls=%async_computation.36 | async-start | bytes 327680 | tf_op jit(solution)/shard_map/reduce_scatter | solution.py:403
  1851.9 229.4 %reduce-scatter.19.cloned.1.call-start = ((), (), s32[]{:S(2)}) async-start(), calls=%async_computation.33 | async-start | bytes 7077888 | tf_op jit(solution)/shard_map/reduce_scatter | solution.py:377
  1936.1 165.7 %reduce-scatter.49.cloned.1.call-start = ((), (), s32[]{:S(2)}) async-start(), calls=%async_computation.48 | async-start | bytes 327680
  1985.4 16.5 copy-start.54
  1985.4 22.7 %copy-start.4 = (f32[4,320,320]{1,2,0:T(8,128)S(1)}, f32[4,320,320]{1,2,0:T(8,128)}, u32[]{:S(2)}) copy-start(f32[4,320,320]{1,2,0:T(8,128)} %get-tuple-element.116) | copy-start | bytes 4915204
  1991.2 115.0 %reduce-scatter.33.cloned.1.call-start = ((), (), s32[]{:S(2)}) async-start(), calls=%async_computation.40 | async-start | bytes 655360 | tf_op jit(solution)/shard_map/reduce_scatter | solution.py:409
  1992.0 141.8 %reduce-scatter.45.cloned.1.call-start = ((), (), s32[]{:S(2)}) async-start(), calls=%async_computation.46 | async-start | bytes 1310720 | tf_op jit(solution)/shard_map/reduce_scatter | solution.py:418
  1992.7 168.6 %reduce-scatter.41.cloned.1.call-start = ((), (), s32[]{:S(2)}) async-start(), calls=%async_computation.44 | async-start | bytes 1310720 | tf_op jit(solution)/shard_map/reduce_scatter | solution.py:415
  2020.8 166.3 %reduce-scatter.21.cloned.1.call-start = ((), (), s32[]{:S(2)}) async-start(), calls=%async_computation.34 | async-start | bytes 983040 | tf_op jit(solution)/shard_map/reduce_scatter | solution.py:400
  (67 other events, 471.5 us)
Sparse Core Ops, SparseCore 0:
  19.1 99.3 all-gather.10
  120.0 14.8 all-gather.20
  136.5 16.8 all-gather.24
  155.4 73.3 all-gather.14
  230.7 49.2 all-gather.12
  308.6 48.2 all-gather.16
  389.5 48.2 all-gather.18
  470.9 122.0 all-gather.22
  783.7 123.1 all-gather.26
  1138.4 64.9 reduce-scatter.34
  1206.9 66.7 reduce-scatter.26
  1277.1 66.8 reduce-scatter.22
  1347.6 87.1 reduce-scatter.30
  1438.7 148.7 reduce-scatter.42
  1591.0 148.0 reduce-scatter.38
  1850.1 18.1 reduce-scatter.46
  1870.7 21.4 reduce-scatter.36
  1894.6 20.0 reduce-scatter.28
  1917.2 20.0 reduce-scatter.24
  1940.8 118.5 reduce-scatter.18
  2062.4 19.4 reduce-scatter.48
  2084.6 21.6 reduce-scatter.32
  2108.8 24.9 reduce-scatter.44
  2136.3 24.9 reduce-scatter.40
  2163.8 23.2 reduce-scatter.20
where the time goes:
time: 2220 us; the launch traced here: 2200 us
  local copies, waits for them, and re-layouts  764 us (34%)
  matrix products  703 us (32%)
  blocking collectives  312 us (14%)
  waiting for transfers between devices  212 us (10%)
  other arithmetic  145 us (7%)
  starting transfers between devices  42.6 us (2%)
    reshape x4, local copies, waits for them, and re-layouts, windows_to_heads(): reshaped.transpose(0, 3, 1, 4, 2, 5, 6)  135 us
    while x5, local copies, waits for them, and re-layouts, local(): lax.map(attend_group, (group_queries_all, group_keys_all, group_values_all))  85.5 us
    unnamed x186, local copies, waits for them, and re-layouts  75.7 us
    all_gather x1, waiting for transfers between devices, local(): lax.all_gather(columns[0], 'clip', axis=0, tiled=True)  75.6 us
    reshape x4, local copies, waits for them, and re-layouts, heads_to_windows(): heads_array.reshape(clip_count, FRAMES, blocks, WS, blocks, WS, heads_loc...  64.1 us
    reshape x4, local copies, waits for them, and re-layouts, windows_to_heads(): grouped.reshape(clip_count, blocks, blocks, FRAMES, WS, WS, local_width)  63.4 us
    dot_general x1, matrix products, local(): jnp.dot(grad_reduced, reduce_full.T, preferred_element_type=single)  62.9 us
    all_gather x1, blocking collectives, local(): lax.all_gather(self_output, 'win', axis=1, tiled=True)  61.9 us
  transfers between devices with their start and end apart: 33, of which 7 were waited for; matrix products, arithmetic and copies ran while one was open for 64% of the time, Pallas kernels for 0%

commit v1 on v0

v1 whole, which is shorter than its diff:
```python
import functools

import jax
import jax.numpy as jnp
from jax import lax
from jax.experimental import pallas as pl
from jax.experimental.pallas import tpu as pltpu
from jax.sharding import PartitionSpec as P

HEADS = 16
HD = 64
FRAMES = 5
GRID = 32
WS = 8
SEQ = 5120
WIN_TOK = 320
NREL = 2025
TXT = 77
QUAD = 4
QW = QUAD * HD
QUADS = HEADS // QUAD
SPAN = 2 * WS - 1
FSPAN = 2 * FRAMES - 1
SIDE = WS * WS
PADK = 384
PADT = 128

epsilon = 1e-06
gelu_coefficient = 0.7978845608028654
scale_factor = HD ** (-0.5)
bfloat = jnp.bfloat16
single = jnp.float32
NEGATIVE = -1e30
VMEM_LIMIT = 60 * 1024 * 1024

NN = (((1,), (0,)), ((), ()))
NT = (((1,), (1,)), ((), ()))
TN = (((0,), (0,)), ((), ()))


def mm(left, right, dims=NN):
    return lax.dot_general(left, right, dims, preferred_element_type=single)


def norm_parts(values):
    centered = values - jnp.mean(values, axis=-1, keepdims=True)
    variance = jnp.mean(centered * centered, axis=-1, keepdims=True)
    inverse = lax.rsqrt(variance + epsilon)
    return centered * inverse, inverse


def norm_back(normed, inverse, grad):
    return inverse * (
        grad
        - jnp.mean(grad, axis=-1, keepdims=True)
        - normed * jnp.mean(grad * normed, axis=-1, keepdims=True)
    )


def params():
    return pltpu.CompilerParams(vmem_limit_bytes=VMEM_LIMIT)


def cost(microseconds):
    return pl.CostEstimate(
        flops=int(microseconds * 760e3),
        bytes_accessed=int(microseconds * 1e3),
        transcendentals=0,
    )


def tie(*values):
    return lax.optimization_barrier(values)


ANY = pl.BlockSpec(memory_space=pl.ANY)
PLACE = pl.BlockSpec(memory_space=pltpu.SMEM)
FIRST_ORDER = ("z", "x", "y")
OTHER_ORDER = ("z", "y", "x")


class Layout:
    def __init__(self, clip_size, win_count):
        self.clip_size, self.win_count = clip_size, win_count
        y = 2 ** ((clip_size.bit_length() - 1) // 2)
        self.size = {"z": clip_size // y, "y": y, "x": win_count // 2, "core": 2}
        self.home = {"z": "clip", "y": "clip", "x": "win", "core": "win"}
        self.stride = {"z": y, "y": 1, "x": 2, "core": 1}
        self.others = clip_size * win_count // 2

    def place(self):
        clip, win = lax.axis_index("clip"), lax.axis_index("win")
        y = self.size["y"]
        return jnp.stack([clip // y, clip % y, win // 2, win % 2]).astype(jnp.int32)

    def swap(self, values, axis, apart):
        home = self.home[axis]
        count = self.clip_size if home == "clip" else self.win_count
        step = apart * self.stride[axis]
        return lax.ppermute(values, home, [(i, i ^ step) for i in range(count)])

    def gather(self, held, order):
        held = held.reshape((-1,) + held.shape[-2:])
        for axis in order:
            apart = 1
            while apart < self.size[axis]:
                held = jnp.concatenate([held, self.swap(held, axis, apart)], axis=0)
                apart *= 2
        return held

    def owner(self, place_ref, order, index, core_apart):
        names = ("z", "y", "x", "core")
        at = {name: place_ref[i] for i, name in enumerate(names)}
        for axis in order:
            at[axis] = at[axis] ^ (index % self.size[axis])
            index = index // self.size[axis]
        core = at["core"] ^ core_apart
        return at["z"] * self.size["y"] + at["y"], at["x"] * 2 + core

    def reduce(self, term, axis, pin, first=0, last=None):
        bits = self.size[axis].bit_length() - 1
        last = bits if last is None else last
        for bit in range(first, last):
            half = term.shape[0] // 2
            part, pin = tie(self.swap(term[half:], axis, 1 << bit), pin)
            total = term[:half].astype(single) + part.astype(single)
            term = total.astype(bfloat)
        if last < bits:
            return term, pin
        return (total[0] if axis == "z" else term[0]), pin


def pack(lead, columns, *stages):
    parts = []
    for stage in stages:
        stage = stage.reshape(stage.shape[:lead] + (-1, stage.shape[-1]))
        parts += [stage[..., i : i + columns] for i in range(0, stage.shape[-1], columns)]
    return jnp.concatenate(parts, axis=lead)


def unpack(values, shapes):
    outs, at, columns = [], 0, values.shape[-1]
    for rows, cols in shapes:
        parts = []
        for _ in range(cols // columns):
            parts.append(values[at : at + rows])
            at += rows
        outs.append(jnp.concatenate(parts, axis=1))
    return outs


def reverse(index, size):
    distance, bits = 0, size.bit_length() - 1
    for b in range(bits):
        distance = distance + (((index >> b) & 1) << (bits - 1 - b))
    return distance


def start_weight(sources, target, sem, layout, place_ref, order, rows, cols, offset=0):
    depth = sources[0].shape[1]
    for apart, source in enumerate(sources):

        def step(i, carry, source=source, apart=apart):
            clip, win = layout.owner(place_ref, order, i, apart)
            for piece in range(rows // depth):
                row = pl.multiple_of(clip * rows + piece * depth, depth)
                column = pl.multiple_of(win * cols, cols)
                pltpu.make_async_copy(
                    source.at[i, :, pl.ds(offset + piece * cols, cols)],
                    target.at[pl.ds(row, depth), pl.ds(column, cols)],
                    sem,
                ).start()
            return carry

        lax.fori_loop(0, layout.others, step, 0)


def start_squares(own, other, targets, sems, layout, place_ref):
    rows, cols = own.shape[1], own.shape[2] // 3
    for i, target in enumerate(targets):
        start_weight(
            (own, other), target, sems.at[i], layout, place_ref, FIRST_ORDER, rows, cols, i * cols
        )


def start_gathered(source, target, sem, layout, cols, offset=0):
    depth = source.shape[1]
    rows = target.shape[0] // layout.clip_size

    def step(c, carry):
        for w in range(layout.win_count):
            for piece in range(rows // depth):
                row = pl.multiple_of(c * rows + piece * depth, depth)
                pltpu.make_async_copy(
                    source.at[c * layout.win_count + w, :, pl.ds(offset + piece * cols, cols)],
                    target.at[pl.ds(row, depth), pl.ds(w * cols, cols)],
                    sem,
                ).start()
        return carry

    lax.fori_loop(0, layout.clip_size, step, 0)


def wait_weight(target, sem):
    pltpu.make_async_copy(target, target, sem).wait()


def window_spec(wins, width):
    return pl.BlockSpec(
        (1, FRAMES, WS, 1, WS, width), lambda i: (i // wins, 0, 0, i % wins, 0, 0)
    )


def rows_spec(width):
    return pl.BlockSpec((1, WIN_TOK, width), lambda i: (i, 0, 0))


def modulation_spec(wins, width):
    return pl.BlockSpec((1, 6, width), lambda i: (i // wins, 0, 0))


def load_window(ref):
    return ref[0, :, :, 0].astype(single).reshape(WIN_TOK, ref.shape[-1])


def store_window(ref, values):
    ref[0, :, :, 0] = values.reshape(FRAMES, WS, WS, ref.shape[-1]).astype(ref.dtype)


def table_kernel(shift_ref, block_ref, out_ref):
    out_ref[...] = jnp.full(out_ref.shape, NEGATIVE, single)
    shift = shift_ref[0]
    for a in range(FRAMES):
        for b in range(FRAMES):
            offset = lax.rem(shift + a, FRAMES) - lax.rem(shift + b, FRAMES) + FRAMES - 1
            out_ref[0, a * SIDE : (a + 1) * SIDE, b * SIDE : (b + 1) * SIDE] = block_ref[0, offset]


def collect_kernel(shift_ref, sum_ref, out_ref):
    out_ref[...] = jnp.zeros(out_ref.shape, single)
    shift = shift_ref[0]
    for a in range(FRAMES):
        for b in range(FRAMES):
            offset = lax.rem(shift + a, FRAMES) - lax.rem(shift + b, FRAMES) + FRAMES - 1
            out_ref[0, offset] += sum_ref[0, a * SIDE : (a + 1) * SIDE, b * SIDE : (b + 1) * SIDE]


def head_spec():
    return pl.BlockSpec((1, WIN_TOK, PADK), lambda h, s: (h // QUAD, 0, h % QUAD))


def side_hot():
    shape = (SPAN * SPAN, SIDE * SIDE)
    offset = lax.broadcasted_iota(jnp.int32, shape, 0)
    pair = lax.broadcasted_iota(jnp.int32, shape, 1)
    first, second = pair // SIDE, pair % SIDE
    rows = first // WS - second // WS + WS - 1
    columns = first % WS - second % WS + WS - 1
    return (rows * SPAN + columns == offset).astype(single)


def bias_table(bias_full, shift):
    flat = bias_full.reshape(HEADS * FSPAN, SPAN * SPAN)
    blocks = jnp.dot(flat, side_hot(), precision=lax.Precision.HIGHEST)
    blocks = blocks.reshape(HEADS, FSPAN, SIDE, SIDE)
    return pl.pallas_call(
        table_kernel,
        grid_spec=pltpu.PrefetchScalarGridSpec(
            num_scalar_prefetch=1,
            grid=(HEADS,),
            in_specs=[pl.BlockSpec((1, FSPAN, SIDE, SIDE), lambda h, s: (h, 0, 0, 0))],
            out_specs=head_spec(),
        ),
        out_shape=jax.ShapeDtypeStruct((QUADS, WIN_TOK, QUAD * PADK), single),
        compiler_params=params(),
        cost_estimate=cost(12),
        name="bias_table",
    )(shift, blocks)


def bias_collect(bias_sum, shift):
    blocks = pl.pallas_call(
        collect_kernel,
        grid_spec=pltpu.PrefetchScalarGridSpec(
            num_scalar_prefetch=1,
            grid=(HEADS,),
            in_specs=[head_spec()],
            out_specs=pl.BlockSpec((1, FSPAN, SIDE, SIDE), lambda h, s: (h, 0, 0, 0)),
        ),
        out_shape=jax.ShapeDtypeStruct((HEADS, FSPAN, SIDE, SIDE), single),
        compiler_params=params(),
        cost_estimate=cost(12),
        name="bias_collect",
    )(shift, bias_sum)
    flat = blocks.reshape(HEADS * FSPAN, SIDE * SIDE)
    summed = lax.dot_general(flat, side_hot(), NT, precision=lax.Precision.HIGHEST)
    return summed.reshape(HEADS, NREL)


def project_kernel(layout, tokens_ref, mod_ref, weight_any, low_ref, out_ref, weight_ref, sem):
    @pl.when(pl.program_id(0) == 0)
    def _():
        start_gathered(weight_any, weight_ref, sem, layout, weight_any.shape[2])
        wait_weight(weight_ref, sem)

    normed, _ = norm_parts(load_window(tokens_ref))
    low = (normed * (1.0 + mod_ref[0, 1:2]) + mod_ref[0, 0:1]).astype(bfloat)
    low_ref[0] = low
    out_ref[0] = mm(low, weight_ref[...]).astype(bfloat)


def head_mask(width_rows, head):
    lane = lax.broadcasted_iota(jnp.int32, (width_rows, QW), 1)
    return (lane >= head * HD) & (lane < (head + 1) * HD)


def stacked(values, pad):
    rows = values.shape[0]
    parts = []
    for h in range(QUAD):
        parts.append(jnp.where(head_mask(rows, h), values, jnp.zeros_like(values)))
        if pad > rows:
            parts.append(jnp.zeros((pad - rows, QW), values.dtype))
    return jnp.concatenate(parts, axis=0)


def attend_kernel(q_ref, k_ref, v_ref, bias_ref, out_ref, total_ref):
    keys = stacked(k_ref[0], PADK)
    values = stacked(v_ref[0], PADK)
    queries = q_ref[0] * jnp.asarray(scale_factor, bfloat)
    scores = mm(queries, keys, NT) + bias_ref[0]
    weights = []
    for h in range(QUAD):
        part = scores[:, h * PADK : (h + 1) * PADK]
        top = jnp.max(part, axis=-1, keepdims=True)
        expanded = jnp.exp(part - top)
        total = jnp.sum(expanded, axis=-1, keepdims=True)
        weights.append((expanded * (1.0 / total)).astype(bfloat))
        total_ref[0, 0, :, h : h + 1] = top + jnp.log(total)
    out_ref[0] = mm(jnp.concatenate(weights, axis=1), values).astype(bfloat)


def attend_back_kernel(
    q_ref, k_ref, v_ref, g_ref, bias_ref, total_ref, out_ref, sum_ref
):
    @pl.when(pl.program_id(1) == 0)
    def _():
        sum_ref[...] = jnp.zeros(sum_ref.shape, single)

    keys = stacked(k_ref[0], PADK)
    values = stacked(v_ref[0], PADK)
    queries = q_ref[0] * jnp.asarray(scale_factor, bfloat)
    grad = g_ref[0]
    scores = mm(queries, keys, NT) + bias_ref[0]
    grad_probs = mm(grad, values, NT)
    queries_t = queries.T
    grad_t = grad.T
    grads, key_parts, value_parts = [], [], []
    for h in range(QUAD):
        at = slice(h * PADK, (h + 1) * PADK)
        rows = slice(h * HD, (h + 1) * HD)
        probs = jnp.exp(scores[:, at] - total_ref[0, 0, :, h : h + 1])
        gp = grad_probs[:, at]
        gs = probs * (gp - jnp.sum(probs * gp, axis=-1, keepdims=True))
        gs_low = gs.astype(bfloat)
        sum_ref[0, :, at] += gs_low.astype(single)
        grads.append(gs_low)
        key_parts.append(mm(queries_t[rows], gs_low))
        value_parts.append(mm(grad_t[rows], probs.astype(bfloat)))
    out_ref[0, 0] = (mm(jnp.concatenate(grads, axis=1), keys) * scale_factor).astype(bfloat)
    out_ref[1, 0] = jnp.concatenate(key_parts, axis=0).T[:WIN_TOK].astype(bfloat)
    out_ref[2, 0] = jnp.concatenate(value_parts, axis=0).T[:WIN_TOK].astype(bfloat)


def quad_spec(offset):
    return pl.BlockSpec((1, WIN_TOK, QW), lambda q, i: (i, 0, q + offset))


BIAS_SPEC = pl.BlockSpec((1, WIN_TOK, QUAD * PADK), lambda q, i: (q, 0, 0))
TOTAL_SPEC = pl.BlockSpec((1, 1, WIN_TOK, QUAD), lambda q, i: (q, i, 0, 0))


def memory_kernel(
    layout, place_ref, text_ref, own_any, other_any, keys_ref, values_ref, weight_ref, sem
):
    @pl.when(pl.program_id(0) == 0)
    def _():
        rows, cols = own_any.shape[1:]
        sources = (own_any, other_any)
        start_weight(sources, weight_ref, sem, layout, place_ref, OTHER_ORDER, rows, cols)
        wait_weight(weight_ref, sem)

    width = text_ref.shape[-1]
    memory = mm(text_ref[0], weight_ref[...]).astype(bfloat)
    for q in range(QUADS):
        keys_ref[0, q] = stacked(memory[:, q * QW : (q + 1) * QW], PADT)
        values_ref[0, q] = stacked(memory[:, width + q * QW : width + (q + 1) * QW], PADT)


def cross_probs(queries, keys):
    scores = mm(queries, keys, NT) * scale_factor
    lane = lax.broadcasted_iota(jnp.int32, (scores.shape[0], PADT), 1)
    parts = []
    for h in range(QUAD):
        part = jnp.where(lane < TXT, scores[:, h * PADT : (h + 1) * PADT], NEGATIVE)
        expanded = jnp.exp(part - jnp.max(part, axis=-1, keepdims=True))
        parts.append(expanded * (1.0 / jnp.sum(expanded, axis=-1, keepdims=True)))
    return parts


def cross_kernel(
    layout,
    place_ref,
    tokens_ref,
    attended_ref,
    mod_ref,
    gain_ref,
    keys_ref,
    values_ref,
    own_any,
    other_any,
    branch_ref,
    left_ref,
    queries_ref,
    sum_ref,
    output_ref,
    query_ref,
    cross_ref,
    sems,
):
    @pl.when(pl.program_id(0) == 0)
    def _():
        start_squares(own_any, other_any, (output_ref, query_ref, cross_ref), sems, layout, place_ref)
        wait_weight(output_ref, sems.at[0])
        wait_weight(query_ref, sems.at[1])
        wait_weight(cross_ref, sems.at[2])

    attended = attended_ref[0]
    left_ref[0, 0] = attended
    branch = mm(attended, output_ref[...])
    branch_ref[0] = branch
    first_sum = load_window(tokens_ref) + mod_ref[0, 2:3] * branch
    normed, _ = norm_parts(first_sum)
    second = (normed * gain_ref[...]).astype(bfloat)
    left_ref[1, 0] = second
    queries = mm(second, query_ref[...]).astype(bfloat)
    queries_ref[0] = queries
    parts = []
    for q in range(QUADS):
        probs = cross_probs(queries[:, q * QW : (q + 1) * QW], keys_ref[0, q])
        low = jnp.concatenate([p.astype(bfloat) for p in probs], axis=1)
        parts.append(mm(low, values_ref[0, q]).astype(bfloat))
    crossed = jnp.concatenate(parts, axis=1)
    left_ref[2, 0] = crossed
    sum_ref[0] = first_sum + mm(crossed, cross_ref[...])


def cross_back_kernel(
    layout,
    wins,
    place_ref,
    tokens_ref,
    mod_ref,
    gain_ref,
    keys_ref,
    values_ref,
    grad_ref,
    queries_ref,
    branch_ref,
    own_any,
    other_any,
    right_ref,
    grad_sum_ref,
    grad_attended_ref,
    memory_ref,
    gain_grad_ref,
    gate_grad_ref,
    output_ref,
    query_ref,
    cross_ref,
    sems,
):
    step = pl.program_id(0)

    @pl.when(step == 0)
    def _():
        start_squares(own_any, other_any, (output_ref, query_ref, cross_ref), sems, layout, place_ref)
        wait_weight(output_ref, sems.at[0])
        wait_weight(query_ref, sems.at[1])
        wait_weight(cross_ref, sems.at[2])
        gain_grad_ref[...] = jnp.zeros(gain_grad_ref.shape, single)

    @pl.when(step % wins == 0)
    def _():
        memory_ref[...] = jnp.zeros(memory_ref.shape, single)
        gate_grad_ref[...] = jnp.zeros(gate_grad_ref.shape, single)

    width = queries_ref.shape[-1]
    grad = grad_ref[0]
    grad_low = grad.astype(bfloat)
    right_ref[2, 0] = grad_low
    grad_crossed = mm(grad_low, cross_ref[...], NT).astype(bfloat)
    queries = queries_ref[0]
    query_parts = []
    for q in range(QUADS):
        at = slice(q * QW, (q + 1) * QW)
        probs = cross_probs(queries[:, at], keys_ref[0, q])
        grad_probs = mm(grad_crossed[:, at], values_ref[0, q], NT)
        queries_t = queries[:, at].T
        grad_t = grad_crossed[:, at].T
        grads = []
        for h in range(QUAD):
            rows = slice(h * HD, (h + 1) * HD)
            gp = grad_probs[:, h * PADT : (h + 1) * PADT]
            gs = probs[h] * (gp - jnp.sum(probs[h] * gp, axis=-1, keepdims=True))
            gs_low = gs.astype(bfloat)
            grads.append(gs_low)
            place = q * QW + h * HD
            memory_ref[0, place : place + HD] += mm(queries_t[rows], gs_low) * scale_factor
            place = width + place
            memory_ref[0, place : place + HD] += mm(grad_t[rows], probs[h].astype(bfloat))
        all_grads = jnp.concatenate(grads, axis=1)
        query_parts.append((mm(all_grads, keys_ref[0, q]) * scale_factor).astype(bfloat))
    grad_queries = jnp.concatenate(query_parts, axis=1)
    right_ref[1, 0] = grad_queries
    grad_second = mm(grad_queries, query_ref[...], NT)
    branch = branch_ref[0]
    normed, inverse = norm_parts(load_window(tokens_ref) + mod_ref[0, 2:3] * branch)
    gain_grad_ref[...] += jnp.sum(grad_second * normed, axis=0, keepdims=True)
    grad_sum = grad + norm_back(normed, inverse, grad_second * gain_ref[...])
    grad_sum_ref[0] = grad_sum
    gate_grad_ref[0] += jnp.sum(grad_sum * branch, axis=0, keepdims=True)
    grad_branch = (mod_ref[0, 2:3] * grad_sum).astype(bfloat)
    right_ref[0, 0] = grad_branch
    grad_attended_ref[0] = mm(grad_branch, output_ref[...], NT).astype(bfloat)


def null_kernel(layout, place_ref, masked_ref, own_any, other_any, out_ref, weight_ref, sem):
    rows, cols = own_any.shape[1:]
    sources = (own_any, other_any)
    start_weight(sources, weight_ref, sem, layout, place_ref, OTHER_ORDER, rows, cols)
    wait_weight(weight_ref, sem)
    masked = masked_ref[...]
    high = masked.astype(bfloat)
    rest = (masked - high.astype(single)).astype(bfloat)
    weight = weight_ref[...]
    out_ref[...] = mm(high, weight, NT) + mm(rest, weight, NT)


def null_text_term(layout, place, masked, own, other):
    width = masked.shape[1] // 2
    whole = pl.BlockSpec(memory_space=pltpu.VMEM)
    return pl.pallas_call(
        functools.partial(null_kernel, layout),
        in_specs=[PLACE, whole, ANY, ANY],
        out_specs=whole,
        out_shape=jax.ShapeDtypeStruct((masked.shape[0], width), single),
        scratch_shapes=[pltpu.VMEM((width, 2 * width), bfloat), pltpu.SemaphoreType.DMA(())],
        compiler_params=params(),
        cost_estimate=cost(5),
        name="null_text",
    )(place, masked, own, other)


def feed_kernel(
    layout,
    wins,
    chunk,
    sum_ref,
    cotangent_ref,
    mod_ref,
    weights_any,
    out_ref,
    third_ref,
    act_ref,
    grad_hidden_ref,
    grad_reduced_ref,
    grad_sum_ref,
    grad_mod_ref,
    expand_ref,
    reduce_ref,
    sems,
):
    step = pl.program_id(0)

    @pl.when(step == 0)
    def _():
        cols = expand_ref.shape[1] // layout.win_count
        start_gathered(weights_any, expand_ref, sems.at[0], layout, cols)
        offset = cols
        cols = reduce_ref.shape[1] // layout.win_count
        start_gathered(weights_any, reduce_ref, sems.at[1], layout, cols, offset)
        wait_weight(expand_ref, sems.at[0])
        wait_weight(reduce_ref, sems.at[1])

    @pl.when(step % wins == 0)
    def _():
        grad_mod_ref[...] = jnp.zeros(grad_mod_ref.shape, single)

    second_sum = sum_ref[0]
    normed, inverse = norm_parts(second_sum)
    third = (normed * (1.0 + mod_ref[0, 4:5]) + mod_ref[0, 3:4]).astype(bfloat)
    third_ref[0] = third
    grad_out = load_window(cotangent_ref)
    gate = mod_ref[0, 5:6]
    grad_reduced = (gate * grad_out).astype(bfloat)
    grad_reduced_ref[0] = grad_reduced
    hidden_width = expand_ref.shape[1]
    for at in range(0, hidden_width, chunk):
        part = slice(at, at + chunk)
        v = mm(third, expand_ref[:, part])
        grad_act = mm(grad_reduced, reduce_ref[part], NT)
        square = v * v
        tanh = jnp.tanh(gelu_coefficient * (v + 0.044715 * (square * v)))
        half = 0.5 * (1.0 + tanh)
        act_ref[0, :, part] = (v * half).astype(bfloat)
        slope = half + (0.5 * gelu_coefficient) * v * (1.0 - tanh * tanh) * (
            1.0 + (3 * 0.044715) * square
        )
        grad_hidden_ref[0, :, part] = (grad_act * slope).astype(bfloat)
    reduced = mm(act_ref[0], reduce_ref[...])
    store_window(out_ref, second_sum + gate * reduced)
    grad_third = mm(grad_hidden_ref[0], expand_ref[...], NT)
    grad_mod_ref[0, 0:1] += jnp.sum(grad_third, axis=0, keepdims=True)
    grad_mod_ref[0, 1:2] += jnp.sum(grad_third * normed, axis=0, keepdims=True)
    grad_mod_ref[0, 2:3] += jnp.sum(grad_out * reduced, axis=0, keepdims=True)
    grad_sum_ref[0] = grad_out + norm_back(normed, inverse, grad_third * (1.0 + mod_ref[0, 4:5]))


def input_back_kernel(
    layout,
    wins,
    tokens_ref,
    mod_ref,
    grad_ref,
    grad_sum_ref,
    weight_any,
    out_ref,
    grad_mod_ref,
    weight_ref,
    sem,
):
    step = pl.program_id(0)

    @pl.when(step == 0)
    def _():
        start_gathered(weight_any, weight_ref, sem, layout, weight_any.shape[2])
        wait_weight(weight_ref, sem)

    @pl.when(step % wins == 0)
    def _():
        grad_mod_ref[...] = jnp.zeros(grad_mod_ref.shape, single)

    grads = jnp.concatenate([grad_ref[0, 0], grad_ref[1, 0], grad_ref[2, 0]], axis=1)
    grad_first = mm(grads, weight_ref[...], NT)
    normed, inverse = norm_parts(load_window(tokens_ref))
    grad_mod_ref[0, 0:1] += jnp.sum(grad_first, axis=0, keepdims=True)
    grad_mod_ref[0, 1:2] += jnp.sum(grad_first * normed, axis=0, keepdims=True)
    back = norm_back(normed, inverse, grad_first * (1.0 + mod_ref[0, 1:2]))
    store_window(out_ref, grad_sum_ref[0] + back)


def owner_column(layout, place_ref, step, core_apart):
    distance = reverse(step, layout.size["x"])
    return (place_ref[2] ^ distance) * 2 + (place_ref[3] ^ core_apart)


def owner_row(layout, place_ref, y, z):
    y, z = reverse(y, layout.size["y"]), reverse(z, layout.size["z"])
    return (place_ref[0] ^ z) * layout.size["y"] + (place_ref[1] ^ y)


def columns_kernel(layout, pieces, added, x_first, place_ref, x_ref, *refs):
    y_refs, out_ref, product_ref = refs[:pieces], refs[-2], refs[-1]
    rows = out_ref.shape[-2]
    cols = out_ref.shape[-1] // pieces
    for i in range(pieces):
        product_ref[:, i * cols : (i + 1) * cols] = mm(x_ref[0], y_refs[i][0], TN)
    for y in range(layout.size["y"]):
        for z in range(layout.size["z"]):
            clip = owner_row(layout, place_ref, y, z)
            part = product_ref[pl.ds(pl.multiple_of(clip * rows, rows), rows)]
            at = (0, y, z, 0) if x_first else (y, 0, z, 0)
            if added:
                part = part + refs[pieces][at].astype(single)
            out_ref[at] = part.astype(bfloat)


def weight_grad(layout, place, x, y, pieces, core_apart, added, name, x_first=False):
    count, tokens, depth = x.shape
    width = y.shape[-1]
    unit = width // layout.win_count
    rows, cols = depth // layout.clip_size, pieces * unit
    size = layout.size

    def unit_spec(i):
        def index(n, j, place_ref):
            at = owner_column(layout, place_ref, j, core_apart) * pieces + i
            return (n * pieces + at // layout.win_count, 0, at % layout.win_count)

        return pl.BlockSpec((1, tokens, unit), index)

    if x_first:
        leading = (size["x"], size["y"], size["z"])
        block = pl.BlockSpec(
            (1,) + leading[1:] + (1, rows, cols), lambda n, j, p: (j, 0, 0, n, 0, 0)
        )
    else:
        leading = (size["y"], size["x"], size["z"])
        block = pl.BlockSpec(
            (size["y"], 1, size["z"], 1, rows, cols), lambda n, j, p: (0, j, 0, n, 0, 0)
        )
    extra = () if added is None else (added,)
    return pl.pallas_call(
        functools.partial(columns_kernel, layout, pieces, added is not None, x_first),
        grid_spec=pltpu.PrefetchScalarGridSpec(
            num_scalar_prefetch=1,
            grid=(count, size["x"]),
            in_specs=[pl.BlockSpec((1, tokens, depth), lambda n, j, p: (n, 0, 0))]
            + [unit_spec(i) for i in range(pieces)]
            + [block] * len(extra),
            out_specs=block,
            scratch_shapes=[pltpu.VMEM((depth, cols), single)],
        ),
        out_shape=jax.ShapeDtypeStruct(leading + (count, rows, cols), bfloat),
        compiler_params=params(),
        cost_estimate=cost(count * size["x"] * tokens * depth * cols / 382e3),
        name=name,
    )(place, x, *([y] * pieces), *extra)


def rows_kernel(layout, added, place_ref, x_ref, *refs):
    size = layout.size["x"]
    y_refs, out_ref = refs[:size], refs[-1]
    left = x_ref[...]
    for j in range(size):
        part = mm(left, y_refs[j][...], TN)
        if added:
            part = part + refs[size][0, j, 0].astype(single)
        out_ref[0, j, 0] = part.astype(bfloat)


def weight_grad_rows(layout, place, x, y, core_apart, added, name):
    tokens, depth = x.shape
    width = y.shape[1]
    rows, cols = depth // layout.clip_size, width // layout.win_count
    size = layout.size

    def left(y_at, z_at, place_ref):
        return (0, owner_row(layout, place_ref, y_at, z_at))

    def right(j):
        return lambda y_at, z_at, place_ref: (
            0,
            owner_column(layout, place_ref, j, core_apart),
        )

    block = pl.BlockSpec((1, size["x"], 1, rows, cols), lambda y_at, z_at, p: (y_at, 0, z_at, 0, 0))
    extra = () if added is None else (added,)
    return pl.pallas_call(
        functools.partial(rows_kernel, layout, added is not None),
        grid_spec=pltpu.PrefetchScalarGridSpec(
            num_scalar_prefetch=1,
            grid=(size["y"], size["z"]),
            in_specs=[pl.BlockSpec((tokens, rows), left)]
            + [pl.BlockSpec((tokens, cols), right(j)) for j in range(size["x"])]
            + [block] * len(extra),
            out_specs=block,
        ),
        out_shape=jax.ShapeDtypeStruct((size["y"], size["x"], size["z"], rows, cols), bfloat),
        compiler_params=params(),
        cost_estimate=cost(size["x"] * tokens * depth * cols / 382e3),
        name=name,
    )(place, x, *([y] * size["x"]), *extra)


def to_windows(values, win_count):
    clips, count, width = values.shape
    blocks = GRID // WS
    if win_count == blocks:
        chunk = WS * GRID
        parts = [values[:, k * chunk : (k + 1) * chunk] for k in range(FRAMES)]
        received = {}
        for k in range(1, blocks):
            pairs = [(w, (w + k) % win_count) for w in range(win_count)]
            received[k] = lax.ppermute(parts[k], "win", pairs)
        own = [parts[0], parts[FRAMES - 1]] + [received[k] for k in range(blocks - 1, 0, -1)]
        return jnp.stack(own, axis=1).reshape(clips, FRAMES, WS, blocks, WS, width)
    halves = win_count // blocks
    wins = blocks // halves
    me = lax.axis_index("win")
    whole = lax.all_gather(values, "win", axis=1, tiled=True)
    whole = whole.reshape(clips, FRAMES, blocks, WS, blocks, WS, width)
    whole = lax.dynamic_slice_in_dim(whole, me // halves, 1, axis=2)
    whole = lax.dynamic_slice_in_dim(whole, (me % halves) * wins, wins, axis=4)
    return whole.reshape(clips, FRAMES, WS, wins, WS, width)


def from_windows(values, win_count, pin):
    clips, _, _, wins, _, width = values.shape
    blocks = GRID // WS
    if win_count == blocks:
        chunk = WS * GRID
        parts = values.reshape(clips, FRAMES, chunk, width)
        sent = {}
        for k in range(1, blocks):
            pairs = [((w + k) % win_count, w) for w in range(win_count)]
            sent[k] = lax.ppermute(parts[:, FRAMES - k], "win", pairs)
        sent, pin = tie(sent, pin)
        own = [parts[:, 0]] + [sent[k] for k in range(1, blocks)] + [parts[:, 1]]
        return jnp.stack(own, axis=1).reshape(clips, FRAMES * chunk, width), pin
    halves = win_count // blocks
    me = lax.axis_index("win")
    whole = lax.all_gather(values, "win", axis=0, tiled=False)
    whole = whole.reshape(blocks, halves, clips, FRAMES, WS, wins, WS, width)
    whole = whole.transpose(2, 3, 0, 4, 1, 5, 6, 7).reshape(clips, SEQ, width)
    count = SEQ // win_count
    return lax.dynamic_slice_in_dim(whole, me * count, count, axis=1), pin


def gather_small(arrays, layout):
    me = lax.axis_index("win")
    held = jnp.concatenate([a.reshape(-1) for a in arrays])[None]
    apart = 1
    while apart < layout.win_count:
        came = lax.ppermute(held, "win", [(i, i ^ apart) for i in range(layout.win_count)])
        upper = (me & apart) > 0
        first, second = jnp.where(upper, came, held), jnp.where(upper, held, came)
        held = jnp.concatenate([first, second], axis=0)
        apart *= 2
    outs, at = [], 0
    for a in arrays:
        outs.append(held[:, at : at + a.size].reshape((layout.win_count,) + a.shape))
        at += a.size
    return outs


def sum_over_win(values, layout):
    me = lax.axis_index("win")
    apart = layout.win_count // 2
    while apart > 0:
        upper = (me & apart) > 0
        first, second = values[:apart], values[apart:]
        sent = jnp.where(upper, first, second)
        kept = jnp.where(upper, second, first)
        pairs = [(i, i ^ apart) for i in range(layout.win_count)]
        values = kept + lax.ppermute(sent, "win", pairs)
        apart //= 2
    return values[0]


def sum_over_clip(values, layout):
    apart = 1
    while apart < layout.clip_size:
        pairs = [(i, i ^ apart) for i in range(layout.clip_size)]
        values = values + lax.ppermute(values, "clip", pairs)
        apart *= 2
    return values


def local(
    tokens,
    cotangent,
    modulation,
    text_features,
    null_mask,
    null_text,
    norm_gain,
    position_bias,
    self_input,
    self_output,
    cross_query,
    cross_memory,
    cross_output,
    expand_weight,
    reduce_weight,
):
    win_count = lax.axis_size("win")
    clip_size = lax.axis_size("clip")
    layout = Layout(clip_size, win_count)
    place = layout.place()
    blocks = GRID // WS
    clips, _, width = tokens.shape
    hidden_width = reduce_weight.shape[0] * clip_size
    both = ("clip", "win")
    me = lax.axis_index("win")

    input_all = lax.all_gather(self_input, both, axis=0, tiled=False)
    small = [position_bias, norm_gain.astype(single), null_text.astype(single)]
    bias_full, gain_full, null_full = gather_small(small, layout)
    bias_full = bias_full.reshape(HEADS, NREL)
    tokens, bias_full = tie(tokens, bias_full)
    windowed = to_windows(tokens, win_count)
    wins = windowed.shape[3]
    windows = clips * wins
    count = windows * WIN_TOK
    columns = width // win_count
    gain_full = gain_full.reshape(1, width)
    null_full = null_full.transpose(1, 0, 2).reshape(TXT, width).astype(bfloat)
    squares = jnp.concatenate([self_output, cross_query, cross_output, cross_memory], axis=1)
    squares, bias_full = tie(squares, bias_full)
    squares_part = layout.gather(squares, ("z",))
    squares_part, windowed = tie(squares_part, windowed)
    memory_part = layout.gather(squares_part[:, :, 3 * columns :], ("y",))
    squares_part = layout.gather(squares_part[:, :, : 3 * columns], ("x",))
    depth = expand_weight.shape[0]
    feed_shard = jnp.concatenate(
        [expand_weight]
        + [reduce_weight[i : i + depth] for i in range(0, reduce_weight.shape[0], depth)],
        axis=1,
    )
    feed_all = lax.all_gather(feed_shard, both, axis=0, tiled=False)

    shift = me if win_count == blocks else jnp.int32(0)
    shift = jnp.asarray(shift, jnp.int32).reshape(1)
    table = bias_table(bias_full, shift)
    windowed, table = tie(windowed, table)

    shape = jax.ShapeDtypeStruct
    rows = functools.partial(shape, dtype=bfloat)
    wide = rows((windows, WIN_TOK, width))
    triple = rows((3, windows, WIN_TOK, width))
    triple_spec = pl.BlockSpec((3, 1, WIN_TOK, width), lambda i: (0, i, 0, 0))
    wide_single = shape((windows, WIN_TOK, width), single)
    DMA = pltpu.SemaphoreType.DMA

    first_low, projected = pl.pallas_call(
        functools.partial(project_kernel, layout),
        grid=(windows,),
        in_specs=[window_spec(wins, width), modulation_spec(wins, width), ANY],
        out_specs=[rows_spec(width), rows_spec(3 * width)],
        out_shape=[wide, rows((windows, WIN_TOK, 3 * width))],
        scratch_shapes=[pltpu.VMEM((width, 3 * width), bfloat), DMA(())],
        compiler_params=params(),
        cost_estimate=cost(26),
        name="project",
    )(windowed, modulation, input_all)
    squares_own = layout.gather(squares_part, FIRST_ORDER[2:])
    memory_own = layout.gather(memory_part, OTHER_ORDER[2:])
    squares_own, memory_own, cotangent, projected_later = tie(
        squares_own, memory_own, cotangent, projected
    )
    squares_other = layout.swap(squares_own, "core", 1)
    memory_other = layout.swap(memory_own, "core", 1)
    grad_windowed = to_windows(cotangent, win_count)

    attended, totals = pl.pallas_call(
        attend_kernel,
        grid=(QUADS, windows),
        in_specs=[quad_spec(0), quad_spec(QUADS), quad_spec(2 * QUADS), BIAS_SPEC],
        out_specs=[quad_spec(0), TOTAL_SPEC],
        out_shape=[wide, shape((QUADS, windows, WIN_TOK, QUAD), single)],
        compiler_params=params(),
        cost_estimate=cost(47),
        name="attend",
    )(projected, projected, projected, table)

    null_flags = null_mask > 0
    used_text = jnp.where(null_flags[:, None, None], null_full[None], text_features)
    text_padded = jnp.pad(used_text, ((0, 0), (0, PADT - TXT), (0, 0)))
    stack_shape = rows((clips, QUADS, QUAD * PADT, QW))
    stack_spec = pl.BlockSpec((1, QUADS, QUAD * PADT, QW), lambda i: (i, 0, 0, 0))
    cross_keys, cross_values = pl.pallas_call(
        functools.partial(memory_kernel, layout),
        grid=(clips,),
        in_specs=[PLACE, pl.BlockSpec((1, PADT, width), lambda i: (i, 0, 0)), ANY, ANY],
        out_specs=[stack_spec, stack_spec],
        out_shape=[stack_shape, stack_shape],
        scratch_shapes=[pltpu.VMEM((width, 2 * width), bfloat), DMA(())],
        compiler_params=params(),
        cost_estimate=cost(6),
        name="memory",
    )(place, text_padded, memory_own, memory_other)

    gain_spec = pl.BlockSpec((1, width), lambda i: (0, 0))
    clip_stack_spec = pl.BlockSpec((1, QUADS, QUAD * PADT, QW), lambda i: (i // wins, 0, 0, 0))
    square = pltpu.VMEM((width, width), bfloat)
    branch, lefts, cross_queries, second_sum = pl.pallas_call(
        functools.partial(cross_kernel, layout),
        grid=(windows,),
        in_specs=[
            PLACE,
            window_spec(wins, width),
            rows_spec(width),
            modulation_spec(wins, width),
            gain_spec,
            clip_stack_spec,
            clip_stack_spec,
            ANY,
            ANY,
        ],
        out_specs=[rows_spec(width), triple_spec, rows_spec(width), rows_spec(width)],
        out_shape=[wide_single, triple, wide, wide_single],
        scratch_shapes=[square, square, square, DMA((3,))],
        compiler_params=params(),
        cost_estimate=cost(42),
        name="cross",
    )(
        place,
        windowed,
        attended,
        modulation,
        gain_full,
        cross_keys,
        cross_values,
        squares_own,
        squares_other,
    )

    window_shape = rows(windowed.shape)
    block_windowed, third_low, activated, grad_hidden, grad_reduced, grad_second_sum, feed_mod = (
        pl.pallas_call(
            functools.partial(feed_kernel, layout, wins, 1024),
            grid=(windows,),
            in_specs=[
                rows_spec(width),
                window_spec(wins, width),
                modulation_spec(wins, width),
                ANY,
            ],
            out_specs=[
                window_spec(wins, width),
                rows_spec(width),
                rows_spec(hidden_width),
                rows_spec(hidden_width),
                rows_spec(width),
                rows_spec(width),
                pl.BlockSpec((1, 3, width), lambda i: (i // wins, 0, 0)),
            ],
            out_shape=[
                window_shape,
                wide,
                rows((windows, WIN_TOK, hidden_width)),
                rows((windows, WIN_TOK, hidden_width)),
                wide,
                wide_single,
                shape((clips, 3, width), single),
            ],
            scratch_shapes=[
                pltpu.VMEM((width, hidden_width), bfloat),
                pltpu.VMEM((hidden_width, width), bfloat),
                DMA((2,)),
            ],
            compiler_params=params(),
            cost_estimate=cost(117),
        name="feed",
        )(second_sum, grad_windowed, modulation, feed_all)
    )

    def flat(values):
        return values.reshape(-1, count, values.shape[-1])

    expand_of = (layout, place, flat(third_low), flat(grad_hidden), 1)
    reduce_of = (layout, place, flat(activated)[0], flat(grad_reduced)[0])
    reduce_sent = layout.swap(weight_grad_rows(*reduce_of, 1, None, "reduce_other"), "core", 1)
    expand_sent = layout.swap(weight_grad(*expand_of, 1, None, "expand_other"), "core", 1)
    reduce_term = weight_grad_rows(*reduce_of, 0, reduce_sent, "reduce_own")
    block_output, reduce_term = from_windows(block_windowed, win_count, reduce_term)
    expand_sent, reduce_term, block_output = tie(expand_sent, reduce_term, block_output)
    expand_term = weight_grad(*expand_of, 0, expand_sent, "expand_own")
    grad_second_sum, expand_term = tie(grad_second_sum, expand_term)

    rights, grad_first_sum, grad_attended, memory_t, gain_term, gate_mod = pl.pallas_call(
        functools.partial(cross_back_kernel, layout, wins),
        grid=(windows,),
        in_specs=[
            PLACE,
            window_spec(wins, width),
            modulation_spec(wins, width),
            gain_spec,
            clip_stack_spec,
            clip_stack_spec,
            rows_spec(width),
            rows_spec(width),
            rows_spec(width),
            ANY,
            ANY,
        ],
        out_specs=[
            triple_spec,
            rows_spec(width),
            rows_spec(width),
            pl.BlockSpec((1, 2 * width, PADT), lambda i: (i // wins, 0, 0)),
            gain_spec,
            pl.BlockSpec((1, 1, width), lambda i: (i // wins, 0, 0)),
        ],
        out_shape=[
            triple,
            wide_single,
            wide,
            shape((clips, 2 * width, PADT), single),
            shape((1, width), single),
            shape((clips, 1, width), single),
        ],
        scratch_shapes=[square, square, square, DMA((3,))],
        compiler_params=params(),
        cost_estimate=cost(63),
        name="cross_back",
    )(
        place,
        windowed,
        modulation,
        gain_full,
        cross_keys,
        cross_values,
        grad_second_sum,
        cross_queries,
        branch,
        squares_own,
        squares_other,
    )
    reduce_stage, grad_attended = layout.reduce(reduce_term, "y", grad_attended)
    rights, memory_t, reduce_stage = tie(rights, memory_t, reduce_stage)

    text_t = text_padded.reshape(1, clips * PADT, width)
    memory_low = memory_t.astype(bfloat).transpose(0, 2, 1).reshape(1, clips * PADT, 2 * width)
    square_of = (layout, place, flat(lefts), flat(rights), 1)
    memory_of = (layout, place, text_t, memory_low, 1)
    square_sent = layout.swap(weight_grad(*square_of, 1, None, "square_other"), "core", 1)
    memory_sent = layout.swap(weight_grad(*memory_of, 1, None, "memory_other"), "core", 1)
    expand_stage, memory_sent = layout.reduce(expand_term, "y", memory_sent)
    square_sent, memory_sent, expand_stage = tie(square_sent, memory_sent, expand_stage)
    square_term = weight_grad(*square_of, 0, square_sent, "square_own")
    memory_sent, square_term = tie(memory_sent, square_term)
    memory_term = weight_grad(*memory_of, 0, memory_sent, "memory_own")
    reduce_stage, memory_term = layout.reduce(reduce_stage, "x", memory_term)
    expand_stage, memory_term = layout.reduce(expand_stage, "x", memory_term)
    feed_stage = pack(1, columns, expand_stage, reduce_stage)
    grad_attended, feed_stage, square_term, memory_term = tie(
        grad_attended, feed_stage, square_term, memory_term
    )

    grad_projected, bias_sum = pl.pallas_call(
        attend_back_kernel,
        grid=(QUADS, windows),
        in_specs=[
            quad_spec(0),
            quad_spec(QUADS),
            quad_spec(2 * QUADS),
            quad_spec(0),
            BIAS_SPEC,
            TOTAL_SPEC,
        ],
        out_specs=[
            pl.BlockSpec((3, 1, WIN_TOK, QW), lambda q, i: (0, i, 0, q)),
            BIAS_SPEC,
        ],
        out_shape=[triple, shape((QUADS, WIN_TOK, QUAD * PADK), single)],
        compiler_params=params(),
        cost_estimate=cost(72),
        name="attend_back",
    )(projected_later, projected_later, projected_later, grad_attended, table, totals)

    input_of = (layout, place, flat(first_low), flat(grad_projected), 3)
    feed_stage, bias_sum = layout.reduce(feed_stage, "z", bias_sum, 0, 1)
    square_stage, bias_sum = layout.reduce(square_term, "y", bias_sum)
    memory_stage, bias_sum = layout.reduce(memory_term, "y", bias_sum)
    rest_stage = pack(2, columns, square_stage, memory_stage)
    grad_projected, rest_stage, feed_stage = tie(grad_projected, rest_stage, feed_stage)
    input_of = (layout, place, flat(first_low), flat(grad_projected), 3)
    input_sent = weight_grad(*input_of, 1, None, "input_other", True)
    masked = jnp.sum(jnp.where(null_flags[:, None, None], memory_t[:, :, :TXT], 0.0), axis=0)
    masked = jnp.pad(masked.T, ((0, 128 - TXT), (0, 0)))
    input_sent, masked = tie(input_sent, masked)
    input_sent = layout.swap(input_sent, "core", 1)
    null_term = null_text_term(layout, place, masked, memory_own, memory_other)[:TXT]
    input_sent, null_term = tie(input_sent, null_term)
    input_term = weight_grad(*input_of, 0, input_sent, "input_own", True)
    feed_grad, input_term = layout.reduce(feed_stage, "z", input_term, 1)
    rest_stage, input_term = layout.reduce(rest_stage, "x", input_term)
    grad_projected, rest_stage, feed_grad, input_term = tie(
        grad_projected, rest_stage, feed_grad, input_term
    )

    tokens_windowed, first_mod = pl.pallas_call(
        functools.partial(input_back_kernel, layout, wins),
        grid=(windows,),
        in_specs=[
            window_spec(wins, width),
            modulation_spec(wins, width),
            triple_spec,
            rows_spec(width),
            ANY,
        ],
        out_specs=[
            window_spec(wins, width),
            pl.BlockSpec((1, 2, width), lambda i: (i // wins, 0, 0)),
        ],
        out_shape=[window_shape, shape((clips, 2, width), single)],
        scratch_shapes=[pltpu.VMEM((width, 3 * width), bfloat), DMA(())],
        compiler_params=params(),
        cost_estimate=cost(29),
        name="input_back",
    )(windowed, modulation, grad_projected, grad_first_sum, input_all)
    rest_grad, tokens_windowed = layout.reduce(rest_stage, "z", tokens_windowed)
    input_stage, tokens_windowed = layout.reduce(input_term, "x", tokens_windowed)
    bias_sum, tokens_windowed = tie(bias_sum, tokens_windowed)
    tokens_grad, _ = from_windows(tokens_windowed, win_count, None)
    input_stage, _ = layout.reduce(input_stage, "y", None)
    self_input_grad = layout.reduce(input_stage, "z", None)[0][0]
    expand_grad, reduce_grad = unpack(feed_grad, ((depth, 4 * columns), (4 * depth, columns)))
    square_grads, cross_memory_grad = unpack(
        rest_grad, ((3 * depth, columns), (depth, 2 * columns))
    )
    square_grads = square_grads.reshape(3, depth, columns)
    heads_local = HEADS // win_count
    position_term = bias_collect(bias_sum, shift)
    modulation_term = jnp.concatenate([first_mod, gate_mod, feed_mod], axis=1)
    by_columns = jnp.concatenate(
        [modulation_term.reshape(clips * 6, width), gain_term, null_term], axis=0
    )
    by_columns = by_columns.reshape(-1, win_count, columns).transpose(1, 0, 2)
    small_term = jnp.concatenate(
        [
            by_columns.reshape(win_count, -1),
            position_term.reshape(win_count, heads_local * NREL),
        ],
        axis=1,
    )
    small_term = sum_over_win(small_term, layout)
    modulation_grad = small_term[: clips * 6 * columns].reshape(clips, 6, columns)
    small_grad = sum_over_clip(small_term[clips * 6 * columns :], layout)
    gain_grad = small_grad[:columns]
    null_grad = small_grad[columns : (1 + TXT) * columns].reshape(TXT, columns)
    position_grad = small_grad[(1 + TXT) * columns :].reshape(heads_local, NREL)
    self_output_grad, cross_query_grad, cross_output_grad = square_grads
    return (
        block_output,
        tokens_grad,
        self_input_grad,
        self_output_grad,
        cross_query_grad,
        cross_memory_grad,
        cross_output_grad,
        expand_grad,
        reduce_grad,
        gain_grad,
        null_grad,
        position_grad,
        modulation_grad,
    )


def solution(mesh):
    in_specs = (
        P("clip", "win", None),
        P("clip", "win", None),
        P("clip", None, None),
        P("clip", None, None),
        P("clip"),
        P(None, "win"),
        P("win"),
        P("win", None),
        P("clip", "win"),
        P("clip", "win"),
        P("clip", "win"),
        P("clip", "win"),
        P("clip", "win"),
        P("clip", "win"),
        P("clip", "win"),
    )
    out_specs = (
        P("clip", "win", None),
        P("clip", "win", None),
        P("clip", "win"),
        P("clip", "win"),
        P("clip", "win"),
        P("clip", "win"),
        P("clip", "win"),
        P("clip", "win"),
        P("clip", "win"),
        P("win"),
        P(None, "win"),
        P("win", None),
        P("clip", None, "win"),
    )
    return jax.shard_map(local, mesh=mesh, in_specs=in_specs, out_specs=out_specs, check_vma=False)
```

time: 2220 us -> 1040 us (0.47)
  matrix products: 703 us -> 8.61 us
  local copies, waits for them, and re-layouts: 764 us -> 103 us
  Pallas kernels: 0 us -> 587 us
  blocking collectives: 312 us -> 0 us
  other arithmetic: 145 us -> 53.5 us
    dot_general x88 -> x2, matrix products: 691 us -> 8.61 us  [the longest x1 5.05 us: bias_collect(): lax.dot_general(flat, side_hot(), NT, precision=lax.Precision.HIGHEST)]
    pallas_call x0 -> x21, Pallas kernels: none -> 587 us  [the longest x1 118 us: local(): pl.pallas_call(functools.partial(feed_kernel, layout, wins, 1024), grid=(...]
    all_gather x7 -> x0, blocking collectives: 270 us -> none  [the longest x1 61.9 us: local(): lax.all_gather(self_output, 'win', axis=1, tiled=True)]
    reshape x18 -> x6, local copies, waits for them, and re-layouts: 277 us -> 8.31 us  [the longest x1 5.31 us: bias_collect(): flat = blocks.reshape(HEADS * FSPAN, SIDE * SIDE)]
    ppermute x0 -> x47, waiting for transfers between devices: none -> 226 us  [the longest x28 135 us: swap(): return lax.ppermute(values, home, [(i, i ^ step) for i in range(count)])]
    while x40 -> x0, local copies, waits for them, and re-layouts: 140 us -> none  [the longest x5 85.5 us: local(): lax.map(attend_group, (group_queries_all, group_keys_all, group_values_all))]
    reduce_sum x26 -> x1, other arithmetic: 89.4 us -> 1.24 us  [local(): jnp.sum(jnp.where(null_flags[:, None, None], memory_t[:, :, :TXT], 0.0),...]
    reduce_scatter x15 -> x0, waiting for transfers between devices: 78.1 us -> none  [the longest x1 25.9 us: local(): lax.psum_scatter(by_rows[6].astype(jnp.bfloat16), 'win', scatter_dimensio...]
  transfers between devices with their start and end apart: 33 -> 49, of which waited for: 7 -> 21; matrix products, arithmetic and copies ran while one was open for 64% -> 13% of each run, Pallas kernels for 0% -> 39%
where the time goes in v1:
time: 1040 us
  Pallas kernels  587 us (56%)
  waiting for transfers between devices  227 us (22%)
  local copies, waits for them, and re-layouts  103 us (10%)
  other arithmetic  53.5 us (5%)
  starting transfers between devices  41.3 us (4%)
  between operations  15.3 us (1%)
    ppermute x28, waiting for transfers between devices, swap(): return lax.ppermute(values, home, [(i, i ^ step) for i in range(count)])  135 us
    pallas_call x1, Pallas kernels, local(): pl.pallas_call(functools.partial(feed_kernel, layout, wins, 1024), grid=(...  118 us
    pallas_call x8, Pallas kernels, weight_grad(): pl.pallas_call(functools.partial(columns_kernel, layout, pieces, added is...  113 us
    pallas_call x1, Pallas kernels, local(): pl.pallas_call(attend_back_kernel, grid=(QUADS, windows), in_specs=[quad_...  72.8 us
    pallas_call x1, Pallas kernels, local(): pl.pallas_call(functools.partial(cross_back_kernel, layout, wins), grid=(...  64.4 us
    ppermute x6, waiting for transfers between devices, from_windows(): sent[k] = lax.ppermute(parts[:, FRAMES - k], 'win', pairs)  47.3 us
    pallas_call x1, Pallas kernels, local(): pl.pallas_call(attend_kernel, grid=(QUADS, windows), in_specs=[quad_spec(...  47 us
    pallas_call x1, Pallas kernels, local(): pl.pallas_call(functools.partial(cross_kernel, layout), grid=(windows,),...  42.8 us
  transfers between devices with their start and end apart: 49, of which 21 were waited for; matrix products, arithmetic and copies ran while one was open for 13% of the time, Pallas kernels for 39%

profile of v1, /device:TPU:0, one launch (start us, length us, event | category | flops | bytes accessed | tf_op | source)
XLA Modules:
  0.0 1036.5 jit_solution(15317026425660403603)
XLA Ops:
  17.5 2.9 collective-permute-start.1
  21.4 6.2 collective-permute-done.1
  30.7 3.1 fusion.76
  34.1 5.5 collective-permute-done.2
  45.4 35.0 %collective-permute-done.3 = bf16[2,128,1280]{2,1,0:T(8,128)(2,1)S(1)} collective-permute-done((bf16[2,128,1280]{2,1,0:T(8,128)(2,1)S(1)}, bf16[2,128,1280]{2,1,0:T(8,128)(2,1)S(1)}, u32[]{:S(2)}, u32[]{:S(2)}) %collective-permute-start.3) | collective-permute-done | bytes 655392 | tf_op jit(solution)/shard_map/ppermute | solution.py:100
  81.6 4.1 collective-permute-done.5
  86.8 11.9 %collective-permute-done.6 = bf16[2,256,1024]{2,1,0:T(8,128)(2,1)S(1)} collective-permute-done((bf16[2,256,1024]{2,1,0:T(8,128)(2,1)S(1)}, bf16[2,256,1024]{2,1,0:T(8,128)(2,1)S(1)}, u32[]{:S(2)}, u32[]{:S(2)}) %collective-permute-start.6) | collective-permute-done | bytes 1048608 | tf_op jit(solution)/shard_map/ppermute | solution.py:786
  102.4 10.8 %collective-permute-done.9 = bf16[4,128,512]{2,1,0:T(8,128)(2,1)S(1)} collective-permute-done((bf16[4,128,512]{2,1,0:T(8,128)(2,1)S(1)}, bf16[4,128,512]{2,1,0:T(8,128)(2,1)S(1)}, u32[]{:S(2)}, u32[]{:S(2)}) %collective-permute-start.9) | collective-permute-done | bytes 524320 | tf_op jit(solution)/shard_map/ppermute | solution.py:100
  115.1 5.3 collective-permute-done.7
  123.3 6.7 fusion.4
  131.6 3.6 fusion.55
  135.2 3.7 copy.80.block_ref
  138.9 12.0 %bias_table.1.bias_ref = f32[4,320,1536]{2,1,0:T(8,128)} custom-call(s32[1]{0:T(128)} %bitcast.10.shift_ref, f32[16,9,64,64]{3,2,1,0:T(8,128)} %copy.80.block_ref), custom_call_target="tpu_custom_call" | custom-call | flops 9120000 | bytes 12000 | tf_op jit(solution)/shard_map/bias_table/pallas_call | solution.py:266
  151.0 2.9 pad_maximum_fusion.2.own_any
  153.9 10.7 %collective-permute-done.8 = bf16[8,128,768]{2,1,0:T(8,128)(2,1)} collective-permute-done((bf16[8,128,768]{2,1,0:T(8,128)(2,1)}, bf16[8,128,768]{2,1,0:T(8,128)(2,1)}, u32[]{:S(2)}, u32[]{:S(2)}) %collective-permute-start.8) | collective-permute-done | bytes 1572896 | tf_op jit(solution)/shard_map/ppermute | solution.py:100
  166.3 26.3 %project.1 = (bf16[8,320,1024]{2,1,0:T(8,128)(2,1)}, bf16[8,320,3072]{2,1,0:T(8,128)(2,1)}) custom-call(bf16[2,5,8,4,8,1024]{5,4,3,2,1,0:T(8,128)(2,1)} %constant_dynamic-update-slice_fusion.tokens_ref, f32[2,6,1024]{2,1,0:T(8,128)} %copy.81.mod_ref, bf16[32,128,768]{2,1,0:T(8,128)(2,1)} %bitcast.148), custom_call_target="tpu_custom_call" | custom-call | flops 19760000 | bytes 26000 | tf_op jit(solution)/shard_map/project/pallas_call | solution.py:927
  192.6 5.1 fusion.75
  205.8 47.0 %attend.1 = (bf16[8,320,1024]{2,1,0:T(8,128)(2,1)}, f32[4,8,320,4]{3,2,1,0:T(8,128)}) custom-call(bf16[8,320,3072]{2,1,0:T(8,128)(2,1)} %get-tuple-element.169.q_ref.k_ref.v_ref, bf16[8,320,3072]{2,1,0:T(8,128)(2,1)} %get-tuple-element.169.q_ref.k_ref.v_ref, bf16[8,320,3072]{2,1,0:T(8,128)(2,1)} %get-tuple-element.169.q_ref.k_ref.v_ref, ...), custom_call_target="tpu_custom_call" | custom-call | flops 35720000 | bytes 47000 | tf_op jit(solution)/shard_map/attend/pallas_call | solution.py:947
  252.8 2.4 constant_dynamic-update-slice_fusion.9
  255.2 2.3 constant_dynamic-update-slice_fusion.8
  257.5 2.4 constant_dynamic-update-slice_fusion.7
  259.9 2.3 constant_dynamic-update-slice_fusion.6
  264.5 6.0 memory.1
  270.5 42.8 %cross.1 = (f32[8,320,1024]{2,1,0:T(8,128)}, bf16[3,8,320,1024]{3,2,1,0:T(8,128)(2,1)}, bf16[8,320,1024]{2,1,0:T(8,128)(2,1)}, f32[8,320,1024]{2,1,0:T(8,128)}) custom-call(s32[4]{0:T(128)} %pad_add_fusion.place_ref, bf16[2,5,8,4,8,1024]{5,4,3,2,1,0:T(8,128)(2,1)} %constant_dynamic-update-slice_fusion.tokens_ref, ...), custom_call_target="tpu_custom_call" | custom-call | flops 31920000 | bytes 42000 | tf_op jit(solution)/shard_map/cross/pallas_call | solution.py:978
  313.4 117.5 %feed.1 = (bf16[2,5,8,4,8,1024]{5,4,3,2,1,0:T(8,128)(2,1)}, bf16[8,320,1024]{2,1,0:T(8,128)(2,1)}, bf16[8,320,4096]{2,1,0:T(8,128)(2,1)}, bf16[8,320,4096]{2,1,0...) custom-call(f32[8,320,1024]{2,1,0:T(8,128)} %get-tuple-element.127.sum_ref, ...), custom_call_target="tpu_custom_call" | custom-call | flops 88920000 | bytes 117000 | tf_op jit(solution)/shard_map/feed/pallas_call | solution.py:1012
  430.9 18.0 %reduce_other.1 = bf16[2,2,4,512,256]{4,3,2,1,0:T(8,128)(2,1)} custom-call(s32[4]{0:T(128)} %pad_add_fusion.place_ref, bf16[2560,4096]{1,0:T(8,128)(2,1)} %bitcast.150, bf16[2560,1024]{1,0:T(8,128)(2,1)} %bitcast.154, bf16[2560,1024]{1,0:T(8,128)(2,1)} %bitcast.155), custom_call_target="tpu_custom_call" | custom-call | flops 10681201664 | bytes 14054212 | tf_op jit(solution)/shard_map/reduce_other/pallas_call | solution.py:760
  449.0 17.7 %expand_other.1 = bf16[2,2,4,1,128,1024]{5,4,3,2,1,0:T(8,128)(2,1)} custom-call(s32[4]{0:T(128)} %pad_add_fusion.place_ref, bf16[1,2560,1024]{2,1,0:T(8,128)(2,1)} %bitcast.192, bf16[1,2560,4096]{2,1,0:T(8,128)(2,1)} %bitcast.190), custom_call_target="tpu_custom_call" | custom-call | flops 10681201664 | bytes 14054212 | tf_op jit(solution)/shard_map/expand_other/pallas_call | solution.py:714
  467.2 4.7 slice_dynamic-update-slice_fusion.3
  473.6 18.4 %reduce_own.1 = bf16[2,2,4,512,256]{4,3,2,1,0:T(8,128)(2,1)} custom-call(s32[4]{0:T(128)} %pad_add_fusion.place_ref, bf16[2560,4096]{1,0:T(8,128)(2,1)} %bitcast.151, bf16[2560,1024]{1,0:T(8,128)(2,1)} %bitcast.156, bf16[2560,1024]{1,0:T(8,128)(2,1)} %bitcast.157, bf16[2,2,4,512,256]{4,3,2,1,0:T(8,128)(2,1)} %collective-permute-done.20.refs_2_), custom_call_target="tpu_custom_call" | custom-call | flops 10681201664 | bytes 14054212 | tf_op jit(solution)/shard_map/reduce_own/pallas_call | solution.py:760
  492.0 5.2 collective-permute-done.17
  497.1 23.0 %collective-permute-done.18 = bf16[2,256,1024]{2,1,0:T(8,128)(2,1)S(1)} collective-permute-done((bf16[2,256,1024]{2,1,0:T(8,128)(2,1)}, bf16[2,256,1024]{2,1,0:T(8,128)(2,1)S(1)}, u32[]{:S(2)}, u32[]{:S(2)}) %collective-permute-start.18) | collective-permute-done | bytes 1048608 | tf_op jit(solution)/shard_map/ppermute | solution.py:808
  523.2 2.3 slice_dynamic-update-slice_fusion.2
  528.5 19.0 %expand_own.1 = bf16[2,2,4,1,128,1024]{5,4,3,2,1,0:T(8,128)(2,1)} custom-call(s32[4]{0:T(128)} %pad_add_fusion.place_ref, bf16[1,2560,1024]{2,1,0:T(8,128)(2,1)} %bitcast.193, bf16[1,2560,4096]{2,1,0:T(8,128)(2,1)} %bitcast.191, bf16[2,2,4,1,128,1024]{5,4,3,2,1,0:T(8,128)(2,1)} %collective-permute-done.16.refs_1_), custom_call_target="tpu_custom_call" | custom-call | flops 10681201664 | bytes 14054212 | tf_op jit(solution)/shard_map/expand_own/pallas_call | solution.py:714
  547.5 64.4 %cross_back.1 = (bf16[3,8,320,1024]{3,2,1,0:T(8,128)(2,1)}, f32[8,320,1024]{2,1,0:T(8,128)}, bf16[8,320,1024]{2,1,0:T(8,128)(2,1)}, f32[2,2048,128]{2,1,0:T(8,12...) custom-call(s32[4]{0:T(128)} %pad_add_fusion.place_ref, ...), custom_call_target="tpu_custom_call" | custom-call | flops 47880000 | bytes 63000 | tf_op jit(solution)/shard_map/cross_back/pallas_call | solution.py:1063
  613.2 2.7 fusion.32
  615.9 17.7 %square_other.1 = bf16[2,2,4,3,128,256]{5,4,3,2,1,0:T(8,128)(2,1)} custom-call(s32[4]{0:T(128)} %pad_add_fusion.place_ref, bf16[3,2560,1024]{2,1,0:T(8,128)(2,1)} %bitcast.144, bf16[3,2560,1024]{2,1,0:T(8,128)(2,1)} %bitcast.146), custom_call_target="tpu_custom_call" | custom-call | flops 8010900992 | bytes 10540659 | tf_op jit(solution)/shard_map/square_other/pallas_call | solution.py:714
  633.6 3.2 slice.302
  638.8 4.0 memory_other.1
  645.5 39.6 %collective-permute-done.23 = bf16[1,2,4,1,128,1024]{5,4,3,2,1,0:T(8,128)(2,1)} collective-permute-done((bf16[1,2,4,1,128,1024]{5,4,3,2,1,0:T(8,128)(2,1)}, bf16[1,2,4,1,128,1024]{5,4,3,2,1,0:T(8,128)(2,1)}, u32[]{:S(2)}, u32[]{:S(2)}) %collective-permute-start.23) | collective-permute-done | bytes 2097184 | tf_op jit(solution)/shard_map/ppermute | solution.py:100
  685.1 3.2 fusion.33
  692.1 18.6 %square_own.1 = bf16[2,2,4,3,128,256]{5,4,3,2,1,0:T(8,128)(2,1)} custom-call(s32[4]{0:T(128)} %pad_add_fusion.place_ref, bf16[3,2560,1024]{2,1,0:T(8,128)(2,1)} %bitcast.145, bf16[3,2560,1024]{2,1,0:T(8,128)(2,1)} %bitcast.147, bf16[2,2,4,3,128,256]{5,4,3,2,1,0:T(8,128)(2,1)} %collective-permute-done.22.refs_1_), custom_call_target="tpu_custom_call" | custom-call | flops 8010900992 | bytes 10540659 | tf_op jit(solution)/shard_map/square_own/pallas_call | solution.py:714
  710.7 4.6 memory_own.1
  727.3 2.4 copy.91
  731.8 72.8 %attend_back.1 = (bf16[3,8,320,1024]{3,2,1,0:T(8,128)(2,1)}, f32[4,320,1536]{2,1,0:T(8,128)}) custom-call(bf16[8,320,3072]{2,1,0:T(8,128)(2,1)} %get-tuple-element.169.q_ref.k_ref.v_ref, bf16[8,320,3072]{2,1,0:T(8,128)(2,1)} %get-tuple-element.169.q_ref.k_ref.v_ref, bf16[8,320,3072]{2,1,0:T(8,128)(2,1)} %get-tuple-element.169.q_ref.k_ref.v_ref, ...), custom_call_target="tpu_custom_call" | custom-call | flops 54720000 | bytes 72000 | tf_op jit(solution)/shard_map/attend_back/pallas_call | solution.py:1133
  804.7 2.9 add_convert_fusion.5
  811.4 15.3 %input_other.1 = bf16[2,2,4,1,128,768]{5,4,3,2,1,0:T(8,128)(2,1)} custom-call(s32[4]{0:T(128)} %pad_add_fusion.place_ref, bf16[1,2560,1024]{2,1,0:T(8,128)(2,1)} %bitcast.152, bf16[3,2560,1024]{2,1,0:T(8,128)(2,1)} %bitcast.138, bf16[3,2560,1024]{2,1,0:T(8,128)(2,1)} %bitcast.139, bf16[3,2560,1024]{2,1,0:T(8,128)(2,1)} %bitcast.140), custom_call_target="tpu_custom_call" | custom-call | flops 8010900992 | bytes 10540659 | tf_op jit(solution)/shard_map/input_other/pallas_call | solution.py:714
  829.0 7.2 null_text.1
  837.1 2.7 collective-permute-start.31
  839.8 16.2 %input_own.1 = bf16[2,2,4,1,128,768]{5,4,3,2,1,0:T(8,128)(2,1)} custom-call(s32[4]{0:T(128)} %pad_add_fusion.place_ref, bf16[1,2560,1024]{2,1,0:T(8,128)(2,1)} %bitcast.153, bf16[3,2560,1024]{2,1,0:T(8,128)(2,1)} %bitcast.141, bf16[3,2560,1024]{2,1,0:T(8,128)(2,1)} %bitcast.142, bf16[3,2560,1024]{2,1,0:T(8,128)(2,1)} %bitcast.143, ...), custom_call_target="tpu_custom_call" | custom-call | flops 8010900992 | bytes 10540659 | tf_op jit(solution)/shard_map/input_own/pallas_call | solution.py:714
  856.0 7.6 collective-permute-done.31
  872.5 29.4 %input_back.1 = (bf16[2,5,8,4,8,1024]{5,4,3,2,1,0:T(8,128)(2,1)}, f32[2,2,1024]{2,1,0:T(2,128)}) custom-call(bf16[2,5,8,4,8,1024]{5,4,3,2,1,0:T(8,128)(2,1)} %constant_dynamic-update-slice_fusion.tokens_ref, f32[2,6,1024]{2,1,0:T(8,128)} %copy.81.mod_ref, bf16[3,8,320,1024]{3,2,1,0:T(8,128)(2,1)} %get-tuple-element.193.grad_ref, ...), custom_call_target="tpu_custom_call" | custom-call | flops 22040000 | bytes 29000 | tf_op jit(solution)/shard_map/input_back/pallas_call | solution.py:1175
  908.7 3.3 collective-permute-start.35
  912.9 12.9 %collective-permute-done.35 = bf16[1,640,256]{2,1,0:T(8,128)(2,1)S(1)} collective-permute-done((bf16[1,640,256]{2,1,0:T(8,128)(2,1)S(1)}, bf16[1,640,256]{2,1,0:T(8,128)(2,1)S(1)}, u32[]{:S(2)}, u32[]{:S(2)}) %collective-permute-start.35) | collective-permute-done | bytes 327712 | tf_op jit(solution)/shard_map/ppermute | solution.py:100
  926.7 12.2 %bias_collect.1 = f32[16,9,64,64]{3,2,1,0:T(8,128)} custom-call(s32[1]{0:T(128)} %bitcast.10.shift_ref, f32[4,320,1536]{2,1,0:T(8,128)} %get-tuple-element.212.sum_ref), custom_call_target="tpu_custom_call" | custom-call | flops 9120000 | bytes 12000 | tf_op jit(solution)/shard_map/bias_collect/pallas_call | solution.py:282
  938.9 5.3 reshape.317
  944.3 5.1 fusion.30
  960.4 4.6 slice_bitcast_fusion
  969.5 9.9 collective-permute-done.44
  980.3 4.0 collective-permute-done.45
  985.1 5.7 collective-permute-done.46
  994.2 19.2 %collective-permute-done.37 = bf16[2,256,1024]{2,1,0:T(8,128)(2,1)} collective-permute-done((bf16[2,256,1024]{2,1,0:T(8,128)(2,1)}, bf16[2,256,1024]{2,1,0:T(8,128)(2,1)}, u32[]{:S(2)}, u32[]{:S(2)}) %collective-permute-start.37) | collective-permute-done | bytes 1048608 | tf_op jit(solution)/shard_map/ppermute | solution.py:808
  1014.4 2.3 bitcast_dynamic-update-slice_fusion.1
  1019.2 2.3 slice_dynamic-update-slice_fusion
  1021.4 7.2 collective-permute-done.41
  (279 shorter events, 126.1 us)
Async XLA Ops:
  7.2 159.1 %all-gather.5.cloned.1.call-start = ((), (), s32[]{:S(2)}) async-start(), calls=%async_computation | async-start | bytes 6488064 | tf_op jit(solution)/shard_map/all_gather | solution.py:888
  7.9 305.4 %all-gather.7.cloned.1.call-start = ((), (), s32[]{:S(2)}) async-start(), calls=%async_computation.1 | async-start | bytes 17301504 | tf_op jit(solution)/shard_map/all_gather | solution.py:912
  15.6 1.5 collective-permute-start
  17.5 10.1 collective-permute-start.1
  28.8 10.8 %collective-permute-start.2 = (bf16[1,128,1280]{2,1,0:T(8,128)(2,1)S(1)}, bf16[1,128,1280]{2,1,0:T(8,128)(2,1)S(1)}, u32[]{:S(2)}, u32[]{:S(2)}) collective-permute-start(bf16[1,128,1280]{2,1,0:T(8,128)(2,1)S(1)} %bitcast.176), channel_id=1, source_target_pairs={{0,8},{4,12},{8,0},{12,4},{16,24},{20,28},{24,16},{28,20},{1,9},{5... | collective-permute-start | bytes 983048 | tf_op jit(solution)/shard_map/ppermute | solution.py:100
  33.8 46.7 %collective-permute-start.4 = (bf16[2,256,1024]{2,1,0:T(8,128)(2,1)S(1)}, bf16[2,256,1024]{2,1,0:T(8,128)(2,1)S(1)}, u32[]{:S(2)}, u32[]{:S(2)}) collective-permute-start(bf16[2,256,1024]{2,1,0:T(8,128)(2,1)S(1)} %get-tuple-element.267), channel_id=1, source_target_pairs={{0,3},{1,0},{2,1},{3,2},{4,7},{5,4},{6,5},{7,6},{8,11},{9,8},{10,9... | collective-permute-start | bytes 3145736 | tf_op jit(solution)/shard_map/ppermute | solution.py:786
  39.7 40.7 %collective-permute-start.3 = (bf16[2,128,1280]{2,1,0:T(8,128)(2,1)S(1)}, bf16[2,128,1280]{2,1,0:T(8,128)(2,1)S(1)}, u32[]{:S(2)}, u32[]{:S(2)}) collective-permute-start(bf16[2,128,1280]{2,1,0:T(8,128)(2,1)S(1)} %pad_maximum_fusion.6), channel_id=1, source_target_pairs={{0,16},{4,20},{8,24},{12,28},{16,0},{20,4},{24,8},{28,12},{1,17},{... | collective-permute-start | bytes 1966088 | tf_op jit(solution)/shard_map/ppermute | solution.py:100
  41.9 43.8 %collective-permute-start.5 = (bf16[2,256,1024]{2,1,0:T(8,128)(2,1)S(1)}, bf16[2,256,1024]{2,1,0:T(8,128)(2,1)S(1)}, u32[]{:S(2)}, u32[]{:S(2)}) collective-permute-start(bf16[2,256,1024]{2,1,0:T(8,128)(2,1)S(1)} %get-tuple-element.266), channel_id=1, source_target_pairs={{0,2},{1,3},{2,0},{3,1},{4,6},{5,7},{6,4},{7,5},{8,10},{9,11},{10,... | collective-permute-start | bytes 3145736 | tf_op jit(solution)/shard_map/ppermute | solution.py:786
  43.2 55.5 %collective-permute-start.6 = (bf16[2,256,1024]{2,1,0:T(8,128)(2,1)S(1)}, bf16[2,256,1024]{2,1,0:T(8,128)(2,1)S(1)}, u32[]{:S(2)}, u32[]{:S(2)}) collective-permute-start(bf16[2,256,1024]{2,1,0:T(8,128)(2,1)S(1)} %get-tuple-element.265), channel_id=1, source_target_pairs={{0,1},{1,2},{2,3},{3,0},{4,5},{5,6},{6,7},{7,4},{8,9},{9,10},{10,1... | collective-permute-start | bytes 3145736 | tf_op jit(solution)/shard_map/ppermute | solution.py:786
  99.8 20.6 %copy-start.11 = (bf16[4,128,768]{2,1,0:T(8,128)(2,1)}, bf16[4,128,768]{2,1,0:T(8,128)(2,1)S(1)}, u32[]{:S(2)}) copy-start(bf16[4,128,768]{2,1,0:T(8,128)(2,1)S(1)} %slice.284) | copy-start | bytes 2359300
  99.8 30.2 %copy-start.33 = (f32[2,6,1024]{2,0,1:T(2,128)S(1)}, f32[2,6,1024]{2,0,1:T(2,128)}, u32[]{:S(2)}) copy-start(f32[2,6,1024]{2,0,1:T(2,128)} %param.17) | copy-start | bytes 147460
  99.8 31.6 %copy-start.41 = (s32[2]{0:T(128)S(1)}, s32[2]{0:T(128)}, u32[]{:S(2)}) copy-start(s32[2]{0:T(128)} %param.19) | copy-start | bytes 28
  99.8 20.5 %collective-permute-start.7 = (bf16[4,128,768]{2,1,0:T(8,128)(2,1)S(1)}, bf16[4,128,768]{2,1,0:T(8,128)(2,1)S(1)}, u32[]{:S(2)}, u32[]{:S(2)}) collective-permute-start(bf16[4,128,768]{2,1,0:T(8,128)(2,1)S(1)} %slice.284), channel_id=1, source_target_pairs={{0,2},{1,3},{2,0},{3,1},{4,6},{5,7},{6,4},{7,5},{8,10},{9,11},{10,... | collective-permute-start | bytes 2359304 | tf_op jit(solution)/shard_map/ppermute | solution.py:100
  100.7 12.5 %collective-permute-start.9 = (bf16[4,128,512]{2,1,0:T(8,128)(2,1)S(1)}, bf16[4,128,512]{2,1,0:T(8,128)(2,1)S(1)}, u32[]{:S(2)}, u32[]{:S(2)}) collective-permute-start(bf16[4,128,512]{2,1,0:T(8,128)(2,1)S(1)} %slice.285), channel_id=1, source_target_pairs={{0,4},{4,0},{8,12},{12,8},{16,20},{20,16},{24,28},{28,24},{1,5},{5... | collective-permute-start | bytes 1572872 | tf_op jit(solution)/shard_map/ppermute | solution.py:100
  102.3 32.9 %copy-start.35 = (pred[4096]{0:T(1024)(128)(4,1)}, pred[4096]{0:T(1024)(128)(4,1)S(1)}, u32[]{:S(2)}) copy-start(pred[4096]{0:T(1024)(128)(4,1)S(1)} %get-tuple-element.289) | copy-start | bytes 12292
  102.3 32.9 %copy-start.37 = (pred[4096]{0:T(1024)(128)(4,1)}, pred[4096]{0:T(1024)(128)(4,1)S(1)}, u32[]{:S(2)}) copy-start(pred[4096]{0:T(1024)(128)(4,1)S(1)} %get-tuple-element.290) | copy-start | bytes 12292
  102.3 32.9 %copy-start.27 = (s32[4096]{0:T(1024)}, s32[4096]{0:T(1024)S(1)}, u32[]{:S(2)}) copy-start(s32[4096]{0:T(1024)S(1)} %get-tuple-element.285) | copy-start | bytes 49156
  102.3 32.9 %copy-start.29 = (s32[4096]{0:T(1024)}, s32[4096]{0:T(1024)S(1)}, u32[]{:S(2)}) copy-start(s32[4096]{0:T(1024)S(1)} %get-tuple-element.286) | copy-start | bytes 49156
  102.4 32.9 %copy-start.31 = (s32[4096]{0:T(1024)}, s32[4096]{0:T(1024)S(1)}, u32[]{:S(2)}) copy-start(s32[4096]{0:T(1024)S(1)} %get-tuple-element.287) | copy-start | bytes 49156
  102.4 32.8 %copy-start.32 = (s32[4096]{0:T(1024)}, s32[4096]{0:T(1024)S(1)}, u32[]{:S(2)}) copy-start(s32[4096]{0:T(1024)S(1)} %get-tuple-element.288) | copy-start | bytes 49156
  114.3 36.6 %collective-permute-start.10 = (bf16[8,128,512]{2,1,0:T(8,128)(2,1)}, bf16[8,128,512]{2,1,0:T(8,128)(2,1)}, u32[]{:S(2)}, u32[]{:S(2)}) collective-permute-start(bf16[8,128,512]{2,1,0:T(8,128)(2,1)} %pad_maximum_fusion.5), channel_id=1, source_target_pairs={{0,2},{1,3},{2,0},{3,1},{4,6},{5,7},{6,4},{7,5},{8,10},{9,11},{10,... | collective-permute-start | bytes 3145736 | tf_op jit(solution)/shard_map/ppermute | solution.py:100
  121.8 42.7 %collective-permute-start.8 = (bf16[8,128,768]{2,1,0:T(8,128)(2,1)}, bf16[8,128,768]{2,1,0:T(8,128)(2,1)}, u32[]{:S(2)}, u32[]{:S(2)}) collective-permute-start(bf16[8,128,768]{2,1,0:T(8,128)(2,1)} %pad_maximum_fusion.3), channel_id=1, source_target_pairs={{0,4},{4,0},{8,12},{12,8},{16,20},{20,16},{24,28},{28,24},{1,5},{5... | collective-permute-start | bytes 4718600 | tf_op jit(solution)/shard_map/ppermute | solution.py:100
  166.2 33.8 %copy-start = (bf16[16,128,768]{2,1,0:T(8,128)(2,1)}, bf16[16,128,768]{2,1,0:T(8,128)(2,1)S(1)}, u32[]{:S(2)}) copy-start(bf16[16,128,768]{2,1,0:T(8,128)(2,1)S(1)} %pad_maximum_fusion.own_any) | copy-start | bytes 9437188
  197.7 59.9 %collective-permute-start.13 = (bf16[2,256,1024]{2,1,0:T(8,128)(2,1)}, bf16[2,256,1024]{2,1,0:T(8,128)(2,1)}, u32[]{:S(2)}, u32[]{:S(2)}) collective-permute-start(bf16[2,256,1024]{2,1,0:T(8,128)(2,1)} %get-tuple-element.262), channel_id=1, source_target_pairs={{0,3},{1,0},{2,1},{3,2},{4,7},{5,4},{6,5},{7,6},{8,11},{9,8},{10,9... | collective-permute-start | bytes 3145736 | tf_op jit(solution)/shard_map/ppermute | solution.py:786
  197.7 62.2 %collective-permute-start.14 = (bf16[2,256,1024]{2,1,0:T(8,128)(2,1)}, bf16[2,256,1024]{2,1,0:T(8,128)(2,1)}, u32[]{:S(2)}, u32[]{:S(2)}) collective-permute-start(bf16[2,256,1024]{2,1,0:T(8,128)(2,1)} %get-tuple-element.261), channel_id=1, source_target_pairs={{0,2},{1,3},{2,0},{3,1},{4,6},{5,7},{6,4},{7,5},{8,10},{9,11},{10,... | collective-permute-start | bytes 3145736 | tf_op jit(solution)/shard_map/ppermute | solution.py:786
  199.5 62.7 %collective-permute-start.15 = (bf16[2,256,1024]{2,1,0:T(8,128)(2,1)}, bf16[2,256,1024]{2,1,0:T(8,128)(2,1)}, u32[]{:S(2)}, u32[]{:S(2)}) collective-permute-start(bf16[2,256,1024]{2,1,0:T(8,128)(2,1)} %get-tuple-element.260), channel_id=1, source_target_pairs={{0,1},{1,2},{2,3},{3,0},{4,5},{5,6},{6,7},{7,4},{8,9},{9,10},{10,1... | collective-permute-start | bytes 3145736 | tf_op jit(solution)/shard_map/ppermute | solution.py:786
  199.9 64.6 %collective-permute-start.11 = (bf16[16,128,512]{2,1,0:T(8,128)(2,1)}, bf16[16,128,512]{2,1,0:T(8,128)(2,1)}, u32[]{:S(2)}, u32[]{:S(2)}) collective-permute-start(bf16[16,128,512]{2,1,0:T(8,128)(2,1)} %pad_maximum_fusion.2.own_any), channel_id=1, source_target_pairs={{0,1},{1,0},{2,3},{3,2},{4,5},{5,4},{6,7},{7,6},{8,9},{9,8},{10,11... | collective-permute-start | bytes 6291464 | tf_op jit(solution)/shard_map/ppermute | solution.py:100
  200.0 70.5 %collective-permute-start.12 = (bf16[16,128,768]{2,1,0:T(8,128)(2,1)S(1)}, bf16[16,128,768]{2,1,0:T(8,128)(2,1)}, u32[]{:S(2)}, u32[]{:S(2)}) collective-permute-start(bf16[16,128,768]{2,1,0:T(8,128)(2,1)S(1)} %pad_maximum_fusion.own_any), channel_id=1, source_target_pairs={{0,1},{1,0},{2,3},{3,2},{4,5},{5,4},{6,7},{7,6},{8,9},{9,8},{10,11... | collective-permute-start | bytes 9437192 | tf_op jit(solution)/shard_map/ppermute | solution.py:100
  448.9 24.7 %collective-permute-start.20 = (bf16[2,2,4,512,256]{4,3,2,1,0:T(8,128)(2,1)}, bf16[2,2,4,512,256]{4,3,2,1,0:T(8,128)(2,1)}, u32[]{:S(2)}, u32[]{:S(2)}) collective-permute-start(bf16[2,2,4,512,256]{4,3,2,1,0:T(8,128)(2,1)} %reduce_other.1), channel_id=1, source_target_pairs={{0,1},{1,0},{2,3},{3,2},{4,5},{5,4},{6,7},{7,6},{8,9},{9,8},{10,11... | collective-permute-start | bytes 12582920 | tf_op jit(solution)/shard_map/ppermute | solution.py:100
  466.8 58.7 %collective-permute-start.16 = (bf16[2,2,4,1,128,1024]{5,4,3,2,1,0:T(8,128)(2,1)}, bf16[2,2,4,1,128,1024]{5,4,3,2,1,0:T(8,128)(2,1)}, u32[]{:S(2)}, u32[]{:S(2)}) collective-permute-start(bf16[2,2,4,1,128,1024]{5,4,3,2,1,0:T(8,128)(2,1)} %expand_other.1), channel_id=1, source_target_pairs={{0,1},{1,0},{2,3},{3,2},{4,5},{5,4},{6,7},{7,6},{8,9},{9,8},{10,11... | collective-permute-start | bytes 12582920 | tf_op jit(solution)/shard_map/ppermute | solution.py:100
  471.9 25.3 %collective-permute-start.17 = (bf16[2,256,1024]{2,1,0:T(8,128)(2,1)}, bf16[2,256,1024]{2,1,0:T(8,128)(2,1)S(1)}, u32[]{:S(2)}, u32[]{:S(2)}) collective-permute-start(bf16[2,256,1024]{2,1,0:T(8,128)(2,1)} %get-tuple-element.258), channel_id=1, source_target_pairs={{1,0},{2,1},{3,2},{0,3},{5,4},{6,5},{7,6},{4,7},{9,8},{10,9},{11,1... | collective-permute-start | bytes 3145736 | tf_op jit(solution)/shard_map/ppermute | solution.py:808
  473.3 46.8 %collective-permute-start.18 = (bf16[2,256,1024]{2,1,0:T(8,128)(2,1)}, bf16[2,256,1024]{2,1,0:T(8,128)(2,1)S(1)}, u32[]{:S(2)}, u32[]{:S(2)}) collective-permute-start(bf16[2,256,1024]{2,1,0:T(8,128)(2,1)} %get-tuple-element.257), channel_id=1, source_target_pairs={{2,0},{3,1},{0,2},{1,3},{6,4},{7,5},{4,6},{5,7},{10,8},{11,9},{8,1... | collective-permute-start | bytes 3145736 | tf_op jit(solution)/shard_map/ppermute | solution.py:808
  473.6 46.5 %collective-permute-start.19 = (bf16[2,256,1024]{2,1,0:T(8,128)(2,1)}, bf16[2,256,1024]{2,1,0:T(8,128)(2,1)S(1)}, u32[]{:S(2)}, u32[]{:S(2)}) collective-permute-start(bf16[2,256,1024]{2,1,0:T(8,128)(2,1)} %get-tuple-element.259), channel_id=1, source_target_pairs={{3,0},{0,1},{1,2},{2,3},{7,4},{4,5},{5,6},{6,7},{11,8},{8,9},{9,10... | collective-permute-start | bytes 3145736 | tf_op jit(solution)/shard_map/ppermute | solution.py:808
  526.9 85.0 %collective-permute-start.21 = (bf16[1,2,4,512,256]{4,3,2,1,0:T(8,128)(2,1)}, bf16[1,2,4,512,256]{4,3,2,1,0:T(8,128)(2,1)S(1)}, u32[]{:S(2)}, u32[]{:S(2)}) collective-permute-start(bf16[1,2,4,512,256]{4,3,2,1,0:T(8,128)(2,1)} %slice.300), channel_id=1, source_target_pairs={{0,4},{4,0},{8,12},{12,8},{16,20},{20,16},{24,28},{28,24},{1,5},{5... | collective-permute-start | bytes 6291464 | tf_op jit(solution)/shard_map/ppermute | solution.py:100
  615.9 27.0 %copy-start.7 = (bf16[2,4,512,256]{3,2,1,0:T(8,128)(2,1)}, bf16[2,4,512,256]{3,2,1,0:T(8,128)(2,1)S(1)}, u32[]{:S(2)}) copy-start(bf16[2,4,512,256]{3,2,1,0:T(8,128)(2,1)S(1)} %fusion.32) | copy-start | bytes 6291460
  633.6 54.7 %collective-permute-start.22 = (bf16[2,2,4,3,128,256]{5,4,3,2,1,0:T(8,128)(2,1)}, bf16[2,2,4,3,128,256]{5,4,3,2,1,0:T(8,128)(2,1)}, u32[]{:S(2)}, u32[]{:S(2)}) collective-permute-start(bf16[2,2,4,3,128,256]{5,4,3,2,1,0:T(8,128)(2,1)} %square_other.1), channel_id=1, source_target_pairs={{0,1},{1,0},{2,3},{3,2},{4,5},{5,4},{6,7},{7,6},{8,9},{9,8},{10,11... | collective-permute-start | bytes 9437192 | tf_op jit(solution)/shard_map/ppermute | solution.py:100
  636.8 48.2 %collective-permute-start.23 = (bf16[1,2,4,1,128,1024]{5,4,3,2,1,0:T(8,128)(2,1)}, bf16[1,2,4,1,128,1024]{5,4,3,2,1,0:T(8,128)(2,1)}, u32[]{:S(2)}, u32[]{:S(2)}) collective-permute-start(bf16[1,2,4,1,128,1024]{5,4,3,2,1,0:T(8,128)(2,1)} %slice.302), channel_id=1, source_target_pairs={{0,4},{4,0},{8,12},{12,8},{16,20},{20,16},{24,28},{28,24},{1,5},{5... | collective-permute-start | bytes 6291464 | tf_op jit(solution)/shard_map/ppermute | solution.py:100
  642.8 42.2 %collective-permute-start.24 = (bf16[2,2,4,1,128,512]{5,4,3,2,1,0:T(8,128)(2,1)}, bf16[2,2,4,1,128,512]{5,4,3,2,1,0:T(8,128)(2,1)}, u32[]{:S(2)}, u32[]{:S(2)}) collective-permute-start(bf16[2,2,4,1,128,512]{5,4,3,2,1,0:T(8,128)(2,1)} %memory_other.1), channel_id=1, source_target_pairs={{0,1},{1,0},{2,3},{3,2},{4,5},{5,4},{6,7},{7,6},{8,9},{9,8},{10,11... | collective-permute-start | bytes 6291464 | tf_op jit(solution)/shard_map/ppermute | solution.py:100
  644.0 71.3 %collective-permute-start.26 = (bf16[1,4,512,256]{3,2,1,0:T(8,128)(2,1)}, bf16[1,4,512,256]{3,2,1,0:T(8,128)(2,1)}, u32[]{:S(2)}, u32[]{:S(2)}) collective-permute-start(bf16[1,4,512,256]{3,2,1,0:T(8,128)(2,1)} %slice.306), channel_id=1, source_target_pairs={{0,2},{1,3},{2,0},{3,1},{4,6},{5,7},{6,4},{7,5},{8,10},{9,11},{10,... | collective-permute-start | bytes 3145736 | tf_op jit(solution)/shard_map/ppermute | solution.py:100
  690.7 24.9 %collective-permute-start.25 = (bf16[1,4,1,128,1024]{4,3,1,0,2:T(8,128)(2,1)}, bf16[1,4,1,128,1024]{4,3,1,0,2:T(8,128)(2,1)}, u32[]{:S(2)}, u32[]{:S(2)}) collective-permute-start(bf16[1,4,1,128,1024]{4,3,1,0,2:T(8,128)(2,1)} %slice.305), channel_id=1, source_target_pairs={{0,2},{1,3},{2,0},{3,1},{4,6},{5,7},{6,4},{7,5},{8,10},{9,11},{10,... | collective-permute-start | bytes 3145736 | tf_op jit(solution)/shard_map/ppermute | solution.py:100
  721.1 86.4 %collective-permute-start.28 = (bf16[1,2,4,3,128,256]{5,4,3,2,1,0:T(8,128)(2,1)}, bf16[1,2,4,3,128,256]{5,4,3,2,1,0:T(8,128)(2,1)}, u32[]{:S(2)}, u32[]{:S(2)}) collective-permute-start(bf16[1,2,4,3,128,256]{5,4,3,2,1,0:T(8,128)(2,1)} %slice.313), channel_id=1, source_target_pairs={{0,4},{4,0},{8,12},{12,8},{16,20},{20,16},{24,28},{28,24},{1,5},{5... | collective-permute-start | bytes 4718600 | tf_op jit(solution)/shard_map/ppermute | solution.py:100
  722.7 82.0 %collective-permute-start.29 = (bf16[2,1024,256]{2,1,0:T(8,128)(2,1)}, bf16[2,1024,256]{2,1,0:T(8,128)(2,1)}, u32[]{:S(2)}, u32[]{:S(2)}) collective-permute-start(bf16[2,1024,256]{2,1,0:T(8,128)(2,1)} %slice.314), channel_id=1, source_target_pairs={{0,8},{4,12},{8,0},{12,4},{16,24},{20,28},{24,16},{28,20},{1,9},{5... | collective-permute-start | bytes 3145736 | tf_op jit(solution)/shard_map/ppermute | solution.py:100
  724.5 85.0 %collective-permute-start.27 = (bf16[1,2,4,1,128,512]{5,4,3,2,1,0:T(8,128)(2,1)}, bf16[1,2,4,1,128,512]{5,4,3,2,1,0:T(8,128)(2,1)}, u32[]{:S(2)}, u32[]{:S(2)}) collective-permute-start(bf16[1,2,4,1,128,512]{5,4,3,2,1,0:T(8,128)(2,1)} %slice.312), channel_id=1, source_target_pairs={{0,4},{4,0},{8,12},{12,8},{16,20},{20,16},{24,28},{28,24},{1,5},{5... | collective-permute-start | bytes 3145736 | tf_op jit(solution)/shard_map/ppermute | solution.py:100
  826.6 13.2 %collective-permute-start.32 = (bf16[2,2,4,1,128,768]{5,4,3,2,1,0:T(8,128)(2,1)}, bf16[2,2,4,1,128,768]{5,4,3,2,1,0:T(8,128)(2,1)}, u32[]{:S(2)}, u32[]{:S(2)}) collective-permute-start(bf16[2,2,4,1,128,768]{5,4,3,2,1,0:T(8,128)(2,1)} %input_other.1), channel_id=1, source_target_pairs={{0,1},{1,0},{2,3},{3,2},{4,5},{5,4},{6,7},{7,6},{8,9},{9,8},{10,11... | collective-permute-start | bytes 9437192 | tf_op jit(solution)/shard_map/ppermute | solution.py:100
  827.8 37.9 %collective-permute-start.30 = (bf16[1,4,640,256]{3,2,1,0:T(8,128)(2,1)}, bf16[1,4,640,256]{3,2,1,0:T(8,128)(2,1)}, u32[]{:S(2)}, u32[]{:S(2)}) collective-permute-start(bf16[1,4,640,256]{3,2,1,0:T(8,128)(2,1)} %slice.321), channel_id=1, source_target_pairs={{0,2},{1,3},{2,0},{3,1},{4,6},{5,7},{6,4},{7,5},{8,10},{9,11},{10,... | collective-permute-start | bytes 3932168 | tf_op jit(solution)/shard_map/ppermute | solution.py:100
  837.1 26.4 %collective-permute-start.31 = (bf16[1,1024,256]{2,1,0:T(8,128)(2,1)}, bf16[1,1024,256]{2,1,0:T(8,128)(2,1)S(1)}, u32[]{:S(2)}, u32[]{:S(2)}) collective-permute-start(bf16[1,1024,256]{2,1,0:T(8,128)(2,1)} %slice.322), channel_id=1, source_target_pairs={{0,16},{4,20},{8,24},{12,28},{16,0},{20,4},{24,8},{28,12},{1,17},{... | collective-permute-start | bytes 1572872 | tf_op jit(solution)/shard_map/ppermute | solution.py:100
  869.1 57.5 %collective-permute-start.33 = (bf16[1,2,4,1,128,768]{5,4,3,2,1,0:T(8,128)(2,1)}, bf16[1,2,4,1,128,768]{5,4,3,2,1,0:T(8,128)(2,1)}, u32[]{:S(2)}, u32[]{:S(2)}) collective-permute-start(bf16[1,2,4,1,128,768]{5,4,3,2,1,0:T(8,128)(2,1)} %slice.326), channel_id=1, source_target_pairs={{0,2},{1,3},{2,0},{3,1},{4,6},{5,7},{6,4},{7,5},{8,10},{9,11},{10,... | collective-permute-start | bytes 4718600 | tf_op jit(solution)/shard_map/ppermute | solution.py:100
  871.1 36.1 %collective-permute-start.34 = (bf16[2,640,256]{2,1,0:T(8,128)(2,1)}, bf16[2,640,256]{2,1,0:T(8,128)(2,1)}, u32[]{:S(2)}, u32[]{:S(2)}) collective-permute-start(bf16[2,640,256]{2,1,0:T(8,128)(2,1)} %slice.328), channel_id=1, source_target_pairs={{0,8},{4,12},{8,0},{12,4},{16,24},{20,28},{24,16},{28,20},{1,9},{5... | collective-permute-start | bytes 1966088 | tf_op jit(solution)/shard_map/ppermute | solution.py:100
  872.4 29.4 %copy-start.34 = (f32[2,3,1024]{2,1,0:T(4,128)S(1)}, f32[2,3,1024]{2,1,0:T(4,128)}, u32[]{:S(2)}) copy-start(f32[2,3,1024]{2,1,0:T(4,128)} %get-tuple-element.209) | copy-start | bytes 73732
  872.5 29.4 %copy-start.39 = (f32[2,1,1024]{2,1,0:T(1,128)S(1)}, f32[2,1,1024]{2,1,0:T(1,128)}, u32[]{:S(2)}) copy-start(f32[2,1,1024]{2,1,0:T(1,128)} %get-tuple-element.208) | copy-start | bytes 24580
  872.5 30.8 %slice-start = ((f32[128,1024]{1,0:T(8,128)}), f32[77,1024]{1,0:T(8,128)S(1)}, s32[]{:S(2)}) async-start(f32[128,1024]{1,0:T(8,128)} %null_text.1), calls=%async_computation.2 | async-start | bytes 655360 | tf_op jit(solution)/shard_map/slice | solution.py:1166
  908.7 17.1 %collective-permute-start.35 = (bf16[1,640,256]{2,1,0:T(8,128)(2,1)S(1)}, bf16[1,640,256]{2,1,0:T(8,128)(2,1)S(1)}, u32[]{:S(2)}, u32[]{:S(2)}) collective-permute-start(bf16[1,640,256]{2,1,0:T(8,128)(2,1)S(1)} %slice.380), channel_id=1, source_target_pairs={{0,16},{4,20},{8,24},{12,28},{16,0},{20,4},{24,8},{28,12},{1,17},{... | collective-permute-start | bytes 983048 | tf_op jit(solution)/shard_map/ppermute | solution.py:100
  952.3 7.7 collective-permute-start.42
  957.8 35.0 %collective-permute-start.39 = (bf16[1,4,1,128,768]{4,3,1,2,0:T(8,128)(2,1)}, bf16[1,4,1,128,768]{4,3,1,2,0:T(8,128)(2,1)}, u32[]{:S(2)}, u32[]{:S(2)}) collective-permute-start(bf16[1,4,1,128,768]{4,3,1,2,0:T(8,128)(2,1)} %slice_bitcast_fusion.6), channel_id=1, source_target_pairs={{0,4},{4,0},{8,12},{12,8},{16,20},{20,16},{24,28},{28,24},{1,5},{5... | collective-permute-start | bytes 2359304 | tf_op jit(solution)/shard_map/ppermute | solution.py:100
  960.3 6.8 collective-permute-start.43
  965.0 27.8 %copy-start.14 = (bf16[1,2,4,1,128,768]{5,4,3,2,1,0:T(8,128)(2,1)S(1)}, bf16[1,2,4,1,128,768]{5,4,3,2,1,0:T(8,128)(2,1)}, u32[]{:S(2)}) copy-start(bf16[1,2,4,1,128,768]{5,4,3,2,1,0:T(8,128)(2,1)} %copy-done.13) | copy-start | bytes 4718596
  965.0 29.2 %collective-permute-start.36 = (bf16[2,256,1024]{2,1,0:T(8,128)(2,1)}, bf16[2,256,1024]{2,1,0:T(8,128)(2,1)S(1)}, u32[]{:S(2)}, u32[]{:S(2)}) collective-permute-start(bf16[2,256,1024]{2,1,0:T(8,128)(2,1)} %get-tuple-element.254), channel_id=1, source_target_pairs={{1,0},{2,1},{3,2},{0,3},{5,4},{6,5},{7,6},{4,7},{9,8},{10,9},{11,1... | collective-permute-start | bytes 3145736 | tf_op jit(solution)/shard_map/ppermute | solution.py:808
  966.8 46.6 %collective-permute-start.37 = (bf16[2,256,1024]{2,1,0:T(8,128)(2,1)}, bf16[2,256,1024]{2,1,0:T(8,128)(2,1)}, u32[]{:S(2)}, u32[]{:S(2)}) collective-permute-start(bf16[2,256,1024]{2,1,0:T(8,128)(2,1)} %get-tuple-element.253), channel_id=1, source_target_pairs={{2,0},{3,1},{0,2},{1,3},{6,4},{7,5},{4,6},{5,7},{10,8},{11,9},{8,1... | collective-permute-start | bytes 3145736 | tf_op jit(solution)/shard_map/ppermute | solution.py:808
  967.1 46.3 %collective-permute-start.38 = (bf16[2,256,1024]{2,1,0:T(8,128)(2,1)}, bf16[2,256,1024]{2,1,0:T(8,128)(2,1)}, u32[]{:S(2)}, u32[]{:S(2)}) collective-permute-start(bf16[2,256,1024]{2,1,0:T(8,128)(2,1)} %get-tuple-element.252), channel_id=1, source_target_pairs={{3,0},{0,1},{1,2},{2,3},{7,4},{4,5},{5,6},{6,7},{11,8},{8,9},{9,10... | collective-permute-start | bytes 3145736 | tf_op jit(solution)/shard_map/ppermute | solution.py:808
  967.6 11.9 %collective-permute-start.44 = (f32[28068]{0:T(1024)S(1)}, f32[28068]{0:T(1024)S(1)}, u32[]{:S(2)}, u32[]{:S(2)}) collective-permute-start(f32[28068]{0:T(1024)S(1)} %slice_reduce_fusion), channel_id=1, source_target_pairs={{0,4},{4,0},{8,12},{12,8},{16,20},{20,16},{24,28},{28,24},{1,5},{5... | collective-permute-start | bytes 336824 | tf_op jit(solution)/shard_map/ppermute | solution.py:856
  979.5 4.9 collective-permute-start.45
  984.4 6.4 collective-permute-start.46
  994.1 24.8 %collective-permute-start.40 = (bf16[2,1,128,768]{3,2,0,1:T(8,128)(2,1)S(1)}, bf16[2,1,128,768]{3,2,0,1:T(8,128)(2,1)S(1)}, u32[]{:S(2)}, u32[]{:S(2)}) collective-permute-start(bf16[2,1,128,768]{3,2,0,1:T(8,128)(2,1)S(1)} %slice_bitcast_fusion.8), channel_id=1, source_target_pairs={{0,8},{4,12},{8,0},{12,4},{16,24},{20,28},{24,16},{28,20},{1,9},{5... | collective-permute-start | bytes 1179656 | tf_op jit(solution)/shard_map/ppermute | solution.py:100
  1019.1 9.6 collective-permute-start.41
  (28 other events, 168.5 us)
Sparse Core Ops, SparseCore 0:
  10.9 97.5 all-gather.4
  111.9 123.8 all-gather.6

commit v2 on v1

v2 whole, which is shorter than its diff:
```python
import functools
import math

import jax
import jax.numpy as jnp
from jax import lax
from jax.experimental import pallas as pl
from jax.experimental.pallas import tpu as pltpu
from jax.sharding import PartitionSpec as P

HEADS = 16
HD = 64
FRAMES = 5
GRID = 32
WS = 8
SEQ = 5120
WIN_TOK = 320
NREL = 2025
TXT = 77
QUAD = 4
QW = QUAD * HD
QUADS = HEADS // QUAD
SPAN = 2 * WS - 1
FSPAN = 2 * FRAMES - 1
SIDE = WS * WS
PAIR = 2 * HD
LANES = QUAD * WIN_TOK
TEXT_ROWS = 80
CHUNK = 256

epsilon = 1e-06
gelu_coefficient = 0.7978845608028654
scale_factor = HD ** (-0.5)
bfloat = jnp.bfloat16
single = jnp.float32
NEGATIVE = -1e30
VMEM_LIMIT = 60 * 1024 * 1024

NN = (((1,), (0,)), ((), ()))
NT = (((1,), (1,)), ((), ()))
TN = (((0,), (0,)), ((), ()))


def mm(left, right, dims=NN):
    return lax.dot_general(left, right, dims, preferred_element_type=single)


def norm_parts(values):
    centered = values - jnp.mean(values, axis=-1, keepdims=True)
    variance = jnp.mean(centered * centered, axis=-1, keepdims=True)
    inverse = lax.rsqrt(variance + epsilon)
    return centered * inverse, inverse


def norm_back(normed, inverse, grad):
    return inverse * (
        grad
        - jnp.mean(grad, axis=-1, keepdims=True)
        - normed * jnp.mean(grad * normed, axis=-1, keepdims=True)
    )


def params():
    return pltpu.CompilerParams(vmem_limit_bytes=VMEM_LIMIT)


def cost(microseconds):
    return pl.CostEstimate(
        flops=int(microseconds * 760e9),
        bytes_accessed=int(microseconds * 1e9),
        transcendentals=0,
    )


def tie(*values):
    return lax.optimization_barrier(values)


ANY = pl.BlockSpec(memory_space=pl.ANY)
PLACE = pl.BlockSpec(memory_space=pltpu.SMEM)
FIRST_ORDER = ("z", "x", "y")
OTHER_ORDER = ("z", "y", "x")


class Term:
    def __init__(self, kept, sent, lead):
        self.kept, self.sent, self.lead = kept, sent, lead


jax.tree_util.register_pytree_node(
    Term, lambda t: ((t.kept, t.sent), t.lead), lambda lead, parts: Term(*parts, lead)
)


class Layout:
    def __init__(self, clip_size, win_count):
        self.clip_size, self.win_count = clip_size, win_count
        y = 2 ** ((clip_size.bit_length() - 1) // 2)
        self.size = {"z": clip_size // y, "y": y, "x": win_count // 2, "core": 2}
        self.home = {"z": "clip", "y": "clip", "x": "win", "core": "win"}
        self.stride = {"z": y, "y": 1, "x": 2, "core": 1}
        self.others = clip_size * win_count // 2

    def place(self):
        clip, win = lax.axis_index("clip"), lax.axis_index("win")
        y = self.size["y"]
        return jnp.stack([clip // y, clip % y, win // 2, win % 2]).astype(jnp.int32)

    def swap(self, values, axis, apart):
        home = self.home[axis]
        count = self.clip_size if home == "clip" else self.win_count
        step = apart * self.stride[axis]
        return lax.ppermute(values, home, [(i, i ^ step) for i in range(count)])

    def gather(self, held, axis, apart, pin):
        part, pin = tie(self.swap(held, axis, apart), pin)
        return held, part, pin

    def gather_axis(self, held, axis, pin):
        apart = 1
        while apart < self.size[axis]:
            held, part, pin = self.gather(held, axis, apart, pin)
            held = jnp.concatenate([held, part], axis=0)
            apart *= 2
        return held, pin

    def gather_last(self, held, axis, pin):
        apart = 1
        while apart < self.size[axis] // 2:
            held, part, pin = self.gather(held, axis, apart, pin)
            held = jnp.concatenate([held, part], axis=0)
            apart *= 2
        return self.gather(held, axis, apart, pin)

    def with_other_core(self, *arrays):
        return list(arrays) + [self.swap(array, "core", 1) for array in arrays]

    def owner(self, place_ref, order, index, core_apart):
        names = ("z", "y", "x", "core")
        at = {name: place_ref[i] for i, name in enumerate(names)}
        for axis in order:
            at[axis] = at[axis] ^ (index % self.size[axis])
            index = index // self.size[axis]
        core = at["core"] ^ core_apart
        return at["z"] * self.size["y"] + at["y"], at["x"] * 2 + core

    def reduce(self, terms, axes, apart, pin):
        came = [self.swap(term.sent, axis, n) for term, axis, n in zip(terms, axes, apart)]
        came, pin = tie(came, pin)
        pairs = []
        for term, part in zip(terms, came):
            kept, lead = term.kept, term.lead
            while lead > 0 and kept.shape[0] == 1:
                kept, part, lead = kept[0], part[0], lead - 1
            pairs.append((kept, part))
        if lead == 0:
            sums = [kept.astype(single) + part.astype(single) for kept, part in pairs]
            return jnp.concatenate(sums, axis=0), pin
        return Term(*add_halves(pairs), lead), pin

    def reduce_axes(self, terms, axes, pin):
        terms = list(terms)
        for i, axis in enumerate(axes):
            for bit in range(self.bits(axis) - 1):
                terms[i], pin = self.reduce([terms[i]], [axis], [1 << bit], pin)
        return self.reduce(terms, axes, [self.size[axis] // 2 for axis in axes], pin)

    def bits(self, axis):
        return self.size[axis].bit_length() - 1


def add_kernel(*refs):
    ins, outs, at = refs[:-2], refs[-2:], 0
    for i in range(0, len(ins), 2):
        count = ins[i].shape[2]
        for half, out_ref in enumerate(outs):
            total = ins[i][half, 0].astype(single) + ins[i + 1][half, 0].astype(single)
            out_ref[0, at : at + count] = total.astype(bfloat)
        at += count


def add_halves(pairs):
    shape = pairs[0][0].shape
    lead = (shape[0] // 2,) + shape[1:-3]
    steps, total = math.prod(lead), sum(kept.shape[-3] for kept, _ in pairs)
    ins, in_specs = [], []
    for pair in pairs:
        tail = pair[0].shape[-3:]
        ins += [array.reshape((2, steps) + tail) for array in pair]
        in_specs += [pl.BlockSpec((2, 1) + tail, lambda i: (0, i, 0, 0, 0))] * 2
    tail = (total,) + shape[-2:]
    outs = pl.pallas_call(
        add_kernel,
        grid=(steps,),
        in_specs=in_specs,
        out_specs=[pl.BlockSpec((1,) + tail, lambda i: (i, 0, 0, 0))] * 2,
        out_shape=[jax.ShapeDtypeStruct((steps,) + tail, bfloat)] * 2,
        compiler_params=params(),
        cost_estimate=cost(0),
        name="add_halves",
    )(*ins)
    return [out.reshape(lead + tail) for out in outs]


def reverse(index, size):
    distance, bits = 0, size.bit_length() - 1
    for b in range(bits):
        distance = distance + (((index >> b) & 1) << (bits - 1 - b))
    return distance


def start_weight(sources, target, sem, layout, place_ref, order, cols, offset=0):
    half = len(sources) // 2
    for k, source in enumerate(sources):
        count, rows = source.shape[:2]

        def step(i, carry, source=source, k=k, count=count, rows=rows):
            clip, win = layout.owner(place_ref, order, i + k % half * count, k // half)
            row = pl.multiple_of(clip * rows, rows)
            column = pl.multiple_of(win * cols, cols)
            pltpu.make_async_copy(
                source.at[i, :, pl.ds(offset, cols)],
                target.at[pl.ds(row, rows), pl.ds(column, cols)],
                sem,
            ).start()
            return carry

        lax.fori_loop(0, count, step, 0)


def start_squares(sources, targets, sems, layout, place_ref):
    cols = sources[0].shape[2] // len(targets)
    for i, target in enumerate(targets):
        start_weight(sources, target, sems.at[i], layout, place_ref, FIRST_ORDER, cols, i * cols)


def start_gathered(source, target, sem, layout, cols, offset=0):
    depth = source.shape[1]
    rows = target.shape[0] // layout.clip_size

    def step(c, carry):
        for w in range(layout.win_count):
            for piece in range(rows // depth):
                row = pl.multiple_of(c * rows + piece * depth, depth)
                pltpu.make_async_copy(
                    source.at[c * layout.win_count + w, :, pl.ds(offset + piece * cols, cols)],
                    target.at[pl.ds(row, depth), pl.ds(w * cols, cols)],
                    sem,
                ).start()
        return carry

    lax.fori_loop(0, layout.clip_size, step, 0)


def wait_weight(target, sem):
    pltpu.make_async_copy(target, target, sem).wait()


def piece_spec(wins, width, frame):
    return pl.BlockSpec(
        (1, 1, WS, 1, WS, width), lambda i: (i // wins, frame, 0, i % wins, 0, 0)
    )


def whole_spec(wins, width):
    return pl.BlockSpec(
        (1, FRAMES, WS, 1, WS, width), lambda i: (i // wins, 0, 0, i % wins, 0, 0)
    )


def rows_spec(width):
    return pl.BlockSpec((1, WIN_TOK, width), lambda i: (i, 0, 0))


def modulation_spec(wins, width):
    return pl.BlockSpec((1, 6, width), lambda i: (i // wins, 0, 0))


def load_window(refs):
    parts = [ref[0, 0, :, 0].astype(single).reshape(SIDE, ref.shape[-1]) for ref in refs]
    return jnp.concatenate(parts, axis=0)


def store_window(refs, values):
    whole, others = refs[0], refs[1:]
    shape = (FRAMES, WS, WS, whole.shape[-1])
    values = values.reshape(shape).astype(whole.dtype)
    if not others:
        whole[0, :, :, 0] = values
        return
    whole[0, 0, :, 0] = values[0]
    whole[0, FRAMES - 1, :, 0] = values[1]
    for i, other in enumerate(others):
        other[0, 0, :, 0] = values[2 + i]


def store_units(ref, index, first, values):
    unit = ref.shape[-1]
    for at in range(0, values.shape[1], unit):
        ref[index, (first + at) // unit, 0] = values[:, at : at + unit]


def frame_offset(shift, query, key):
    return lax.rem(shift + query, FRAMES) - lax.rem(shift + key, FRAMES) + FRAMES - 1


def frame_blocks():
    for key in range(FRAMES):
        for query in range(FRAMES):
            for pair in range(QUAD // 2):
                lane = query * QW + pair * PAIR
                yield key, query, pair, slice(key * SIDE, (key + 1) * SIDE), slice(lane, lane + PAIR)


def table_kernel(shift_ref, block_ref, out_ref):
    for key, query, pair, rows, lanes in frame_blocks():
        offset = frame_offset(shift_ref[0], query, key)
        out_ref[0, rows, lanes] = block_ref[pair, offset]


def collect_kernel(shift_ref, sum_ref, out_ref, pairs_ref):
    pairs_ref[...] = jnp.zeros(pairs_ref.shape, single)
    for key, query, pair, rows, lanes in frame_blocks():
        offset = frame_offset(shift_ref[0], query, key)
        pairs_ref[pair, offset] += sum_ref[0, rows, lanes]
    for head in range(QUAD):
        lanes = slice(head % 2 * HD, (head % 2 + 1) * HD)
        out_ref[head] = pairs_ref[head // 2, :, :, lanes]


QUAD_SPEC = pl.BlockSpec((1, WIN_TOK, LANES), lambda q, s: (q, 0, 0))
BLOCKS_SPEC = pl.BlockSpec((QUAD // 2, FSPAN, SIDE, PAIR), lambda q, s: (q, 0, 0, 0))


def side_hot():
    shape = (SPAN * SPAN, SIDE * SIDE)
    offset = lax.broadcasted_iota(jnp.int32, shape, 0)
    pair = lax.broadcasted_iota(jnp.int32, shape, 1)
    key, query = pair // SIDE, pair % SIDE
    rows = query // WS - key // WS + WS - 1
    columns = query % WS - key % WS + WS - 1
    return (rows * SPAN + columns == offset).astype(single)


def table_blocks(bias_full):
    flat = bias_full.reshape(HEADS * FSPAN, SPAN * SPAN)
    blocks = jnp.dot(flat, side_hot(), precision=lax.Precision.HIGHEST)
    blocks = blocks.reshape(HEADS // 2, 2, FSPAN, SIDE, SIDE).transpose(0, 2, 3, 1, 4)
    return blocks.reshape(HEADS // 2, FSPAN, SIDE, PAIR)


def bias_table(blocks, shift):
    return pl.pallas_call(
        table_kernel,
        grid_spec=pltpu.PrefetchScalarGridSpec(
            num_scalar_prefetch=1,
            grid=(QUADS,),
            in_specs=[BLOCKS_SPEC],
            out_specs=QUAD_SPEC,
        ),
        out_shape=jax.ShapeDtypeStruct((QUADS, WIN_TOK, LANES), single),
        compiler_params=params(),
        cost_estimate=cost(5),
        name="bias_table",
    )(shift, blocks)


def bias_blocks(bias_sum, shift):
    return pl.pallas_call(
        collect_kernel,
        grid_spec=pltpu.PrefetchScalarGridSpec(
            num_scalar_prefetch=1,
            grid=(QUADS,),
            in_specs=[QUAD_SPEC],
            out_specs=pl.BlockSpec((QUAD, FSPAN, SIDE, SIDE), lambda q, s: (q, 0, 0, 0)),
            scratch_shapes=[pltpu.VMEM((QUAD // 2, FSPAN, SIDE, PAIR), single)],
        ),
        out_shape=jax.ShapeDtypeStruct((HEADS, FSPAN, SIDE, SIDE), single),
        compiler_params=params(),
        cost_estimate=cost(5),
        name="bias_collect",
    )(shift, bias_sum).reshape(HEADS * FSPAN, SIDE * SIDE)


def bias_collect(flat):
    summed = lax.dot_general(flat, side_hot(), NT, precision=lax.Precision.HIGHEST)
    return summed.reshape(HEADS, NREL)


def project_kernel(layout, *refs):
    token_refs, refs = refs[:FRAMES], refs[FRAMES:]
    mod_ref, weight_any, low_ref, out_ref, weight_ref, sem = refs

    @pl.when(pl.program_id(0) == 0)
    def _():
        start_gathered(weight_any, weight_ref, sem, layout, weight_any.shape[2])
        wait_weight(weight_ref, sem)

    normed, _ = norm_parts(load_window(token_refs))
    low = (normed * (1.0 + mod_ref[0, 1:2]) + mod_ref[0, 0:1]).astype(bfloat)
    low_ref[0] = low
    out_ref[0] = mm(low, weight_ref[...]).astype(bfloat)


def head_mask(rows, head):
    lane = lax.broadcasted_iota(jnp.int32, (rows, QW), 1)
    return (lane >= head * HD) & (lane < (head + 1) * HD)


def spread(values):
    masks = [head_mask(SIDE, h) for h in range(QUAD)]
    parts = []
    for frame in range(FRAMES):
        rows = values[frame * SIDE : (frame + 1) * SIDE]
        parts += [jnp.where(mask, rows, jnp.zeros_like(rows)) for mask in masks]
    return jnp.concatenate(parts, axis=0)


def own_heads(product):
    lane = lax.broadcasted_iota(jnp.int32, (SIDE, PAIR), 1)
    rows = []
    for frame in range(FRAMES):
        parts = []
        for pair in range(QUAD // 2):
            at = frame * QW + pair * PAIR
            block = product[pair * PAIR : (pair + 1) * PAIR, at : at + PAIR].T
            parts.append(jnp.where(lane < HD, block[:SIDE], block[SIDE:]))
        rows.append(jnp.concatenate(parts, axis=1))
    return jnp.concatenate(rows, axis=0)


def softmax_down(scores):
    expanded = jnp.exp(scores - jnp.max(scores, axis=0, keepdims=True))
    return expanded * (1.0 / jnp.sum(expanded, axis=0, keepdims=True))


def lane_chunks():
    return [slice(c, c + CHUNK) for c in range(0, LANES, CHUNK)]


def attend_kernel(projected_ref, bias_ref, out_ref, probs_ref, scores_ref):
    width = out_ref.shape[-1]
    for q in range(QUADS):
        at, slot = slice(q * QW, (q + 1) * QW), q % 2
        queries = spread(projected_ref[0, :, at] * jnp.asarray(scale_factor, bfloat))
        keys = projected_ref[0, :, width + q * QW : width + (q + 1) * QW]
        values = projected_ref[0, :, 2 * width + q * QW : 2 * width + (q + 1) * QW]
        scores_ref[slot] = mm(keys, queries, NT)
        for lanes in lane_chunks():
            scores = scores_ref[slot, :, lanes] + bias_ref[q, :, lanes]
            probs_ref[0, q, :, lanes] = softmax_down(scores).astype(bfloat)
        out_ref[0, :, at] = own_heads(mm(values, probs_ref[0, q], TN)).astype(bfloat)


def attend_back_kernel(
    projected_ref, grad_ref, probs_ref, out_ref, sum_ref, grad_probs_ref, grad_scores_ref
):
    @pl.when(pl.program_id(0) == 0)
    def _():
        sum_ref[...] = jnp.zeros(sum_ref.shape, single)

    width = grad_ref.shape[-1]
    for q in range(QUADS):
        at, slot = slice(q * QW, (q + 1) * QW), q % 2
        queries = spread(projected_ref[0, :, at] * jnp.asarray(scale_factor, bfloat))
        keys = projected_ref[0, :, width + q * QW : width + (q + 1) * QW]
        values = projected_ref[0, :, 2 * width + q * QW : 2 * width + (q + 1) * QW]
        grads = spread(grad_ref[0, :, at])
        grad_probs_ref[slot] = mm(values, grads, NT)
        store_units(out_ref, 2, q * QW, mm(probs_ref[0, q], grads).astype(bfloat))
        for lanes in lane_chunks():
            probs = probs_ref[0, q, :, lanes].astype(single)
            weighted = probs * grad_probs_ref[slot, :, lanes]
            grad_scores = weighted - probs * jnp.sum(weighted, axis=0, keepdims=True)
            grad_scores_ref[slot, :, lanes] = grad_scores.astype(bfloat)
            sum_ref[q, :, lanes] += grad_scores
        store_units(out_ref, 1, q * QW, mm(grad_scores_ref[slot], queries).astype(bfloat))
        grad_queries = own_heads(mm(keys, grad_scores_ref[slot], TN))
        store_units(out_ref, 0, q * QW, (grad_queries * scale_factor).astype(bfloat))


BIAS_SPEC = pl.BlockSpec((QUADS, WIN_TOK, LANES), lambda i: (0, 0, 0))
PROBS_SPEC = pl.BlockSpec((1, QUADS, WIN_TOK, LANES), lambda i: (i, 0, 0, 0))


def memory_kernel(layout, place_ref, text_ref, *refs):
    sources, (memory_ref, weight_ref, sem) = refs[:4], refs[4:]

    @pl.when(pl.program_id(0) == 0)
    def _():
        cols = sources[0].shape[2]
        start_weight(sources, weight_ref, sem, layout, place_ref, OTHER_ORDER, cols)
        wait_weight(weight_ref, sem)

    memory_ref[0] = mm(text_ref[0], weight_ref[...]).astype(bfloat)


def cross_probs(queries, keys):
    scores = mm(keys, queries, NT)
    whole = TXT // 8 * 8
    row = lax.broadcasted_iota(jnp.int32, (TEXT_ROWS - whole, LANES), 0) + whole
    rest = jnp.where(row < TXT, scores[whole:], NEGATIVE)
    return softmax_down(jnp.concatenate([scores[:whole], rest], axis=0))


def cross_kernel(layout, place_ref, *refs):
    token_refs, refs = refs[:FRAMES], refs[FRAMES:]
    attended_ref, mod_ref, gain_ref, memory_ref = refs[:4]
    sources, refs = refs[4:8], refs[8:]
    branch_ref, left_ref, queries_ref, sum_ref, output_ref, query_ref, cross_ref, sems = refs

    @pl.when(pl.program_id(0) == 0)
    def _():
        start_squares(sources, (output_ref, query_ref, cross_ref), sems, layout, place_ref)
        wait_weight(output_ref, sems.at[0])
        wait_weight(query_ref, sems.at[1])
        wait_weight(cross_ref, sems.at[2])

    attended = attended_ref[0]
    left_ref[0, 0] = attended
    branch = mm(attended, output_ref[...])
    branch_ref[0] = branch
    first_sum = load_window(token_refs) + mod_ref[0, 2:3] * branch
    normed, _ = norm_parts(first_sum)
    second = (normed * gain_ref[...]).astype(bfloat)
    left_ref[1, 0] = second
    queries = mm(second, query_ref[...]).astype(bfloat)
    queries_ref[0] = queries
    width = queries.shape[1]
    parts = []
    for q in range(QUADS):
        at = slice(q * QW, (q + 1) * QW)
        scaled = spread(queries[:, at] * jnp.asarray(scale_factor, bfloat))
        probs = cross_probs(scaled, memory_ref[0, :, at]).astype(bfloat)
        values = memory_ref[0, :, width + q * QW : width + (q + 1) * QW]
        parts.append(own_heads(mm(values, probs, TN)).astype(bfloat))
    crossed = jnp.concatenate(parts, axis=1)
    left_ref[2, 0] = crossed
    sum_ref[0] = first_sum + mm(crossed, cross_ref[...])


def cross_back_kernel(layout, wins, place_ref, *refs):
    token_refs, refs = refs[:FRAMES], refs[FRAMES:]
    mod_ref, gain_ref, memory_ref, grad_ref, queries_ref, branch_ref = refs[:6]
    sources, refs = refs[6:10], refs[10:]
    right_ref, grad_sum_ref, grad_attended_ref = refs[:3]
    grad_memory_ref, gain_grad_ref, gate_grad_ref = refs[3:6]
    output_ref, query_ref, cross_ref, sems = refs[6:]
    step = pl.program_id(0)

    @pl.when(step == 0)
    def _():
        start_squares(sources, (output_ref, query_ref, cross_ref), sems, layout, place_ref)
        wait_weight(output_ref, sems.at[0])
        wait_weight(query_ref, sems.at[1])
        wait_weight(cross_ref, sems.at[2])
        gain_grad_ref[...] = jnp.zeros(gain_grad_ref.shape, single)

    @pl.when(step % wins == 0)
    def _():
        grad_memory_ref[...] = jnp.zeros(grad_memory_ref.shape, single)
        gate_grad_ref[...] = jnp.zeros(gate_grad_ref.shape, single)

    width = queries_ref.shape[-1]
    grad = grad_ref[0]
    grad_low = grad.astype(bfloat)
    store_units(right_ref, 2, 0, grad_low)
    grad_crossed = mm(grad_low, cross_ref[...], NT).astype(bfloat)
    queries = queries_ref[0]
    query_parts = []
    for q in range(QUADS):
        at = slice(q * QW, (q + 1) * QW)
        value_at = slice(width + q * QW, width + (q + 1) * QW)
        scaled = spread(queries[:, at] * jnp.asarray(scale_factor, bfloat))
        grads = spread(grad_crossed[:, at])
        keys = memory_ref[0, :, at]
        probs = cross_probs(scaled, keys)
        weighted = probs * mm(memory_ref[0, :, value_at], grads, NT)
        grad_scores = weighted - probs * jnp.sum(weighted, axis=0, keepdims=True)
        grad_scores = grad_scores.astype(bfloat)
        grad_memory_ref[0, :, at] += mm(grad_scores, scaled)
        grad_memory_ref[0, :, value_at] += mm(probs.astype(bfloat), grads)
        part = own_heads(mm(keys, grad_scores, TN))
        query_parts.append((part * scale_factor).astype(bfloat))
    grad_queries = jnp.concatenate(query_parts, axis=1)
    store_units(right_ref, 1, 0, grad_queries)
    grad_second = mm(grad_queries, query_ref[...], NT)
    branch = branch_ref[0]
    normed, inverse = norm_parts(load_window(token_refs) + mod_ref[0, 2:3] * branch)
    gain_grad_ref[...] += jnp.sum(grad_second * normed, axis=0, keepdims=True)
    grad_sum = grad + norm_back(normed, inverse, grad_second * gain_ref[...])
    grad_sum_ref[0] = grad_sum
    gate_grad_ref[0] += jnp.sum(grad_sum * branch, axis=0, keepdims=True)
    grad_branch = (mod_ref[0, 2:3] * grad_sum).astype(bfloat)
    store_units(right_ref, 0, 0, grad_branch)
    grad_attended_ref[0] = mm(grad_branch, output_ref[...], NT).astype(bfloat)


def null_kernel(layout, place_ref, masked_ref, *refs):
    sources, (out_ref, weight_ref, sem) = refs[:4], refs[4:]
    cols = sources[0].shape[2]
    start_weight(sources, weight_ref, sem, layout, place_ref, OTHER_ORDER, cols)
    wait_weight(weight_ref, sem)
    masked = masked_ref[...]
    high = masked.astype(bfloat)
    rest = (masked - high.astype(single)).astype(bfloat)
    weight = weight_ref[...]
    out_ref[...] = mm(high, weight, NT) + mm(rest, weight, NT)


def null_text_term(layout, place, masked, sources):
    width = masked.shape[1] // 2
    whole = pl.BlockSpec(memory_space=pltpu.VMEM)
    return pl.pallas_call(
        functools.partial(null_kernel, layout),
        in_specs=[PLACE, whole, ANY, ANY, ANY, ANY],
        out_specs=whole,
        out_shape=jax.ShapeDtypeStruct((masked.shape[0], width), single),
        scratch_shapes=[pltpu.VMEM((width, 2 * width), bfloat), pltpu.SemaphoreType.DMA(())],
        compiler_params=params(),
        cost_estimate=cost(5),
        name="null_text",
    )(place, masked, *sources)


def feed_kernel(layout, wins, chunk, sent, *refs):
    grad_out_refs, refs = refs[:FRAMES], refs[FRAMES:]
    sum_ref, mod_ref, weights_any = refs[:3]
    out_refs, refs = refs[3 : 4 + sent], refs[4 + sent :]
    third_ref, act_ref, grad_hidden_ref, grad_reduced_ref, grad_sum_ref, grad_mod_ref = refs[:6]
    expand_ref, reduce_ref, sems = refs[6:]
    step = pl.program_id(0)

    @pl.when(step == 0)
    def _():
        cols = expand_ref.shape[1] // layout.win_count
        start_gathered(weights_any, expand_ref, sems.at[0], layout, cols)
        offset = cols
        cols = reduce_ref.shape[1] // layout.win_count
        start_gathered(weights_any, reduce_ref, sems.at[1], layout, cols, offset)
        wait_weight(expand_ref, sems.at[0])
        wait_weight(reduce_ref, sems.at[1])

    @pl.when(step % wins == 0)
    def _():
        grad_mod_ref[...] = jnp.zeros(grad_mod_ref.shape, single)

    second_sum = sum_ref[0]
    normed, inverse = norm_parts(second_sum)
    third = (normed * (1.0 + mod_ref[0, 4:5]) + mod_ref[0, 3:4]).astype(bfloat)
    third_ref[0] = third
    grad_out = load_window(grad_out_refs)
    gate = mod_ref[0, 5:6]
    grad_reduced = (gate * grad_out).astype(bfloat)
    grad_reduced_ref[0] = grad_reduced
    hidden_width = expand_ref.shape[1]
    for at in range(0, hidden_width, chunk):
        part = slice(at, at + chunk)
        v = mm(third, expand_ref[:, part])
        grad_act = mm(grad_reduced, reduce_ref[part], NT)
        square = v * v
        tanh = jnp.tanh(gelu_coefficient * (v + 0.044715 * (square * v)))
        half = 0.5 * (1.0 + tanh)
        act_ref[0, :, part] = (v * half).astype(bfloat)
        slope = half + (0.5 * gelu_coefficient) * v * (1.0 - tanh * tanh) * (
            1.0 + (3 * 0.044715) * square
        )
        grad_hidden_ref[0, :, part] = (grad_act * slope).astype(bfloat)
    reduced = mm(act_ref[0], reduce_ref[...])
    store_window(out_refs, second_sum + gate * reduced)
    grad_third = mm(grad_hidden_ref[0], expand_ref[...], NT)
    grad_mod_ref[0, 0:1] += jnp.sum(grad_third, axis=0, keepdims=True)
    grad_mod_ref[0, 1:2] += jnp.sum(grad_third * normed, axis=0, keepdims=True)
    grad_mod_ref[0, 2:3] += jnp.sum(grad_out * reduced, axis=0, keepdims=True)
    grad_sum_ref[0] = grad_out + norm_back(normed, inverse, grad_third * (1.0 + mod_ref[0, 4:5]))


def input_back_kernel(layout, wins, sent, *refs):
    token_refs, refs = refs[:FRAMES], refs[FRAMES:]
    mod_ref, grad_ref, grad_sum_ref, weight_any = refs[:4]
    out_refs, (grad_mod_ref, weight_ref, sem) = refs[4 : 5 + sent], refs[5 + sent :]
    step = pl.program_id(0)

    @pl.when(step == 0)
    def _():
        start_gathered(weight_any, weight_ref, sem, layout, weight_any.shape[2])
        wait_weight(weight_ref, sem)

    @pl.when(step % wins == 0)
    def _():
        grad_mod_ref[...] = jnp.zeros(grad_mod_ref.shape, single)

    units = [grad_ref[k, u, 0] for k in range(3) for u in range(grad_ref.shape[1])]
    grads = jnp.concatenate(units, axis=1)
    grad_first = mm(grads, weight_ref[...], NT)
    normed, inverse = norm_parts(load_window(token_refs))
    grad_mod_ref[0, 0:1] += jnp.sum(grad_first, axis=0, keepdims=True)
    grad_mod_ref[0, 1:2] += jnp.sum(grad_first * normed, axis=0, keepdims=True)
    back = norm_back(normed, inverse, grad_first * (1.0 + mod_ref[0, 1:2]))
    store_window(out_refs, grad_sum_ref[0] + back)


def owner_column(layout, place_ref, step, core_apart):
    distance = reverse(step, layout.size["x"])
    return (place_ref[2] ^ distance) * 2 + (place_ref[3] ^ core_apart)


def owner_row(layout, place_ref, y, z):
    y, z = reverse(y, layout.size["y"]), reverse(z, layout.size["z"])
    return (place_ref[0] ^ z) * layout.size["y"] + (place_ref[1] ^ y)


def columns_kernel(layout, pieces, added, x_first, pair, place_ref, x_ref, *refs):
    outs = 2 if pair else 1
    y_refs, out_refs, product_ref = refs[:pieces], refs[-1 - outs : -1], refs[-1]
    split, rows, width = out_refs[0].shape[-3:]
    cols = product_ref.shape[1] // pieces
    for i in range(pieces):
        product_ref[:, i * cols : (i + 1) * cols] = mm(x_ref[0], y_refs[i][0], TN)

    def store(out_ref, first_y, last_y):
        for y in range(first_y, last_y):
            for z in range(layout.size["z"]):
                clip = owner_row(layout, place_ref, y, z)
                part = product_ref[pl.ds(pl.multiple_of(clip * rows, rows), rows)]
                for i in range(split):
                    piece = part[:, i * width : (i + 1) * width]
                    if added:
                        at = (0, y, z, i) if x_first else (y, 0, z, i)
                        piece = piece + refs[pieces][at].astype(single)
                    at = (0, y, z, i) if x_first else (y - first_y, 0, z, i)
                    out_ref[at] = piece.astype(bfloat)

    size_y = layout.size["y"]
    if not pair:
        store(out_refs[0], 0, size_y)
    elif x_first:
        half = layout.size["x"] // 2
        pl.when(pl.program_id(1) < half)(lambda: store(out_refs[0], 0, size_y))
        pl.when(pl.program_id(1) >= half)(lambda: store(out_refs[1], 0, size_y))
    else:
        store(out_refs[0], 0, size_y // 2)
        store(out_refs[1], size_y // 2, size_y)


def weight_grad(
    layout, place, x, y, pieces, added, name, x_first=False, split=1, entries=None, into=None, first=0
):
    pair = added is not None
    core_apart = 0 if pair else 1
    count, tokens, depth = x.shape
    unit = y.shape[-1] if y.ndim == 4 else y.shape[-1] // layout.win_count
    rows, cols = depth // layout.clip_size, pieces * unit
    size = layout.size

    def unit_spec(i):
        def index(n, j, place_ref):
            at = owner_column(layout, place_ref, j, core_apart) * pieces + i
            return (n * pieces + at // layout.win_count, 0, at % layout.win_count)

        if y.ndim == 3:
            return pl.BlockSpec((1, tokens, unit), index)

        def unit_index(n, j, place_ref):
            entry, _, at = index(n, j, place_ref)
            return (entry, at, 0, 0)

        return pl.BlockSpec((1, None, tokens, unit), unit_index)

    axes = ("x", "y", "z") if x_first else ("y", "x", "z")
    leading = tuple(size[axis] for axis in axes)
    half = leading[0] // 2

    def block(start, part):
        step = size["x"] if part is None else half
        lead = (1,) + leading[1:] if x_first else (leading[0] if part is None else half, 1, size["z"])

        def index(n, j, place_ref):
            at = n + start // split
            if not x_first:
                return (0, j, 0, at, 0, 0)
            if part is not None:
                j = jnp.clip(j - part * half, 0, step - 1)
            return (j, 0, 0, at, 0, 0)

        return pl.BlockSpec(lead + (split, rows, cols // split), index)

    if pair:
        out_specs = [block(first, 0), block(first, 1)]
        total = entries or count * split
        out_lead = (half,) + leading[1:]
    else:
        out_specs = [block(0, None)]
        total, out_lead = count * split, leading
    extra = ([added] if pair else []) + ([into.kept, into.sent] if into else [])
    extra_specs = ([block(0, None)] if pair else []) + ([ANY, ANY] if into else [])
    start = 2 + pieces + (1 if pair else 0)
    out_shape = jax.ShapeDtypeStruct(out_lead + (total, rows, cols // split), bfloat)
    outs = pl.pallas_call(
        functools.partial(columns_kernel, layout, pieces, pair, x_first, pair),
        grid_spec=pltpu.PrefetchScalarGridSpec(
            num_scalar_prefetch=1,
            grid=(count, size["x"]),
            in_specs=[pl.BlockSpec((1, tokens, depth), lambda n, j, p: (n, 0, 0))]
            + [unit_spec(i) for i in range(pieces)]
            + extra_specs,
            out_specs=out_specs,
            scratch_shapes=[pltpu.VMEM((depth, cols), single)],
        ),
        out_shape=[out_shape] * len(out_specs),
        input_output_aliases={start: 0, start + 1: 1} if into else {},
        compiler_params=params(),
        cost_estimate=cost(count * size["x"] * tokens * depth * cols / 382e3),
        name=name,
    )(place, x, *([y] * pieces), *extra)
    return Term(outs[0], outs[1], 3) if pair else outs[0]


def rows_kernel(layout, pair, place_ref, x_ref, *refs):
    size = layout.size["x"]
    y_refs, out_refs = refs[:size], refs[-2 if pair else -1 :]
    left = x_ref[...]

    def store(out_ref):
        for j in range(size):
            part = mm(left, y_refs[j][...], TN).reshape(out_ref.shape[3:])
            if pair:
                part = part + refs[size][0, j, 0].astype(single)
            out_ref[0, j, 0] = part.astype(bfloat)

    if not pair:
        store(out_refs[0])
        return
    half = layout.size["y"] // 2
    pl.when(pl.program_id(0) < half)(lambda: store(out_refs[0]))
    pl.when(pl.program_id(0) >= half)(lambda: store(out_refs[1]))


def weight_grad_rows(layout, place, x, y, split, added, name):
    tokens, depth = x.shape
    width = y.shape[1]
    rows, cols = depth // layout.clip_size, width // layout.win_count
    size = layout.size
    half = size["y"] // 2
    pair = added is not None

    def left(y_at, z_at, place_ref):
        return (0, owner_row(layout, place_ref, y_at, z_at))

    def right(j):
        return lambda y_at, z_at, place_ref: (
            0,
            owner_column(layout, place_ref, j, 0 if pair else 1),
        )

    def block(part):
        def index(y_at, z_at, place_ref):
            if part == 0:
                z_at = jnp.where(y_at < half, z_at, size["z"] - 1)
                y_at = jnp.minimum(y_at, half - 1)
            elif part == 1:
                z_at = jnp.where(y_at < half, 0, z_at)
                y_at = jnp.maximum(y_at - half, 0)
            return (y_at, 0, z_at, 0, 0, 0)

        return pl.BlockSpec((1, size["x"], 1, split, rows // split, cols), index)

    out_lead = (half if pair else size["y"], size["x"], size["z"])
    out_shape = jax.ShapeDtypeStruct(out_lead + (split, rows // split, cols), bfloat)
    outs = pl.pallas_call(
        functools.partial(rows_kernel, layout, pair),
        grid_spec=pltpu.PrefetchScalarGridSpec(
            num_scalar_prefetch=1,
            grid=(size["y"], size["z"]),
            in_specs=[pl.BlockSpec((tokens, rows), left)]
            + [pl.BlockSpec((tokens, cols), right(j)) for j in range(size["x"])]
            + [block(None)] * pair,
            out_specs=[block(0), block(1)] if pair else [block(None)],
        ),
        out_shape=[out_shape] * (2 if pair else 1),
        compiler_params=params(),
        cost_estimate=cost(size["x"] * tokens * depth * cols / 382e3),
        name=name,
    )(place, x, *([y] * size["x"]), *([added] if pair else []))
    return Term(outs[0], outs[1], 3) if pair else outs[0]


def to_windows(values, win_count):
    clips, count, width = values.shape
    blocks = GRID // WS
    if win_count == blocks:
        own = values.reshape(clips, FRAMES, WS, blocks, WS, width)
        received = []
        for k in range(blocks - 1, 0, -1):
            pairs = [(w, (w + k) % win_count) for w in range(win_count)]
            received.append((lax.ppermute(own[:, k : k + 1], "win", pairs), 0))
        return [(own, 0), (own, FRAMES - 1)] + received
    halves = win_count // blocks
    wins = blocks // halves
    me = lax.axis_index("win")
    whole = lax.all_gather(values, "win", axis=1, tiled=True)
    whole = whole.reshape(clips, FRAMES, blocks, WS, blocks, WS, width)
    whole = lax.dynamic_slice_in_dim(whole, me // halves, 1, axis=2)
    whole = lax.dynamic_slice_in_dim(whole, (me % halves) * wins, wins, axis=4)
    whole = whole.reshape(clips, FRAMES, WS, wins, WS, width)
    return [(whole, f) for f in range(FRAMES)]


def sent_count(win_count):
    return FRAMES - 2 if win_count == GRID // WS else 0


def send_back(sent, win_count, pin):
    blocks = GRID // WS
    received = []
    for i, array in enumerate(sent):
        k = blocks - 1 - i
        pairs = [((w + k) % win_count, w) for w in range(win_count)]
        received.append(lax.ppermute(array, "win", pairs))
    return tie(received, pin)


def put_together(whole, received, win_count):
    clips, _, _, wins, _, width = whole.shape
    blocks = GRID // WS
    if win_count == blocks:
        for i, array in enumerate(received):
            whole = lax.dynamic_update_slice_in_dim(whole, array, blocks - 1 - i, axis=1)
        return whole.reshape(clips, FRAMES * WS * blocks * WS, width)
    halves = win_count // blocks
    me = lax.axis_index("win")
    whole = lax.all_gather(whole, "win", axis=0, tiled=False)
    whole = whole.reshape(blocks, halves, clips, FRAMES, WS, wins, WS, width)
    whole = whole.transpose(2, 3, 0, 4, 1, 5, 6, 7).reshape(clips, SEQ, width)
    count = SEQ // win_count
    return lax.dynamic_slice_in_dim(whole, me * count, count, axis=1)


def gather_first(arrays, squares, layout):
    me = lax.axis_index("win")
    held, squares = jnp.concatenate([a.reshape(-1) for a in arrays])[None], squares[None]
    win_bits = layout.win_count.bit_length() - 1
    for bit in range(max(win_bits, layout.bits("z"))):
        apart, came, part = layout.win_count >> (bit + 1), held, squares
        if bit < win_bits:
            pairs = [(i, i ^ apart) for i in range(layout.win_count)]
            came = lax.ppermute(held, "win", pairs)
        if bit < layout.bits("z"):
            part = layout.swap(squares, "z", 1 << bit)
        came, part = tie(came, part)
        if bit < win_bits:
            upper = (me & apart) > 0
            first, second = jnp.where(upper, came, held), jnp.where(upper, held, came)
            held = jnp.stack([first, second], axis=1).reshape(2 * held.shape[0], held.shape[1])
        if bit < layout.bits("z"):
            squares = jnp.concatenate([squares, part], axis=0)
    outs, at = [], 0
    for a in arrays:
        outs.append(held[:, at : at + a.size].reshape((layout.win_count,) + a.shape))
        at += a.size
    return outs, squares


def sum_over_win(values, layout):
    me = lax.axis_index("win")
    apart = layout.win_count // 2
    while apart > 0:
        upper = (me & apart) > 0
        first, second = values[:apart], values[apart:]
        sent = jnp.where(upper, first, second)
        kept = jnp.where(upper, second, first)
        pairs = [(i, i ^ apart) for i in range(layout.win_count)]
        values = kept + lax.ppermute(sent, "win", pairs)
        apart //= 2
    return values[0]


def sum_over_clip(values, layout, apart, end):
    while apart < end:
        pairs = [(i, i ^ apart) for i in range(layout.clip_size)]
        values = values + lax.ppermute(values, "clip", pairs)
        apart *= 2
    return values


def local(
    tokens,
    cotangent,
    modulation,
    text_features,
    null_mask,
    null_text,
    norm_gain,
    position_bias,
    self_input,
    self_output,
    cross_query,
    cross_memory,
    cross_output,
    expand_weight,
    reduce_weight,
):
    win_count = lax.axis_size("win")
    clip_size = lax.axis_size("clip")
    layout = Layout(clip_size, win_count)
    place = layout.place()
    blocks = GRID // WS
    clips, _, width = tokens.shape
    hidden_width = reduce_weight.shape[0] * clip_size
    both = ("clip", "win")
    me = lax.axis_index("win")

    input_all = lax.all_gather(self_input, both, axis=0, tiled=False)
    small = [position_bias, norm_gain.astype(single), null_text.astype(single)]
    squares = jnp.concatenate([self_output, cross_query, cross_output, cross_memory], axis=1)
    (bias_full, gain_full, null_full), squares = gather_first(small, squares, layout)
    bias_full = bias_full.reshape(HEADS, NREL)
    pieces = to_windows(tokens, win_count)
    wins = pieces[0][0].shape[3]
    windows = clips * wins
    count = windows * WIN_TOK
    sent = sent_count(win_count)
    columns = width // win_count
    gain_full = gain_full.reshape(1, width)
    null_full = null_full.transpose(1, 0, 2).reshape(TXT, width).astype(bfloat)
    shift = me if win_count == blocks else jnp.int32(0)
    shift = jnp.asarray(shift, jnp.int32).reshape(1)
    blocks_of_bias = table_blocks(bias_full)
    memory_part, squares_part = squares[:, :, 3 * columns :], squares[:, :, : 3 * columns]
    memory_part, blocks_of_bias = layout.gather_axis(memory_part, "y", blocks_of_bias)
    squares_part, blocks_of_bias = layout.gather_axis(squares_part, "x", blocks_of_bias)
    memory_part, squares_part, blocks_of_bias = tie(memory_part, squares_part, blocks_of_bias)
    table = bias_table(blocks_of_bias, shift)
    table, arrays = tie(table, [p[0] for p in pieces])
    pieces = [(array, frame) for array, (_, frame) in zip(arrays, pieces)]
    depth = expand_weight.shape[0]
    feed_shard = jnp.concatenate(
        [expand_weight]
        + [reduce_weight[i : i + depth] for i in range(0, reduce_weight.shape[0], depth)],
        axis=1,
    )
    feed_all = lax.all_gather(feed_shard, both, axis=0, tiled=False)

    token_specs = [piece_spec(wins, width, frame) for _, frame in pieces]
    tokens_in = [array for array, _ in pieces]

    shape = jax.ShapeDtypeStruct
    rows = functools.partial(shape, dtype=bfloat)
    wide = rows((windows, WIN_TOK, width))
    triple = rows((3, windows, WIN_TOK, width))
    triple_spec = pl.BlockSpec((3, 1, WIN_TOK, width), lambda i: (0, i, 0, 0))
    units = rows((3, win_count, windows, WIN_TOK, columns))
    units_spec = pl.BlockSpec((3, win_count, 1, WIN_TOK, columns), lambda i: (0, 0, i, 0, 0))
    wide_single = shape((windows, WIN_TOK, width), single)
    DMA = pltpu.SemaphoreType.DMA

    first_low, projected = pl.pallas_call(
        functools.partial(project_kernel, layout),
        grid=(windows,),
        in_specs=token_specs + [modulation_spec(wins, width), ANY],
        out_specs=[rows_spec(width), rows_spec(3 * width)],
        out_shape=[wide, rows((windows, WIN_TOK, 3 * width))],
        scratch_shapes=[pltpu.VMEM((width, 3 * width), bfloat), DMA(())],
        compiler_params=params(),
        cost_estimate=cost(26),
        name="project",
    )(*tokens_in, modulation, input_all)
    memory_near, memory_far, projected = layout.gather_last(memory_part, "x", projected)
    squares_near, squares_far, projected = layout.gather_last(squares_part, "y", projected)
    memory_all = layout.with_other_core(memory_near, memory_far)
    squares_all = layout.with_other_core(squares_near, squares_far)

    attended, probs = pl.pallas_call(
        attend_kernel,
        grid=(windows,),
        in_specs=[rows_spec(3 * width), BIAS_SPEC],
        out_specs=[rows_spec(width), PROBS_SPEC],
        out_shape=[wide, rows((windows, QUADS, WIN_TOK, LANES))],
        scratch_shapes=[pltpu.VMEM((2, WIN_TOK, LANES), single)],
        compiler_params=params(),
        cost_estimate=cost(37),
        name="attend",
    )(projected, table)

    cotangent, attended = tie(cotangent, attended)
    grad_pieces = to_windows(cotangent, win_count)

    null_flags = null_mask > 0
    used_text = jnp.where(null_flags[:, None, None], null_full[None], text_features)
    text_padded = jnp.pad(used_text, ((0, 0), (0, TEXT_ROWS - TXT), (0, 0)))
    text_spec = pl.BlockSpec((1, TEXT_ROWS, width), lambda i: (i, 0, 0))
    memory = pl.pallas_call(
        functools.partial(memory_kernel, layout),
        grid=(clips,),
        in_specs=[PLACE, text_spec, ANY, ANY, ANY, ANY],
        out_specs=pl.BlockSpec((1, TEXT_ROWS, 2 * width), lambda i: (i, 0, 0)),
        out_shape=rows((clips, TEXT_ROWS, 2 * width)),
        scratch_shapes=[pltpu.VMEM((width, 2 * width), bfloat), DMA(())],
        compiler_params=params(),
        cost_estimate=cost(6),
        name="memory",
    )(place, text_padded, *memory_all)

    gain_spec = pl.BlockSpec((1, width), lambda i: (0, 0))
    memory_spec = pl.BlockSpec((1, TEXT_ROWS, 2 * width), lambda i: (i // wins, 0, 0))
    square = pltpu.VMEM((width, width), bfloat)
    branch, lefts, cross_queries, second_sum = pl.pallas_call(
        functools.partial(cross_kernel, layout),
        grid=(windows,),
        in_specs=[
            PLACE,
            *token_specs,
            rows_spec(width),
            modulation_spec(wins, width),
            gain_spec,
            memory_spec,
            ANY,
            ANY,
            ANY,
            ANY,
        ],
        out_specs=[rows_spec(width), triple_spec, rows_spec(width), rows_spec(width)],
        out_shape=[wide_single, triple, wide, wide_single],
        scratch_shapes=[square, square, square, DMA((3,))],
        compiler_params=params(),
        cost_estimate=cost(42),
        name="cross",
    )(
        place,
        *tokens_in,
        attended,
        modulation,
        gain_full,
        memory,
        *squares_all,
    )

    window_shape = (clips, FRAMES, WS, wins, WS, width)
    piece_shape = (clips, 1, WS, wins, WS, width)
    out_specs = [whole_spec(wins, width)] + [piece_spec(wins, width, 0)] * sent
    out_shapes = [rows(window_shape)] + [rows(piece_shape)] * sent
    feed_out = pl.pallas_call(
        functools.partial(feed_kernel, layout, wins, 1024, sent),
        grid=(windows,),
        in_specs=[piece_spec(wins, width, frame) for _, frame in grad_pieces]
        + [rows_spec(width), modulation_spec(wins, width), ANY],
        out_specs=out_specs
        + [
            rows_spec(width),
            rows_spec(hidden_width),
            rows_spec(hidden_width),
            rows_spec(width),
            rows_spec(width),
            pl.BlockSpec((1, 3, width), lambda i: (i // wins, 0, 0)),
        ],
        out_shape=out_shapes
        + [
            wide,
            rows((windows, WIN_TOK, hidden_width)),
            rows((windows, WIN_TOK, hidden_width)),
            wide,
            wide_single,
            shape((clips, 3, width), single),
        ],
        scratch_shapes=[
            pltpu.VMEM((width, hidden_width), bfloat),
            pltpu.VMEM((hidden_width, width), bfloat),
            DMA((2,)),
        ],
        compiler_params=params(),
        cost_estimate=cost(117),
        name="feed",
    )(*[array for array, _ in grad_pieces], second_sum, modulation, feed_all)
    block_pieces, feed_out = feed_out[: 1 + sent], feed_out[1 + sent :]
    third_low, activated, grad_hidden, grad_reduced, grad_second_sum, feed_mod = feed_out

    def flat(values):
        return values.reshape(-1, count, values.shape[-1])

    def flat_units(values):
        return values.reshape(-1, win_count, count, columns)

    expand_of = (layout, place, flat(third_low), flat(grad_hidden), 1)
    reduce_of = (layout, place, flat(activated)[0], flat(grad_reduced)[0], 4)
    reduce_sent = layout.swap(weight_grad_rows(*reduce_of, None, "reduce_other"), "core", 1)
    expand_sent = layout.swap(weight_grad(*expand_of, None, "expand_other", True, 4), "core", 1)
    reduce_term = weight_grad_rows(*reduce_of, reduce_sent, "reduce_own")
    expand_sent, reduce_term = tie(expand_sent, reduce_term)
    expand_term = weight_grad(*expand_of, expand_sent, "expand_own", True, 4)
    grad_second_sum, expand_term = tie(grad_second_sum, expand_term)

    rights, grad_first_sum, grad_attended, grad_memory, gain_term, gate_mod = pl.pallas_call(
        functools.partial(cross_back_kernel, layout, wins),
        grid=(windows,),
        in_specs=[
            PLACE,
            *token_specs,
            modulation_spec(wins, width),
            gain_spec,
            memory_spec,
            rows_spec(width),
            rows_spec(width),
            rows_spec(width),
            ANY,
            ANY,
            ANY,
            ANY,
        ],
        out_specs=[
            units_spec,
            rows_spec(width),
            rows_spec(width),
            memory_spec,
            gain_spec,
            pl.BlockSpec((1, 1, width), lambda i: (i // wins, 0, 0)),
        ],
        out_shape=[
            units,
            wide_single,
            wide,
            shape((clips, TEXT_ROWS, 2 * width), single),
            shape((1, width), single),
            shape((clips, 1, width), single),
        ],
        scratch_shapes=[square, square, square, DMA((3,))],
        compiler_params=params(),
        cost_estimate=cost(63),
        name="cross_back",
    )(
        place,
        *tokens_in,
        modulation,
        gain_full,
        memory,
        grad_second_sum,
        cross_queries,
        branch,
        *squares_all,
    )
    reduce_stage, grad_attended = layout.reduce_axes([reduce_term], ["y"], grad_attended)
    expand_stage, grad_attended = layout.reduce_axes([expand_term], ["x"], grad_attended)
    rights, grad_memory, reduce_stage, expand_stage = tie(
        rights, grad_memory, reduce_stage, expand_stage
    )

    text_rows = text_padded.reshape(1, clips * TEXT_ROWS, width)
    memory_low = grad_memory.astype(bfloat).reshape(1, clips * TEXT_ROWS, 2 * width)
    square_of = (layout, place, flat(lefts), flat_units(rights), 1)
    memory_of = (layout, place, text_rows, memory_low, 1)
    memory_sent = weight_grad(*memory_of, None, "memory_other", split=2)
    rights, memory_sent = tie(rights, memory_sent)
    memory_sent = layout.swap(memory_sent, "core", 1)
    square_sent = weight_grad(*square_of, None, "square_other")
    masked = jnp.sum(jnp.where(null_flags[:, None, None], grad_memory, 0.0), axis=0)
    square_sent, masked = tie(square_sent, masked)
    square_sent = layout.swap(square_sent, "core", 1)
    null_term = null_text_term(layout, place, masked, memory_all)[:TXT]
    memory_sent, null_term = tie(memory_sent, null_term)
    rest_term = weight_grad(*memory_of, memory_sent, "memory_own", split=2, entries=5)
    square_sent, rest_term = tie(square_sent, rest_term)
    rest_term = weight_grad(
        *square_of, square_sent, "square_own", entries=5, into=rest_term, first=2
    )
    feed_stage, rest_term = layout.reduce_axes([expand_stage, reduce_stage], ["y", "x"], rest_term)
    grad_attended, feed_stage, rest_term, block_pieces = tie(
        grad_attended, feed_stage, rest_term, block_pieces
    )

    grad_projected, bias_sum = pl.pallas_call(
        attend_back_kernel,
        grid=(windows,),
        in_specs=[rows_spec(3 * width), rows_spec(width), PROBS_SPEC],
        out_specs=[units_spec, BIAS_SPEC],
        out_shape=[units, shape((QUADS, WIN_TOK, LANES), single)],
        scratch_shapes=[
            pltpu.VMEM((2, WIN_TOK, LANES), single),
            pltpu.VMEM((2, WIN_TOK, LANES), bfloat),
        ],
        compiler_params=params(),
        cost_estimate=cost(48),
        name="attend_back",
    )(projected, grad_attended, probs)

    feed_stage, bias_sum = layout.reduce([feed_stage], ["z"], [1], bias_sum)
    rest_stage, bias_sum = layout.reduce_axes([rest_term], ["y"], bias_sum)
    block_came, bias_sum = send_back(block_pieces[1:], win_count, bias_sum)
    grad_projected, rest_stage, feed_stage, block_came = tie(
        grad_projected, rest_stage, feed_stage, block_came
    )
    input_of = (layout, place, flat(first_low), flat_units(grad_projected), 3)
    input_sent = weight_grad(*input_of, None, "input_other", True, 3)
    input_sent = layout.swap(input_sent, "core", 1)
    input_term = weight_grad(*input_of, input_sent, "input_own", True, 3)
    bias_sum, input_term = tie(bias_sum, input_term)
    position_flat = bias_blocks(bias_sum, shift)
    for bit in range(1, layout.bits("z")):
        feed_stage, position_flat = layout.reduce([feed_stage], ["z"], [1 << bit], position_flat)
    rest_stage, position_flat = layout.reduce_axes([rest_stage], ["x"], position_flat)
    position_term = bias_collect(position_flat)
    grad_projected, rest_stage, feed_grad, position_term = tie(
        grad_projected, rest_stage, feed_stage, position_term
    )

    input_out = pl.pallas_call(
        functools.partial(input_back_kernel, layout, wins, sent),
        grid=(windows,),
        in_specs=token_specs + [modulation_spec(wins, width), units_spec, rows_spec(width), ANY],
        out_specs=out_specs + [pl.BlockSpec((1, 2, width), lambda i: (i // wins, 0, 0))],
        out_shape=out_shapes + [shape((clips, 2, width), single)],
        scratch_shapes=[pltpu.VMEM((width, 3 * width), bfloat), DMA(())],
        compiler_params=params(),
        cost_estimate=cost(29),
        name="input_back",
    )(*tokens_in, modulation, grad_projected, grad_first_sum, input_all)
    first_mod = input_out[-1]
    input_stage, first_mod = layout.reduce_axes([input_term], ["x"], first_mod)
    input_stage, first_mod = tie(input_stage, first_mod)
    rest_stage, first_mod = layout.reduce([rest_stage], ["z"], [1], first_mod)
    expand_grad = jnp.concatenate(list(feed_grad[:4]), axis=1)
    reduce_grad = feed_grad[4:].reshape(4 * depth, columns)
    heads_local = HEADS // win_count
    modulation_term = jnp.concatenate([first_mod, gate_mod, feed_mod], axis=1)
    by_columns = jnp.concatenate(
        [modulation_term.reshape(clips * 6, width), gain_term, null_term], axis=0
    )
    by_columns = by_columns.reshape(-1, win_count, columns).transpose(1, 0, 2)
    small_term = jnp.concatenate(
        [
            by_columns.reshape(win_count, -1),
            position_term.reshape(win_count, heads_local * NREL),
        ],
        axis=1,
    )
    small_term = sum_over_win(small_term, layout)
    block_whole, block_came, small_term = tie(block_pieces[0], block_came, small_term)
    block_output = put_together(block_whole, block_came, win_count)
    for bit in range(1, layout.bits("z")):
        rest_stage, small_term = layout.reduce([rest_stage], ["z"], [1 << bit], small_term)
    cross_memory_grad = jnp.concatenate([rest_stage[0], rest_stage[1]], axis=1)
    input_stage, small_term = layout.reduce_axes([input_stage], ["y"], small_term)
    modulation_grad = small_term[: clips * 6 * columns].reshape(clips, 6, columns)
    small_grad = sum_over_clip(small_term[clips * 6 * columns :], layout, 1, clip_size // 2)
    tokens_came, small_grad = send_back(input_out[1 : 1 + sent], win_count, small_grad)
    tokens_grad = put_together(input_out[0], tokens_came, win_count)
    input_stage, small_grad = layout.reduce([input_stage], ["z"], [1], small_grad)
    small_grad = sum_over_clip(small_grad, layout, clip_size // 2, clip_size)
    gain_grad = small_grad[:columns]
    null_grad = small_grad[columns : (1 + TXT) * columns].reshape(TXT, columns)
    position_grad = small_grad[(1 + TXT) * columns :].reshape(heads_local, NREL)
    for bit in range(1, layout.bits("z")):
        input_stage, small_grad = layout.reduce([input_stage], ["z"], [1 << bit], small_grad)
    self_input_grad = jnp.concatenate(list(input_stage), axis=1)
    self_output_grad, cross_query_grad, cross_output_grad = rest_stage[2:]
    return (
        block_output,
        tokens_grad,
        self_input_grad,
        self_output_grad,
        cross_query_grad,
        cross_memory_grad,
        cross_output_grad,
        expand_grad,
        reduce_grad,
        gain_grad,
        null_grad,
        position_grad,
        modulation_grad,
    )


def solution(mesh):
    in_specs = (
        P("clip", "win", None),
        P("clip", "win", None),
        P("clip", None, None),
        P("clip", None, None),
        P("clip"),
        P(None, "win"),
        P("win"),
        P("win", None),
        P("clip", "win"),
        P("clip", "win"),
        P("clip", "win"),
        P("clip", "win"),
        P("clip", "win"),
        P("clip", "win"),
        P("clip", "win"),
    )
    out_specs = (
        P("clip", "win", None),
        P("clip", "win", None),
        P("clip", "win"),
        P("clip", "win"),
        P("clip", "win"),
        P("clip", "win"),
        P("clip", "win"),
        P("clip", "win"),
        P("clip", "win"),
        P("win"),
        P(None, "win"),
        P("win", None),
        P("clip", None, "win"),
    )
    return jax.shard_map(local, mesh=mesh, in_specs=in_specs, out_specs=out_specs, check_vma=False)
```

time: 1040 us -> 839 us (0.81)
  waiting for transfers between devices: 227 us -> 120 us
  local copies, waits for them, and re-layouts: 103 us -> 51.9 us
  Pallas kernels: 587 us -> 562 us
  other arithmetic: 53.5 us -> 29.5 us
    ppermute x28 -> x29, waiting for transfers between devices: 135 us -> 78.9 us  [swap(): return lax.ppermute(values, home, [(i, i ^ step) for i in range(count)])]
    ppermute x14, waiting for transfers between devices: 70.5 us -> 15.4 us  [the longest x6 14.8 us: to_windows(): received.append((lax.ppermute(own[:, k:k + 1], 'win', pairs), 0))]
    unnamed x112 -> x76, local copies, waits for them, and re-layouts: 37.8 us -> 5.38 us
    slice x25 -> x6, local copies, waits for them, and re-layouts: 26.2 us -> 8.2 us  [the longest x2 7.19 us: to_windows(): received.append((lax.ppermute(own[:, k:k + 1], 'win', pairs), 0))]
    dynamic_update_slice x0 -> x6, local copies, waits for them, and re-layouts: none -> 12.5 us  [put_together(): lax.dynamic_update_slice_in_dim(whole, array, blocks - 1 - i, axis=1)]
    pallas_call x15 -> x25, Pallas kernels: 428 us -> 421 us  [the longest x1 118 us: local(): pl.pallas_call(functools.partial(feed_kernel, layout, wins, 1024, sent),...]
    ppermute x28 -> x29, starting transfers between devices: 27 us -> 26.5 us  [swap(): return lax.ppermute(values, home, [(i, i ^ step) for i in range(count)])]
  transfers between devices with their start and end apart: 49 -> 50, of which waited for: 21 -> 18; matrix products, arithmetic and copies ran while one was open for 13% -> 9% of each run, Pallas kernels for 39% -> 42%
where the time goes in v2:
time: 839 us; the launch traced here: 828 us
  Pallas kernels  562 us (67%)
  waiting for transfers between devices  120 us (14%)
  local copies, waits for them, and re-layouts  51.9 us (6%)
  starting transfers between devices  42.9 us (5%)
  other arithmetic  29.5 us (4%)
  between operations  15.4 us (2%)
    pallas_call x1, Pallas kernels, local(): pl.pallas_call(functools.partial(feed_kernel, layout, wins, 1024, sent),...  118 us
    pallas_call x8, Pallas kernels, weight_grad(): pl.pallas_call(functools.partial(columns_kernel, layout, pieces, pair, x_...  113 us
    ppermute x29, waiting for transfers between devices, swap(): return lax.ppermute(values, home, [(i, i ^ step) for i in range(count)])  78.9 us
    pallas_call x1, Pallas kernels, local(): pl.pallas_call(functools.partial(cross_back_kernel, layout, wins), grid=(...  56.5 us
    pallas_call x1, Pallas kernels, local(): pl.pallas_call(attend_back_kernel, grid=(windows,), in_specs=[rows_spec(3...  48 us
    pallas_call x1, Pallas kernels, local(): pl.pallas_call(functools.partial(cross_kernel, layout), grid=(windows,),...  41 us
    pallas_call x2, Pallas kernels, weight_grad_rows(): pl.pallas_call(functools.partial(rows_kernel, layout, pair), grid_spec=pl...  37.3 us
    pallas_call x1, Pallas kernels, local(): pl.pallas_call(attend_kernel, grid=(windows,), in_specs=[rows_spec(3 * wi...  36.8 us
  transfers between devices with their start and end apart: 50, of which 18 were waited for; matrix products, arithmetic and copies ran while one was open for 9% of the time, Pallas kernels for 42%

profile of v2, /device:TPU:0, one launch (start us, length us, event | category | flops | bytes accessed | tf_op | source)
XLA Modules:
  0.0 827.5 jit_solution(15361772789464300518)
XLA Ops:
  9.0 3.1 collective-permute-start.1
  16.1 3.6 fusion.65
  19.7 1.7 collective-permute-start.8
  23.0 6.8 fusion.4
  30.0 2.7 collective-permute-start.3
  35.5 31.8 %collective-permute-done.3 = bf16[2,128,1280]{2,1,0:T(8,128)(2,1)S(1)} collective-permute-done((bf16[2,128,1280]{2,1,0:T(8,128)(2,1)S(1)}, bf16[2,128,1280]{2,1,0:T(8,128)(2,1)S(1)}, u32[]{:S(2)}, u32[]{:S(2)}) %collective-permute-start.3) | collective-permute-done | bytes 655392 | tf_op jit(solution)/shard_map/ppermute | solution.py:113
  72.9 3.6 convolution_bitcast_fusion
  76.6 5.9 copy.49
  82.5 6.0 reshape.316.block_ref
  90.5 2.1 pad_maximum_fusion.1.refs_0_
  92.6 10.5 %collective-permute-done.5 = bf16[4,128,768]{2,1,0:T(8,128)(2,1)} collective-permute-done((bf16[4,128,768]{2,1,0:T(8,128)(2,1)S(1)}, bf16[4,128,768]{2,1,0:T(8,128)(2,1)}, u32[]{:S(2)}, u32[]{:S(2)}) %collective-permute-start.5) | collective-permute-done | bytes 786464 | tf_op jit(solution)/shard_map/ppermute | solution.py:113
  103.1 2.5 pad_maximum_fusion.refs_9_.refs_11_
  106.1 4.9 bias_table.1.bias_ref
  114.3 25.9 %project.1 = (bf16[8,320,1024]{2,1,0:T(8,128)(2,1)}, bf16[8,320,3072]{2,1,0:T(8,128)(2,1)}) custom-call(bf16[2,5,8,4,8,1024]{5,4,3,2,1,0:T(8,128)(2,1)} %bitcast.128, bf16[2,5,8,4,8,1024]{5,4,3,2,1,0:T(8,128)(2,1)} %bitcast.129, bf16[2,1,8,4,8,1024]{5,4,3,2,1,0:T(8,128)(2,1)} %collective-permute-done.8.refs_2_, ...), custom_call_target="tpu_custom_call" | custom-call | flops 19759999483904 | bytes 25999998976 | tf_op jit(solution)/shard_map/project/pallas_call | solution.py:1057
  140.5 13.1 %collective-permute-done.6.refs_10_.refs_12_ = bf16[8,128,768]{2,1,0:T(8,128)(2,1)} collective-permute-done((bf16[8,128,768]{2,1,0:T(8,128)(2,1)}, bf16[8,128,768]{2,1,0:T(8,128)(2,1)}, u32[]{:S(2)}, u32[]{:S(2)}) %collective-permute-start.6) | collective-permute-done | bytes 1572896 | tf_op jit(solution)/shard_map/ppermute | solution.py:113
  153.6 36.8 %attend.1 = (bf16[8,320,1024]{2,1,0:T(8,128)(2,1)}, bf16[8,4,320,1280]{3,2,1,0:T(8,128)(2,1)}) custom-call(bf16[8,320,3072]{2,1,0:T(8,128)(2,1)} %get-tuple-element.203.projected_ref, f32[4,320,1280]{2,1,0:T(8,128)} %bias_table.1.bias_ref), custom_call_target="tpu_custom_call" | custom-call | flops 28120000233472 | bytes 36999999488 | tf_op jit(solution)/shard_map/attend/pallas_call | solution.py:1073
  190.3 3.6 fusion.64
  196.1 5.8 memory.1.refs_8_.refs_7_
  201.9 41.0 %cross.1 = (f32[8,320,1024]{2,1,0:T(8,128)}, bf16[3,8,320,1024]{3,2,1,0:T(8,128)(2,1)}, bf16[8,320,1024]{2,1,0:T(8,128)(2,1)}, f32[8,320,1024]{2,1,0:T(8,128)}) custom-call(s32[4]{0:T(128)} %pad_add_fusion.place_ref, bf16[2,5,8,4,8,1024]{5,4,3,2,1,0:T(8,128)(2,1)} %bitcast.130, bf16[2,5,8,4,8,1024]{5,4,3,2,1,0:T(8,128)(2,1)} %bitcast.131, ...), custom_call_target="tpu_custom_call" | custom-call | flops 31919999811584 | bytes 41999998976 | tf_op jit(solution)/shard_map/cross/pallas_call | solution.py:1107
  243.0 14.8 %collective-permute-done.12.refs_3_ = bf16[2,1,8,4,8,1024]{5,4,3,2,1,0:T(8,128)(2,1)} collective-permute-done((bf16[2,1,8,4,8,1024]{5,4,3,2,1,0:T(8,128)(2,1)}, bf16[2,1,8,4,8,1024]{5,4,3,2,1,0:T(8,128)(2,1)}, u32[]{:S(2)}, u32[]{:S(2)}) %collective-permute-start.12) | collective-permute-done | bytes 1048608 | tf_op jit(solution)/shard_map/ppermute | solution.py:896
  257.8 117.8 %feed.1 = (bf16[2,5,8,4,8,1024]{5,4,3,2,1,0:T(8,128)(2,1)}, bf16[2,1,8,4,8,1024]{5,4,3,2,1,0:T(8,128)(2,1)}, bf16[2,1,8,4,8,1024]{5,4,3,2,1,0:T(8,128)(2,1)}, bf...) custom-call(bf16[2,5,8,4,8,1024]{5,4,3,2,1,0:T(8,128)(2,1)} %bitcast, ...), custom_call_target="tpu_custom_call" | custom-call | flops 88919999774720 | bytes 117000003584 | tf_op jit(solution)/shard_map/feed/pallas_call | solution.py:1142
  375.6 18.1 %reduce_other.1 = bf16[2,2,4,4,128,256]{5,4,3,2,1,0:T(8,128)(2,1)} custom-call(s32[4]{0:T(128)} %pad_add_fusion.place_ref, bf16[2560,4096]{1,0:T(8,128)(2,1)} %bitcast.166, bf16[2560,1024]{1,0:T(8,128)(2,1)} %bitcast.182, bf16[2560,1024]{1,0:T(8,128)(2,1)} %bitcast.183), custom_call_target="tpu_custom_call" | custom-call | flops 10681201413062656 | bytes 14054211977216 | tf_op jit(solution)/shard_map/reduce_other/pallas_call | solution.py:870
  393.7 17.8 %expand_other.1 = bf16[2,2,4,4,128,256]{5,4,3,2,1,0:T(8,128)(2,1)} custom-call(s32[4]{0:T(128)} %pad_add_fusion.place_ref, bf16[1,2560,1024]{2,1,0:T(8,128)(2,1)} %bitcast.180, bf16[1,2560,4096]{2,1,0:T(8,128)(2,1)} %bitcast.164), custom_call_target="tpu_custom_call" | custom-call | flops 10681201413062656 | bytes 14054211977216 | tf_op jit(solution)/shard_map/expand_other/pallas_call | solution.py:799
  412.0 19.3 %reduce_own.1 = (bf16[1,2,4,4,128,256]{5,4,3,2,1,0:T(8,128)(2,1)}, bf16[1,2,4,4,128,256]{5,4,3,2,1,0:T(8,128)(2,1)}) custom-call(s32[4]{0:T(128)} %pad_add_fusion.place_ref, bf16[2560,4096]{1,0:T(8,128)(2,1)} %bitcast.167, bf16[2560,1024]{1,0:T(8,128)(2,1)} %bitcast.184, bf16[2560,1024]{1,0:T(8,128)(2,1)} %bitcast.185, ...), custom_call_target="tpu_custom_call" | custom-call | flops 10681201413062656 | bytes 14054211977216 | tf_op jit(solution)/shard_map/reduce_own/pallas_call | solution.py:870
  431.3 19.4 %expand_own.1 = (bf16[1,2,4,4,128,256]{5,4,3,2,1,0:T(8,128)(2,1)}, bf16[1,2,4,4,128,256]{5,4,3,2,1,0:T(8,128)(2,1)}) custom-call(s32[4]{0:T(128)} %pad_add_fusion.place_ref, bf16[1,2560,1024]{2,1,0:T(8,128)(2,1)} %bitcast.181, bf16[1,2560,4096]{2,1,0:T(8,128)(2,1)} %bitcast.165, bf16[2,2,4,4,128,256]{5,4,3,2,1,0:T(8,128)(2,1)} %collective-permute-done.18.refs_1_), custom_call_target="tpu_custom_call" | custom-call | flops 10681201413062656 | bytes 14054211977216 | tf_op jit(solution)/shard_map/expand_own/pallas_call | solution.py:799
  452.7 56.5 %cross_back.1 = (bf16[3,4,8,320,256]{4,3,2,1,0:T(8,128)(2,1)}, f32[8,320,1024]{2,1,0:T(8,128)}, bf16[8,320,1024]{2,1,0:T(8,128)(2,1)}, f32[2,80,2048]{2,1,0:T(8,...) custom-call(s32[4]{0:T(128)} %pad_add_fusion.place_ref, bf16[2,5,8,4,8,1024]{5,4,3,2,1,0:T(8,128)(2,1)} %bitcast.132, ...), custom_call_target="tpu_custom_call" | custom-call | flops 47880001814528 | bytes 62999998464 | tf_op jit(solution)/shard_map/cross_back/pallas_call | solution.py:1192
  509.3 4.3 add_halves.11
  513.6 4.2 add_halves.10
  517.8 3.6 fusion.66
  521.4 17.7 %square_other.1 = bf16[2,2,4,3,128,256]{5,4,3,2,1,0:T(8,128)(2,1)} custom-call(s32[4]{0:T(128)} %pad_add_fusion.place_ref, bf16[3,2560,1024]{2,1,0:T(8,128)(2,1)} %bitcast.168, bf16[3,4,2560,256]{3,2,1,0:T(8,128)(2,1)} %bitcast.176), custom_call_target="tpu_custom_call" | custom-call | flops 8010901059796992 | bytes 10540659245056 | tf_op jit(solution)/shard_map/square_other/pallas_call | solution.py:799
  539.1 3.9 memory_other.1
  543.9 1.7 collective-permute-start.23
  545.6 6.9 null_text.1
  552.5 4.5 memory_own.1
  557.0 18.3 %square_own.1 = (bf16[1,2,4,5,128,256]{5,4,3,2,1,0:T(8,128)(2,1)}, bf16[1,2,4,5,128,256]{5,4,3,2,1,0:T(8,128)(2,1)}) custom-call(s32[4]{0:T(128)} %pad_add_fusion.place_ref, bf16[3,2560,1024]{2,1,0:T(8,128)(2,1)} %bitcast.169, bf16[3,4,2560,256]{3,2,1,0:T(8,128)(2,1)} %bitcast.177, ...), custom_call_target="tpu_custom_call", output_to_operand_aliasing={{0}: (4, {}), {1}: (5, {})} | custom-call | flops 8010901059796992 | bytes 10540659245056 | tf_op jit(solution)/shard_map/square_own/pallas_call | solution.py:799
  575.3 3.4 add_halves.12
  583.6 48.0 %attend_back.1 = (bf16[3,4,8,320,256]{4,3,2,1,0:T(8,128)(2,1)}, f32[4,320,1280]{2,1,0:T(8,128)}) custom-call(bf16[8,320,3072]{2,1,0:T(8,128)(2,1)} %get-tuple-element.203.projected_ref, bf16[8,320,1024]{2,1,0:T(8,128)(2,1)} %get-tuple-element.268.grad_ref, bf16[8,4,320,1280]{3,2,1,0:T(8,128)(2,1)} %get-tuple-element.269.probs_ref), custom_call_target="tpu_custom_call" | custom-call | flops 36480000983040 | bytes 48000000000 | tf_op jit(solution)/shard_map/attend_back/pallas_call | solution.py:1269
  631.6 2.6 add_halves.14
  634.3 4.1 collective-permute-done.26
  638.4 4.6 add_halves.13
  643.0 15.1 %input_other.1 = bf16[2,2,4,3,128,256]{5,4,3,2,1,0:T(8,128)(2,1)} custom-call(s32[4]{0:T(128)} %pad_add_fusion.place_ref, bf16[1,2560,1024]{2,1,0:T(8,128)(2,1)} %bitcast.178, bf16[3,4,2560,256]{3,2,1,0:T(8,128)(2,1)} %bitcast.170, bf16[3,4,2560,256]{3,2,1,0:T(8,128)(2,1)} %bitcast.171, bf16[3,4,2560,256]{3,2,1,0:T(8,128)(2,1)} %bitcast.172), custom_call_target="tpu_custom_call" | custom-call | flops 8010901059796992 | bytes 10540659245056 | tf_op jit(solution)/shard_map/input_other/pallas_call | solution.py:799
  660.8 2.4 collective-permute-start.32
  664.0 1.7 copy-done.31
  665.7 16.4 %input_own.1 = (bf16[1,2,4,3,128,256]{5,4,3,2,1,0:T(8,128)(2,1)}, bf16[1,2,4,3,128,256]{5,4,3,2,1,0:T(8,128)(2,1)}) custom-call(s32[4]{0:T(128)} %pad_add_fusion.place_ref, bf16[1,2560,1024]{2,1,0:T(8,128)(2,1)} %bitcast.179, bf16[3,4,2560,256]{3,2,1,0:T(8,128)(2,1)} %bitcast.173, bf16[3,4,2560,256]{3,2,1,0:T(8,128)(2,1)} %bitcast.174, ...), custom_call_target="tpu_custom_call" | custom-call | flops 8010901059796992 | bytes 10540659245056 | tf_op jit(solution)/shard_map/input_own/pallas_call | solution.py:799
  682.1 6.1 bias_collect.1
  688.2 3.9 reshape.337
  692.1 2.3 collective-permute-done.31
  694.5 2.7 fusion.30
  698.0 2.1 add_bitcast_fusion
  700.1 2.6 add_halves.15
  703.9 29.6 %input_back.1 = (bf16[2,5,8,4,8,1024]{5,4,3,2,1,0:T(8,128)(2,1)}, bf16[2,1,8,4,8,1024]{5,4,3,2,1,0:T(8,128)(2,1)}, bf16[2,1,8,4,8,1024]{5,4,3,2,1,0:T(8,128)(2,1...) custom-call(bf16[2,5,8,4,8,1024]{5,4,3,2,1,0:T(8,128)(2,1)} %bitcast.134, ...), custom_call_target="tpu_custom_call" | custom-call | flops 22040000069632 | bytes 28999999488 | tf_op jit(solution)/shard_map/input_back/pallas_call | solution.py:1304
  733.7 5.1 collective-permute-done.35
  738.8 4.1 add_halves.16
  748.4 2.2 add_halves.17
  756.7 10.8 %collective-permute-done.42 = bf16[1,5,128,256]{3,2,1,0:T(8,128)(2,1)S(1)} collective-permute-done((bf16[1,5,128,256]{3,2,1,0:T(8,128)(2,1)}, bf16[1,5,128,256]{3,2,1,0:T(8,128)(2,1)S(1)}, u32[]{:S(2)}, u32[]{:S(2)}) %collective-permute-start.42) | collective-permute-done | bytes 327712 | tf_op jit(solution)/shard_map/ppermute | solution.py:113
  767.5 2.3 constant_dynamic-update-slice_fusion.6
  769.7 2.3 constant_dynamic-update-slice_fusion.5
  776.1 2.3 constant_dynamic-update-slice_fusion.4
  778.4 2.2 add_halves.18
  784.1 9.4 %collective-permute-done.44 = f32[28068]{0:T(1024)S(1)} collective-permute-done((f32[28068]{0:T(1024)S(1)}, f32[28068]{0:T(1024)S(1)}, u32[]{:S(2)}, u32[]{:S(2)}) %collective-permute-start.44) | collective-permute-done | bytes 112304 | tf_op jit(solution)/shard_map/ppermute | solution.py:981
  793.6 2.3 constant_dynamic-update-slice_fusion.3
  796.7 1.9 add_halves.19
  799.9 2.3 constant_dynamic-update-slice_fusion.2
  804.9 11.7 %collective-permute-done.47 = f32[28068]{0:T(1024)S(1)} collective-permute-done((f32[28068]{0:T(1024)S(1)}, f32[28068]{0:T(1024)S(1)}, u32[]{:S(2)}, u32[]{:S(2)}) %collective-permute-start.47) | collective-permute-done | bytes 112304 | tf_op jit(solution)/shard_map/ppermute | solution.py:981
  (224 shorter events, 65.6 us)
Async XLA Ops:
  7.2 14.8 %copy-start.10 = (bf16[128,1024]{1,0:T(8,128)(2,1)S(1)}, bf16[128,1024]{1,0:T(8,128)(2,1)}, u32[]{:S(2)}) copy-start(bf16[128,1024]{1,0:T(8,128)(2,1)} %param.28) | copy-start | bytes 786436
  7.2 14.8 %copy-start.11 = (bf16[512,256]{1,0:T(8,128)(2,1)S(1)}, bf16[512,256]{1,0:T(8,128)(2,1)}, u32[]{:S(2)}) copy-start(bf16[512,256]{1,0:T(8,128)(2,1)} %param.29) | copy-start | bytes 786436
  7.2 107.1 %all-gather.5.cloned.1.call-start = ((), (), s32[]{:S(2)}) async-start(), calls=%async_computation | async-start | bytes 6488064 | tf_op jit(solution)/shard_map/all_gather | solution.py:1013
  7.9 249.8 %all-gather.7.cloned.1.call-start = ((), (), s32[]{:S(2)}) async-start(), calls=%async_computation.1 | async-start | bytes 17301504 | tf_op jit(solution)/shard_map/all_gather | solution.py:1042
  9.0 20.9 %collective-permute-start.1 = (bf16[1,128,1280]{2,1,0:T(8,128)(2,1)S(1)}, bf16[1,128,1280]{2,1,0:T(8,128)(2,1)S(1)}, u32[]{:S(2)}, u32[]{:S(2)}) collective-permute-start(bf16[1,128,1280]{2,1,0:T(8,128)(2,1)S(1)} %maximum_bitcast_fusion), channel_id=1, source_target_pairs={{0,8},{4,12},{8,0},{12,4},{16,24},{20,28},{24,16},{28,20},{1,9},{5... | collective-permute-start | bytes 983048 | tf_op jit(solution)/shard_map/ppermute | solution.py:113
  14.6 15.3 %collective-permute-start = (f32[1,28068]{1,0:T(1,128)S(1)}, f32[1,28068]{1,0:T(1,128)S(1)}, u32[]{:S(2)}, u32[]{:S(2)}) collective-permute-start(f32[1,28068]{1,0:T(1,128)S(1)} %broadcast_in_dim.38), channel_id=1, source_target_pairs={{0,2},{1,3},{2,0},{3,1},{4,6},{5,7},{6,4},{7,5},{8,10},{9,11},{10,... | collective-permute-start | bytes 336824 | tf_op jit(solution)/shard_map/ppermute | solution.py:947
  16.1 18.3 %copy-start.20 = (f32[2,6,1024]{2,0,1:T(2,128)S(1)}, f32[2,6,1024]{2,0,1:T(2,128)}, u32[]{:S(2)}) copy-start(f32[2,6,1024]{2,0,1:T(2,128)} %param.17) | copy-start | bytes 147460
  16.1 18.9 %copy-start.32 = (s32[2]{0:T(128)S(1)}, s32[2]{0:T(128)}, u32[]{:S(2)}) copy-start(s32[2]{0:T(128)} %param.19) | copy-start | bytes 28
  19.7 91.3 %collective-permute-start.10 = (bf16[2,1,8,4,8,1024]{5,4,3,2,1,0:T(8,128)(2,1)}, bf16[2,1,8,4,8,1024]{5,4,3,2,1,0:T(8,128)(2,1)}, u32[]{:S(2)}, u32[]{:S(2)}) collective-permute-start(bf16[2,1,8,4,8,1024]{5,4,3,2,1,0:T(8,128)(2,1)} %get-tuple-element.386), channel_id=1, source_target_pairs={{0,1},{1,2},{2,3},{3,0},{4,5},{5,6},{6,7},{7,4},{8,9},{9,10},{10,1... | collective-permute-start | bytes 3145736 | tf_op jit(solution)/shard_map/ppermute | solution.py:896
  19.7 92.8 %collective-permute-start.8 = (bf16[2,1,8,4,8,1024]{5,4,3,2,1,0:T(8,128)(2,1)}, bf16[2,1,8,4,8,1024]{5,4,3,2,1,0:T(8,128)(2,1)}, u32[]{:S(2)}, u32[]{:S(2)}) collective-permute-start(bf16[2,1,8,4,8,1024]{5,4,3,2,1,0:T(8,128)(2,1)} %get-tuple-element.388), channel_id=1, source_target_pairs={{0,3},{1,0},{2,1},{3,2},{4,7},{5,4},{6,5},{7,6},{8,11},{9,8},{10,9... | collective-permute-start | bytes 3145736 | tf_op jit(solution)/shard_map/ppermute | solution.py:896
  21.4 91.3 %collective-permute-start.9 = (bf16[2,1,8,4,8,1024]{5,4,3,2,1,0:T(8,128)(2,1)}, bf16[2,1,8,4,8,1024]{5,4,3,2,1,0:T(8,128)(2,1)}, u32[]{:S(2)}, u32[]{:S(2)}) collective-permute-start(bf16[2,1,8,4,8,1024]{5,4,3,2,1,0:T(8,128)(2,1)} %get-tuple-element.387), channel_id=1, source_target_pairs={{0,2},{1,3},{2,0},{3,1},{4,6},{5,7},{6,4},{7,5},{8,10},{9,11},{10,... | collective-permute-start | bytes 3145736 | tf_op jit(solution)/shard_map/ppermute | solution.py:896
  30.0 37.3 %collective-permute-start.3 = (bf16[2,128,1280]{2,1,0:T(8,128)(2,1)S(1)}, bf16[2,128,1280]{2,1,0:T(8,128)(2,1)S(1)}, u32[]{:S(2)}, u32[]{:S(2)}) collective-permute-start(bf16[2,128,1280]{2,1,0:T(8,128)(2,1)S(1)} %pad_maximum_fusion.4), channel_id=1, source_target_pairs={{0,16},{4,20},{8,24},{12,28},{16,0},{20,4},{24,8},{28,12},{1,17},{... | collective-permute-start | bytes 1966088 | tf_op jit(solution)/shard_map/ppermute | solution.py:113
  33.7 1.8 collective-permute-start.2
  35.0 53.7 %copy-start.29 = (pred[2]{0:T(512)(128)(4,1)}, pred[2]{0:T(512)(128)(4,1)S(1)}, u32[]{:S(2)}) copy-start(pred[2]{0:T(512)(128)(4,1)S(1)} %broadcast_compare_fusion) | copy-start | bytes 10
  71.0 19.5 %collective-permute-start.4 = (bf16[4,128,512]{2,1,0:T(8,128)(2,1)S(1)}, bf16[4,128,512]{2,1,0:T(8,128)(2,1)}, u32[]{:S(2)}, u32[]{:S(2)}) collective-permute-start(bf16[4,128,512]{2,1,0:T(8,128)(2,1)S(1)} %copy-done.1), channel_id=1, source_target_pairs={{0,4},{4,0},{8,12},{12,8},{16,20},{20,16},{24,28},{28,24},{1,5},{5... | collective-permute-start | bytes 1572872 | tf_op jit(solution)/shard_map/ppermute | solution.py:113
  72.5 30.6 %collective-permute-start.5 = (bf16[4,128,768]{2,1,0:T(8,128)(2,1)S(1)}, bf16[4,128,768]{2,1,0:T(8,128)(2,1)}, u32[]{:S(2)}, u32[]{:S(2)}) collective-permute-start(bf16[4,128,768]{2,1,0:T(8,128)(2,1)S(1)} %pad_maximum_fusion.2), channel_id=1, source_target_pairs={{0,2},{1,3},{2,0},{3,1},{4,6},{5,7},{6,4},{7,5},{8,10},{9,11},{10,... | collective-permute-start | bytes 2359304 | tf_op jit(solution)/shard_map/ppermute | solution.py:113
  105.6 34.6 %collective-permute-start.7 = (bf16[8,128,512]{2,1,0:T(8,128)(2,1)}, bf16[8,128,512]{2,1,0:T(8,128)(2,1)}, u32[]{:S(2)}, u32[]{:S(2)}) collective-permute-start(bf16[8,128,512]{2,1,0:T(8,128)(2,1)} %pad_maximum_fusion.1.refs_0_), channel_id=1, source_target_pairs={{0,2},{1,3},{2,0},{3,1},{4,6},{5,7},{6,4},{7,5},{8,10},{9,11},{10,... | collective-permute-start | bytes 3145736 | tf_op jit(solution)/shard_map/ppermute | solution.py:113
  106.1 89.5 %collective-permute-start.14 = (bf16[8,128,512]{2,1,0:T(8,128)(2,1)}, bf16[8,128,512]{2,1,0:T(8,128)(2,1)}, u32[]{:S(2)}, u32[]{:S(2)}) collective-permute-start(bf16[8,128,512]{2,1,0:T(8,128)(2,1)} %pad_maximum_fusion.1.refs_0_), channel_id=1, source_target_pairs={{0,1},{1,0},{2,3},{3,2},{4,5},{5,4},{6,7},{7,6},{8,9},{9,8},{10,11... | collective-permute-start | bytes 3145736 | tf_op jit(solution)/shard_map/ppermute | solution.py:113
  111.0 42.6 %collective-permute-start.6 = (bf16[8,128,768]{2,1,0:T(8,128)(2,1)}, bf16[8,128,768]{2,1,0:T(8,128)(2,1)}, u32[]{:S(2)}, u32[]{:S(2)}) collective-permute-start(bf16[8,128,768]{2,1,0:T(8,128)(2,1)} %pad_maximum_fusion.refs_9_.refs_11_), channel_id=1, source_target_pairs={{0,4},{4,0},{8,12},{12,8},{16,20},{20,16},{24,28},{28,24},{1,5},{5... | collective-permute-start | bytes 4718600 | tf_op jit(solution)/shard_map/ppermute | solution.py:113
  112.5 89.5 %collective-permute-start.16 = (bf16[8,128,768]{2,1,0:T(8,128)(2,1)}, bf16[8,128,768]{2,1,0:T(8,128)(2,1)}, u32[]{:S(2)}, u32[]{:S(2)}) collective-permute-start(bf16[8,128,768]{2,1,0:T(8,128)(2,1)} %pad_maximum_fusion.refs_9_.refs_11_), channel_id=1, source_target_pairs={{0,1},{1,0},{2,3},{3,2},{4,5},{5,4},{6,7},{7,6},{8,9},{9,8},{10,11... | collective-permute-start | bytes 4718600 | tf_op jit(solution)/shard_map/ppermute | solution.py:113
  140.2 55.9 %collective-permute-start.15 = (bf16[8,128,512]{2,1,0:T(8,128)(2,1)}, bf16[8,128,512]{2,1,0:T(8,128)(2,1)}, u32[]{:S(2)}, u32[]{:S(2)}) collective-permute-start(bf16[8,128,512]{2,1,0:T(8,128)(2,1)} %collective-permute-done.7.refs_1_), channel_id=1, source_target_pairs={{0,1},{1,0},{2,3},{3,2},{4,5},{5,4},{6,7},{7,6},{8,9},{9,8},{10,11... | collective-permute-start | bytes 3145736 | tf_op jit(solution)/shard_map/ppermute | solution.py:113
  190.3 11.6 %collective-permute-start.17 = (bf16[8,128,768]{2,1,0:T(8,128)(2,1)}, bf16[8,128,768]{2,1,0:T(8,128)(2,1)}, u32[]{:S(2)}, u32[]{:S(2)}) collective-permute-start(bf16[8,128,768]{2,1,0:T(8,128)(2,1)} %collective-permute-done.6.refs_10_.refs_12_), channel_id=1, source_target_pairs={{0,1},{1,0},{2,3},{3,2},{4,5},{5,4},{6,7},{7,6},{8,9},{9,8},{10,11... | collective-permute-start | bytes 4718600 | tf_op jit(solution)/shard_map/ppermute | solution.py:113
  194.0 49.0 %collective-permute-start.11 = (bf16[2,1,8,4,8,1024]{5,4,3,2,1,0:T(8,128)(2,1)}, bf16[2,1,8,4,8,1024]{5,4,3,2,1,0:T(8,128)(2,1)}, u32[]{:S(2)}, u32[]{:S(2)}) collective-permute-start(bf16[2,1,8,4,8,1024]{5,4,3,2,1,0:T(8,128)(2,1)} %get-tuple-element.385), channel_id=1, source_target_pairs={{0,3},{1,0},{2,1},{3,2},{4,7},{5,4},{6,5},{7,6},{8,11},{9,8},{10,9... | collective-permute-start | bytes 3145736 | tf_op jit(solution)/shard_map/ppermute | solution.py:896
  195.6 62.2 %collective-permute-start.12 = (bf16[2,1,8,4,8,1024]{5,4,3,2,1,0:T(8,128)(2,1)}, bf16[2,1,8,4,8,1024]{5,4,3,2,1,0:T(8,128)(2,1)}, u32[]{:S(2)}, u32[]{:S(2)}) collective-permute-start(bf16[2,1,8,4,8,1024]{5,4,3,2,1,0:T(8,128)(2,1)} %get-tuple-element.384), channel_id=1, source_target_pairs={{0,2},{1,3},{2,0},{3,1},{4,6},{5,7},{6,4},{7,5},{8,10},{9,11},{10,... | collective-permute-start | bytes 3145736 | tf_op jit(solution)/shard_map/ppermute | solution.py:896
  196.1 61.7 %collective-permute-start.13 = (bf16[2,1,8,4,8,1024]{5,4,3,2,1,0:T(8,128)(2,1)}, bf16[2,1,8,4,8,1024]{5,4,3,2,1,0:T(8,128)(2,1)}, u32[]{:S(2)}, u32[]{:S(2)}) collective-permute-start(bf16[2,1,8,4,8,1024]{5,4,3,2,1,0:T(8,128)(2,1)} %get-tuple-element.383), channel_id=1, source_target_pairs={{0,1},{1,2},{2,3},{3,0},{4,5},{5,6},{6,7},{7,4},{8,9},{9,10},{10,1... | collective-permute-start | bytes 3145736 | tf_op jit(solution)/shard_map/ppermute | solution.py:896
  393.7 18.3 %collective-permute-start.19 = (bf16[2,2,4,4,128,256]{5,4,3,2,1,0:T(8,128)(2,1)}, bf16[2,2,4,4,128,256]{5,4,3,2,1,0:T(8,128)(2,1)}, u32[]{:S(2)}, u32[]{:S(2)}) collective-permute-start(bf16[2,2,4,4,128,256]{5,4,3,2,1,0:T(8,128)(2,1)} %reduce_other.1), channel_id=1, source_target_pairs={{0,1},{1,0},{2,3},{3,2},{4,5},{5,4},{6,7},{7,6},{8,9},{9,8},{10,11... | collective-permute-start | bytes 12582920 | tf_op jit(solution)/shard_map/ppermute | solution.py:113
  411.5 19.8 %collective-permute-start.18 = (bf16[2,2,4,4,128,256]{5,4,3,2,1,0:T(8,128)(2,1)}, bf16[2,2,4,4,128,256]{5,4,3,2,1,0:T(8,128)(2,1)}, u32[]{:S(2)}, u32[]{:S(2)}) collective-permute-start(bf16[2,2,4,4,128,256]{5,4,3,2,1,0:T(8,128)(2,1)} %expand_other.1), channel_id=1, source_target_pairs={{0,1},{1,0},{2,3},{3,2},{4,5},{5,4},{6,7},{7,6},{8,9},{9,8},{10,11... | collective-permute-start | bytes 12582920 | tf_op jit(solution)/shard_map/ppermute | solution.py:113
  450.7 58.5 %collective-permute-start.21 = (bf16[1,2,4,4,128,256]{5,4,3,2,1,0:T(8,128)(2,1)}, bf16[1,2,4,4,128,256]{5,4,3,2,1,0:T(8,128)(2,1)}, u32[]{:S(2)}, u32[]{:S(2)}) collective-permute-start(bf16[1,2,4,4,128,256]{5,4,3,2,1,0:T(8,128)(2,1)} %get-tuple-element.222), channel_id=1, source_target_pairs={{0,4},{4,0},{8,12},{12,8},{16,20},{20,16},{24,28},{28,24},{1,5},{5... | collective-permute-start | bytes 6291464 | tf_op jit(solution)/shard_map/ppermute | solution.py:113
  452.2 57.1 %collective-permute-start.20 = (bf16[1,2,4,4,128,256]{5,4,3,2,1,0:T(8,128)(2,1)}, bf16[1,2,4,4,128,256]{5,4,3,2,1,0:T(8,128)(2,1)}, u32[]{:S(2)}, u32[]{:S(2)}) collective-permute-start(bf16[1,2,4,4,128,256]{5,4,3,2,1,0:T(8,128)(2,1)} %get-tuple-element.221), channel_id=1, source_target_pairs={{0,2},{1,3},{2,0},{3,1},{4,6},{5,7},{6,4},{7,5},{8,10},{9,11},{10,... | collective-permute-start | bytes 6291464 | tf_op jit(solution)/shard_map/ppermute | solution.py:113
  452.7 65.0 %copy-start.30 = (pred[2]{0:T(512)(128)(4,1)S(1)}, pred[2]{0:T(512)(128)(4,1)}, u32[]{:S(2)}) copy-start(pred[2]{0:T(512)(128)(4,1)} %copy-done.29) | copy-start | bytes 10
  543.0 9.4 %collective-permute-start.25 = (bf16[2,2,4,2,128,256]{5,4,3,2,1,0:T(8,128)(2,1)}, bf16[2,2,4,2,128,256]{5,4,3,2,1,0:T(8,128)(2,1)}, u32[]{:S(2)}, u32[]{:S(2)}) collective-permute-start(bf16[2,2,4,2,128,256]{5,4,3,2,1,0:T(8,128)(2,1)} %memory_other.1), channel_id=1, source_target_pairs={{0,1},{1,0},{2,3},{3,2},{4,5},{5,4},{6,7},{7,6},{8,9},{9,8},{10,11... | collective-permute-start | bytes 6291464 | tf_op jit(solution)/shard_map/ppermute | solution.py:113
  543.0 13.9 %collective-permute-start.24 = (bf16[2,2,4,3,128,256]{5,4,3,2,1,0:T(8,128)(2,1)}, bf16[2,2,4,3,128,256]{5,4,3,2,1,0:T(8,128)(2,1)}, u32[]{:S(2)}, u32[]{:S(2)}) collective-permute-start(bf16[2,2,4,3,128,256]{5,4,3,2,1,0:T(8,128)(2,1)} %square_other.1), channel_id=1, source_target_pairs={{0,1},{1,0},{2,3},{3,2},{4,5},{5,4},{6,7},{7,6},{8,9},{9,8},{10,11... | collective-permute-start | bytes 9437192 | tf_op jit(solution)/shard_map/ppermute | solution.py:113
  543.5 31.8 %collective-permute-start.22 = (bf16[1,4,4,128,256]{4,3,2,1,0:T(8,128)(2,1)}, bf16[1,4,4,128,256]{4,3,2,1,0:T(8,128)(2,1)}, u32[]{:S(2)}, u32[]{:S(2)}) collective-permute-start(bf16[1,4,4,128,256]{4,3,2,1,0:T(8,128)(2,1)} %bitcast.31), channel_id=1, source_target_pairs={{0,4},{4,0},{8,12},{12,8},{16,20},{20,16},{24,28},{28,24},{1,5},{5... | collective-permute-start | bytes 3145736 | tf_op jit(solution)/shard_map/ppermute | solution.py:113
  543.9 31.4 %collective-permute-start.23 = (bf16[1,4,4,128,256]{4,3,2,1,0:T(8,128)(2,1)}, bf16[1,4,4,128,256]{4,3,2,1,0:T(8,128)(2,1)}, u32[]{:S(2)}, u32[]{:S(2)}) collective-permute-start(bf16[1,4,4,128,256]{4,3,2,1,0:T(8,128)(2,1)} %bitcast.27), channel_id=1, source_target_pairs={{0,2},{1,3},{2,0},{3,1},{4,6},{5,7},{6,4},{7,5},{8,10},{9,11},{10,... | collective-permute-start | bytes 3145736 | tf_op jit(solution)/shard_map/ppermute | solution.py:113
  578.7 53.0 %collective-permute-start.27 = (bf16[2,8,128,256]{3,2,1,0:T(8,128)(2,1)}, bf16[2,8,128,256]{3,2,1,0:T(8,128)(2,1)}, u32[]{:S(2)}, u32[]{:S(2)}) collective-permute-start(bf16[2,8,128,256]{3,2,1,0:T(8,128)(2,1)} %get-tuple-element.273), channel_id=1, source_target_pairs={{0,8},{4,12},{8,0},{12,4},{16,24},{20,28},{24,16},{28,20},{1,9},{5... | collective-permute-start | bytes 3145736 | tf_op jit(solution)/shard_map/ppermute | solution.py:113
  580.1 58.3 %collective-permute-start.26 = (bf16[1,2,4,5,128,256]{5,4,3,2,1,0:T(8,128)(2,1)}, bf16[1,2,4,5,128,256]{5,4,3,2,1,0:T(8,128)(2,1)}, u32[]{:S(2)}, u32[]{:S(2)}) collective-permute-start(bf16[1,2,4,5,128,256]{5,4,3,2,1,0:T(8,128)(2,1)} %get-tuple-element.272), channel_id=1, source_target_pairs={{0,4},{4,0},{8,12},{12,8},{16,20},{20,16},{24,28},{28,24},{1,5},{5... | collective-permute-start | bytes 7864328 | tf_op jit(solution)/shard_map/ppermute | solution.py:113
  581.6 56.8 %collective-permute-start.28 = (bf16[2,1,8,4,8,1024]{5,4,3,2,1,0:T(8,128)(2,1)}, bf16[2,1,8,4,8,1024]{5,4,3,2,1,0:T(8,128)(2,1)}, u32[]{:S(2)}, u32[]{:S(2)}) collective-permute-start(bf16[2,1,8,4,8,1024]{5,4,3,2,1,0:T(8,128)(2,1)} %get-tuple-element.283), channel_id=1, source_target_pairs={{3,0},{0,1},{1,2},{2,3},{7,4},{4,5},{5,6},{6,7},{11,8},{8,9},{9,10... | collective-permute-start | bytes 3145736 | tf_op jit(solution)/shard_map/ppermute | solution.py:919
  581.6 56.8 %collective-permute-start.29 = (bf16[2,1,8,4,8,1024]{5,4,3,2,1,0:T(8,128)(2,1)}, bf16[2,1,8,4,8,1024]{5,4,3,2,1,0:T(8,128)(2,1)}, u32[]{:S(2)}, u32[]{:S(2)}) collective-permute-start(bf16[2,1,8,4,8,1024]{5,4,3,2,1,0:T(8,128)(2,1)} %get-tuple-element.284), channel_id=1, source_target_pairs={{2,0},{3,1},{0,2},{1,3},{6,4},{7,5},{4,6},{5,7},{10,8},{11,9},{8,1... | collective-permute-start | bytes 3145736 | tf_op jit(solution)/shard_map/ppermute | solution.py:919
  582.2 56.2 %collective-permute-start.30 = (bf16[2,1,8,4,8,1024]{5,4,3,2,1,0:T(8,128)(2,1)}, bf16[2,1,8,4,8,1024]{5,4,3,2,1,0:T(8,128)(2,1)}, u32[]{:S(2)}, u32[]{:S(2)}) collective-permute-start(bf16[2,1,8,4,8,1024]{5,4,3,2,1,0:T(8,128)(2,1)} %get-tuple-element.285), channel_id=1, source_target_pairs={{1,0},{2,1},{3,2},{0,3},{5,4},{6,5},{7,6},{4,7},{9,8},{10,9},{11,1... | collective-permute-start | bytes 3145736 | tf_op jit(solution)/shard_map/ppermute | solution.py:919
  643.0 15.6 %copy-start.28 = (f32[1,1024]{1,0:T(1,128)S(1)}, f32[1,1024]{1,0:T(1,128)}, u32[]{:S(2)}) copy-start(f32[1,1024]{1,0:T(1,128)} %get-tuple-element.323) | copy-start | bytes 12292
  643.0 16.9 %copy-start.8 = (f32[80,1024]{1,0:T(8,128)S(1)}, f32[80,1024]{1,0:T(8,128)}, u32[]{:S(2)}) copy-start(f32[80,1024]{1,0:T(8,128)} %null_text.1) | copy-start | bytes 983044
  658.2 5.9 collective-permute-start.33
  660.8 31.3 %collective-permute-start.32 = (bf16[1,8,128,256]{3,2,1,0:T(8,128)(2,1)}, bf16[1,8,128,256]{3,2,1,0:T(8,128)(2,1)}, u32[]{:S(2)}, u32[]{:S(2)}) collective-permute-start(bf16[1,8,128,256]{3,2,1,0:T(8,128)(2,1)} %get-tuple-element.296), channel_id=1, source_target_pairs={{0,16},{4,20},{8,24},{12,28},{16,0},{20,4},{24,8},{28,12},{1,17},{... | collective-permute-start | bytes 1572872 | tf_op jit(solution)/shard_map/ppermute | solution.py:113
  663.2 31.2 %collective-permute-start.31 = (bf16[1,4,5,128,256]{4,3,2,1,0:T(8,128)(2,1)}, bf16[1,4,5,128,256]{4,3,2,1,0:T(8,128)(2,1)}, u32[]{:S(2)}, u32[]{:S(2)}) collective-permute-start(bf16[1,4,5,128,256]{4,3,2,1,0:T(8,128)(2,1)} %bitcast.162), channel_id=1, source_target_pairs={{0,2},{1,3},{2,0},{3,1},{4,6},{5,7},{6,4},{7,5},{8,10},{9,11},{10,... | collective-permute-start | bytes 3932168 | tf_op jit(solution)/shard_map/ppermute | solution.py:113
  702.7 36.0 %collective-permute-start.35 = (bf16[1,2,4,3,128,256]{5,4,3,2,1,0:T(8,128)(2,1)}, bf16[1,2,4,3,128,256]{5,4,3,2,1,0:T(8,128)(2,1)}, u32[]{:S(2)}, u32[]{:S(2)}) collective-permute-start(bf16[1,2,4,3,128,256]{5,4,3,2,1,0:T(8,128)(2,1)} %get-tuple-element.311), channel_id=1, source_target_pairs={{0,2},{1,3},{2,0},{3,1},{4,6},{5,7},{6,4},{7,5},{8,10},{9,11},{10,... | collective-permute-start | bytes 4718600 | tf_op jit(solution)/shard_map/ppermute | solution.py:113
  703.3 39.6 %collective-permute-start.34 = (bf16[2,5,128,256]{3,2,1,0:T(8,128)(2,1)}, bf16[2,5,128,256]{3,2,1,0:T(8,128)(2,1)}, u32[]{:S(2)}, u32[]{:S(2)}) collective-permute-start(bf16[2,5,128,256]{3,2,1,0:T(8,128)(2,1)} %get-tuple-element.309), channel_id=1, source_target_pairs={{0,8},{4,12},{8,0},{12,4},{16,24},{20,28},{24,16},{28,20},{1,9},{5... | collective-permute-start | bytes 1966088 | tf_op jit(solution)/shard_map/ppermute | solution.py:113
  703.8 29.7 %copy-start.5 = (f32[16,2025]{1,0:T(8,128)S(1)}, f32[16,2025]{1,0:T(8,128)}, u32[]{:S(2)}) copy-start(f32[16,2025]{1,0:T(8,128)} %reshape.338) | copy-start | bytes 388804
  703.8 39.1 %copy-start.21 = (f32[2,3,1024]{2,1,0:T(4,128)S(1)}, f32[2,3,1024]{2,1,0:T(4,128)}, u32[]{:S(2)}) copy-start(f32[2,3,1024]{2,1,0:T(4,128)} %get-tuple-element.322) | copy-start | bytes 73732
  703.8 39.1 %copy-start.27 = (f32[2,1,1024]{2,1,0:T(1,128)S(1)}, f32[2,1,1024]{2,1,0:T(1,128)}, u32[]{:S(2)}) copy-start(f32[2,1,1024]{2,1,0:T(1,128)} %get-tuple-element.321) | copy-start | bytes 24580
  703.8 39.9 %copy-start.2 = (f32[77,4,256]{2,1,0:T(4,128)S(1)}, f32[77,4,256]{2,1,0:T(4,128)}, u32[]{:S(2)}) copy-start(f32[77,4,256]{2,1,0:T(4,128)} %concatenate.57) | copy-start | bytes 946180
  703.8 39.9 %copy-start.26 = (f32[1,4,256]{2,1,0:T(4,128)S(1)}, f32[1,4,256]{2,1,0:T(4,128)}, u32[]{:S(2)}) copy-start(f32[1,4,256]{2,1,0:T(4,128)} %concatenate.56) | copy-start | bytes 12292
  703.8 43.7 %copy-start = (f32[8,128,256]{2,1,0:T(8,128)S(1)}, f32[8,128,256]{2,1,0:T(8,128)}, u32[]{:S(2)}) copy-start(f32[8,128,256]{2,1,0:T(8,128)} %add_bitcast_fusion) | copy-start | bytes 3145732
  744.0 9.0 %collective-permute-start.36 = (f32[2,31140]{1,0:T(2,128)S(1)}, f32[2,31140]{1,0:T(2,128)S(1)}, u32[]{:S(2)}, u32[]{:S(2)}) collective-permute-start(f32[2,31140]{1,0:T(2,128)S(1)} %broadcast_select_fusion), channel_id=1, source_target_pairs={{0,2},{1,3},{2,0},{3,1},{4,6},{5,7},{6,4},{7,5},{8,10},{9,11},{10,... | collective-permute-start | bytes 747368 | tf_op jit(solution)/shard_map/ppermute | solution.py:973
  744.6 48.8 %collective-permute-start.38 = (bf16[2,1,8,4,8,1024]{5,4,3,2,1,0:T(8,128)(2,1)}, bf16[2,1,8,4,8,1024]{5,4,3,2,1,0:T(8,128)(2,1)}, u32[]{:S(2)}, u32[]{:S(2)}) collective-permute-start(bf16[2,1,8,4,8,1024]{5,4,3,2,1,0:T(8,128)(2,1)} %get-tuple-element.331), channel_id=1, source_target_pairs={{3,0},{0,1},{1,2},{2,3},{7,4},{4,5},{5,6},{6,7},{11,8},{8,9},{9,10... | collective-permute-start | bytes 3145736 | tf_op jit(solution)/shard_map/ppermute | solution.py:919
  744.6 48.8 %collective-permute-start.39 = (bf16[2,1,8,4,8,1024]{5,4,3,2,1,0:T(8,128)(2,1)}, bf16[2,1,8,4,8,1024]{5,4,3,2,1,0:T(8,128)(2,1)}, u32[]{:S(2)}, u32[]{:S(2)}) collective-permute-start(bf16[2,1,8,4,8,1024]{5,4,3,2,1,0:T(8,128)(2,1)} %get-tuple-element.332), channel_id=1, source_target_pairs={{2,0},{3,1},{0,2},{1,3},{6,4},{7,5},{4,6},{5,7},{10,8},{11,9},{8,1... | collective-permute-start | bytes 3145736 | tf_op jit(solution)/shard_map/ppermute | solution.py:919
  746.1 47.5 %collective-permute-start.40 = (bf16[2,1,8,4,8,1024]{5,4,3,2,1,0:T(8,128)(2,1)}, bf16[2,1,8,4,8,1024]{5,4,3,2,1,0:T(8,128)(2,1)S(1)}, u32[]{:S(2)}, u32[]{:S(2)}) collective-permute-start(bf16[2,1,8,4,8,1024]{5,4,3,2,1,0:T(8,128)(2,1)} %get-tuple-element.333), channel_id=1, source_target_pairs={{1,0},{2,1},{3,2},{0,3},{5,4},{6,5},{7,6},{4,7},{9,8},{10,9},{11,1... | collective-permute-start | bytes 3145736 | tf_op jit(solution)/shard_map/ppermute | solution.py:919
  750.7 16.8 %collective-permute-start.42 = (bf16[1,5,128,256]{3,2,1,0:T(8,128)(2,1)}, bf16[1,5,128,256]{3,2,1,0:T(8,128)(2,1)S(1)}, u32[]{:S(2)}, u32[]{:S(2)}) collective-permute-start(bf16[1,5,128,256]{3,2,1,0:T(8,128)(2,1)} %get-tuple-element.337), channel_id=1, source_target_pairs={{0,16},{4,20},{8,24},{12,28},{16,0},{20,4},{24,8},{28,12},{1,17},{... | collective-permute-start | bytes 983048 | tf_op jit(solution)/shard_map/ppermute | solution.py:113
  753.4 1.4 collective-permute-start.37
  754.8 19.8 %collective-permute-start.41 = (bf16[1,4,3,128,256]{4,3,2,1,0:T(8,128)(2,1)}, bf16[1,4,3,128,256]{4,3,2,1,0:T(8,128)(2,1)S(1)}, u32[]{:S(2)}, u32[]{:S(2)}) collective-permute-start(bf16[1,4,3,128,256]{4,3,2,1,0:T(8,128)(2,1)} %bitcast.163), channel_id=1, source_target_pairs={{0,4},{4,0},{8,12},{12,8},{16,20},{20,16},{24,28},{28,24},{1,5},{5... | collective-permute-start | bytes 2359304 | tf_op jit(solution)/shard_map/ppermute | solution.py:113
  774.6 6.5 collective-permute-start.43
  780.6 15.3 %collective-permute-start.45 = (bf16[2,3,128,256]{3,2,1,0:T(8,128)(2,1)}, bf16[2,3,128,256]{3,2,1,0:T(8,128)(2,1)S(1)}, u32[]{:S(2)}, u32[]{:S(2)}) collective-permute-start(bf16[2,3,128,256]{3,2,1,0:T(8,128)(2,1)} %get-tuple-element.347), channel_id=1, source_target_pairs={{0,8},{4,12},{8,0},{12,4},{16,24},{20,28},{24,16},{28,20},{1,9},{5... | collective-permute-start | bytes 1179656 | tf_op jit(solution)/shard_map/ppermute | solution.py:113
  781.2 12.3 %collective-permute-start.44 = (f32[28068]{0:T(1024)S(1)}, f32[28068]{0:T(1024)S(1)}, u32[]{:S(2)}, u32[]{:S(2)}) collective-permute-start(f32[28068]{0:T(1024)S(1)} %slice_add_fusion), channel_id=1, source_target_pairs={{0,8},{4,12},{8,0},{12,4},{16,24},{20,28},{24,16},{28,20},{1,9},{5... | collective-permute-start | bytes 336824 | tf_op jit(solution)/shard_map/ppermute | solution.py:981
  798.6 19.9 %collective-permute-start.46 = (bf16[1,3,128,256]{3,2,1,0:T(8,128)(2,1)}, bf16[1,3,128,256]{3,2,1,0:T(8,128)(2,1)S(1)}, u32[]{:S(2)}, u32[]{:S(2)}) collective-permute-start(bf16[1,3,128,256]{3,2,1,0:T(8,128)(2,1)} %get-tuple-element.351), channel_id=1, source_target_pairs={{0,16},{4,20},{8,24},{12,28},{16,0},{20,4},{24,8},{28,12},{1,17},{... | collective-permute-start | bytes 589832 | tf_op jit(solution)/shard_map/ppermute | solution.py:113
  802.1 14.4 %collective-permute-start.47 = (f32[28068]{0:T(1024)S(1)}, f32[28068]{0:T(1024)S(1)}, u32[]{:S(2)}, u32[]{:S(2)}) collective-permute-start(f32[28068]{0:T(1024)S(1)} %add.150), channel_id=1, source_target_pairs={{0,16},{4,20},{8,24},{12,28},{16,0},{20,4},{24,8},{28,12},{1,17},{... | collective-permute-start | bytes 336824 | tf_op jit(solution)/shard_map/ppermute | solution.py:981
  (19 other events, 142.4 us)
Sparse Core Ops, SparseCore 0:
  10.9 103.3 all-gather.4
  117.7 131.2 all-gather.6

commit v3 on v2

--- a/solution.py
+++ b/solution.py
@@ -145,8 +145,14 @@
         return at["z"] * self.size["y"] + at["y"], at["x"] * 2 + core
 
     def reduce(self, terms, axes, apart, pin):
+        came, pin = self.exchange(terms, axes, apart, pin)
+        return self.combine(terms, came), pin
+
+    def exchange(self, terms, axes, apart, pin):
         came = [self.swap(term.sent, axis, n) for term, axis, n in zip(terms, axes, apart)]
-        came, pin = tie(came, pin)
+        return tie(came, pin)
+
+    def combine(self, terms, came):
         pairs = []
         for term, part in zip(terms, came):
             kept, lead = term.kept, term.lead
@@ -155,8 +161,8 @@
             pairs.append((kept, part))
         if lead == 0:
             sums = [kept.astype(single) + part.astype(single) for kept, part in pairs]
-            return jnp.concatenate(sums, axis=0), pin
-        return Term(*add_halves(pairs), lead), pin
+            return jnp.concatenate(sums, axis=0)
+        return Term(*add_halves(pairs), lead)
 
     def reduce_axes(self, terms, axes, pin):
         terms = list(terms)
@@ -1315,7 +1321,7 @@
     first_mod = input_out[-1]
     input_stage, first_mod = layout.reduce_axes([input_term], ["x"], first_mod)
     input_stage, first_mod = tie(input_stage, first_mod)
-    rest_stage, first_mod = layout.reduce([rest_stage], ["z"], [1], first_mod)
+    rest_came, first_mod = layout.exchange([rest_stage], ["z"], [1], first_mod)
     expand_grad = jnp.concatenate(list(feed_grad[:4]), axis=1)
     reduce_grad = feed_grad[4:].reshape(4 * depth, columns)
     heads_local = HEADS // win_count
@@ -1334,21 +1340,24 @@
     small_term = sum_over_win(small_term, layout)
     block_whole, block_came, small_term = tie(block_pieces[0], block_came, small_term)
     block_output = put_together(block_whole, block_came, win_count)
-    for bit in range(1, layout.bits("z")):
-        rest_stage, small_term = layout.reduce([rest_stage], ["z"], [1 << bit], small_term)
-    cross_memory_grad = jnp.concatenate([rest_stage[0], rest_stage[1]], axis=1)
+    rest_came, small_term = tie(rest_came, small_term)
+    rest_stage = layout.combine([rest_stage], rest_came)
     input_stage, small_term = layout.reduce_axes([input_stage], ["y"], small_term)
     modulation_grad = small_term[: clips * 6 * columns].reshape(clips, 6, columns)
     small_grad = sum_over_clip(small_term[clips * 6 * columns :], layout, 1, clip_size // 2)
+    for bit in range(1, layout.bits("z")):
+        rest_stage, small_grad = layout.reduce([rest_stage], ["z"], [1 << bit], small_grad)
+    input_stage, small_grad = layout.reduce([input_stage], ["z"], [1], small_grad)
+    input_stage, small_grad = tie(input_stage, small_grad)
     tokens_came, small_grad = send_back(input_out[1 : 1 + sent], win_count, small_grad)
     tokens_grad = put_together(input_out[0], tokens_came, win_count)
-    input_stage, small_grad = layout.reduce([input_stage], ["z"], [1], small_grad)
     small_grad = sum_over_clip(small_grad, layout, clip_size // 2, clip_size)
     gain_grad = small_grad[:columns]
     null_grad = small_grad[columns : (1 + TXT) * columns].reshape(TXT, columns)
     position_grad = small_grad[(1 + TXT) * columns :].reshape(heads_local, NREL)
     for bit in range(1, layout.bits("z")):
         input_stage, small_grad = layout.reduce([input_stage], ["z"], [1 << bit], small_grad)
+    cross_memory_grad = jnp.concatenate([rest_stage[0], rest_stage[1]], axis=1)
     self_input_grad = jnp.concatenate(list(input_stage), axis=1)
     self_output_grad, cross_query_grad, cross_output_grad = rest_stage[2:]
     return (

time: 839 us -> 832 us (level)
    ppermute x3, waiting for transfers between devices: 21 us -> 5.97 us  [sum_over_clip(): values = values + lax.ppermute(values, 'clip', pairs)]
  transfers between devices with their start and end apart: 50 -> 50, of which waited for: 18 -> 19; matrix products, arithmetic and copies ran while one was open for 9% -> 9% of each run, Pallas kernels for 42% -> 43%
where the time goes in v3:
time: 832 us; the launch traced here: 820 us
  Pallas kernels  562 us (68%)
  waiting for transfers between devices  112 us (13%)
  local copies, waits for them, and re-layouts  51.9 us (6%)
  starting transfers between devices  43 us (5%)
  other arithmetic  29.5 us (4%)
  between operations  15.4 us (2%)
    pallas_call x1, Pallas kernels, local(): pl.pallas_call(functools.partial(feed_kernel, layout, wins, 1024, sent),...  118 us
    pallas_call x8, Pallas kernels, weight_grad(): pl.pallas_call(functools.partial(columns_kernel, layout, pieces, pair, x_...  113 us
    ppermute x29, waiting for transfers between devices, swap(): return lax.ppermute(values, home, [(i, i ^ step) for i in range(count)])  83 us
    pallas_call x1, Pallas kernels, local(): pl.pallas_call(functools.partial(cross_back_kernel, layout, wins), grid=(...  56.5 us
    pallas_call x1, Pallas kernels, local(): pl.pallas_call(attend_back_kernel, grid=(windows,), in_specs=[rows_spec(3...  48 us
    pallas_call x1, Pallas kernels, local(): pl.pallas_call(functools.partial(cross_kernel, layout), grid=(windows,),...  41 us
    pallas_call x2, Pallas kernels, weight_grad_rows(): pl.pallas_call(functools.partial(rows_kernel, layout, pair), grid_spec=pl...  37.3 us
    pallas_call x1, Pallas kernels, local(): pl.pallas_call(attend_kernel, grid=(windows,), in_specs=[rows_spec(3 * wi...  36.8 us
  transfers between devices with their start and end apart: 50, of which 19 were waited for; matrix products, arithmetic and copies ran while one was open for 9% of the time, Pallas kernels for 43%

profile of v3, /device:TPU:0, one launch (start us, length us, event | category | flops | bytes accessed | tf_op | source)
XLA Modules:
  0.0 820.4 jit_solution(9918269538830394846)
XLA Ops:
  9.0 3.1 collective-permute-start.1
  16.1 3.6 fusion.65
  23.0 6.8 fusion.4
  30.0 2.7 collective-permute-start.3
  35.5 31.8 %collective-permute-done.3 = bf16[2,128,1280]{2,1,0:T(8,128)(2,1)S(1)} collective-permute-done((bf16[2,128,1280]{2,1,0:T(8,128)(2,1)S(1)}, bf16[2,128,1280]{2,1,0:T(8,128)(2,1)S(1)}, u32[]{:S(2)}, u32[]{:S(2)}) %collective-permute-start.3) | collective-permute-done | bytes 655392 | tf_op jit(solution)/shard_map/ppermute | solution.py:113
  72.9 3.6 convolution_bitcast_fusion
  76.6 5.9 copy.49
  82.5 6.0 reshape.316.block_ref
  90.5 2.1 pad_maximum_fusion.1.refs_0_
  92.6 10.5 %collective-permute-done.5 = bf16[4,128,768]{2,1,0:T(8,128)(2,1)} collective-permute-done((bf16[4,128,768]{2,1,0:T(8,128)(2,1)S(1)}, bf16[4,128,768]{2,1,0:T(8,128)(2,1)}, u32[]{:S(2)}, u32[]{:S(2)}) %collective-permute-start.5) | collective-permute-done | bytes 786464 | tf_op jit(solution)/shard_map/ppermute | solution.py:113
  103.1 2.5 pad_maximum_fusion.refs_9_.refs_11_
  106.1 4.9 bias_table.1.bias_ref
  114.3 25.9 %project.1 = (bf16[8,320,1024]{2,1,0:T(8,128)(2,1)}, bf16[8,320,3072]{2,1,0:T(8,128)(2,1)}) custom-call(bf16[2,5,8,4,8,1024]{5,4,3,2,1,0:T(8,128)(2,1)} %bitcast.128, bf16[2,5,8,4,8,1024]{5,4,3,2,1,0:T(8,128)(2,1)} %bitcast.129, bf16[2,1,8,4,8,1024]{5,4,3,2,1,0:T(8,128)(2,1)} %collective-permute-done.8.refs_2_, ...), custom_call_target="tpu_custom_call" | custom-call | flops 19759999483904 | bytes 25999998976 | tf_op jit(solution)/shard_map/project/pallas_call | solution.py:1063
  140.5 13.1 %collective-permute-done.6.refs_10_.refs_12_ = bf16[8,128,768]{2,1,0:T(8,128)(2,1)} collective-permute-done((bf16[8,128,768]{2,1,0:T(8,128)(2,1)}, bf16[8,128,768]{2,1,0:T(8,128)(2,1)}, u32[]{:S(2)}, u32[]{:S(2)}) %collective-permute-start.6) | collective-permute-done | bytes 1572896 | tf_op jit(solution)/shard_map/ppermute | solution.py:113
  153.6 36.8 %attend.1 = (bf16[8,320,1024]{2,1,0:T(8,128)(2,1)}, bf16[8,4,320,1280]{3,2,1,0:T(8,128)(2,1)}) custom-call(bf16[8,320,3072]{2,1,0:T(8,128)(2,1)} %get-tuple-element.208.projected_ref, f32[4,320,1280]{2,1,0:T(8,128)} %bias_table.1.bias_ref), custom_call_target="tpu_custom_call" | custom-call | flops 28120000233472 | bytes 36999999488 | tf_op jit(solution)/shard_map/attend/pallas_call | solution.py:1079
  190.3 3.6 fusion.64
  196.1 5.8 memory.1.refs_8_.refs_7_
  201.9 41.0 %cross.1 = (f32[8,320,1024]{2,1,0:T(8,128)}, bf16[3,8,320,1024]{3,2,1,0:T(8,128)(2,1)}, bf16[8,320,1024]{2,1,0:T(8,128)(2,1)}, f32[8,320,1024]{2,1,0:T(8,128)}) custom-call(s32[4]{0:T(128)} %pad_add_fusion.place_ref, bf16[2,5,8,4,8,1024]{5,4,3,2,1,0:T(8,128)(2,1)} %bitcast.130, bf16[2,5,8,4,8,1024]{5,4,3,2,1,0:T(8,128)(2,1)} %bitcast.131, ...), custom_call_target="tpu_custom_call" | custom-call | flops 31919999811584 | bytes 41999998976 | tf_op jit(solution)/shard_map/cross/pallas_call | solution.py:1113
  243.0 14.8 %collective-permute-done.12.refs_3_ = bf16[2,1,8,4,8,1024]{5,4,3,2,1,0:T(8,128)(2,1)} collective-permute-done((bf16[2,1,8,4,8,1024]{5,4,3,2,1,0:T(8,128)(2,1)}, bf16[2,1,8,4,8,1024]{5,4,3,2,1,0:T(8,128)(2,1)}, u32[]{:S(2)}, u32[]{:S(2)}) %collective-permute-start.12) | collective-permute-done | bytes 1048608 | tf_op jit(solution)/shard_map/ppermute | solution.py:902
  257.8 117.8 %feed.1 = (bf16[2,5,8,4,8,1024]{5,4,3,2,1,0:T(8,128)(2,1)}, bf16[2,1,8,4,8,1024]{5,4,3,2,1,0:T(8,128)(2,1)}, bf16[2,1,8,4,8,1024]{5,4,3,2,1,0:T(8,128)(2,1)}, bf...) custom-call(bf16[2,5,8,4,8,1024]{5,4,3,2,1,0:T(8,128)(2,1)} %bitcast, ...), custom_call_target="tpu_custom_call" | custom-call | flops 88919999774720 | bytes 117000003584 | tf_op jit(solution)/shard_map/feed/pallas_call | solution.py:1148
  375.6 18.1 %reduce_other.1 = bf16[2,2,4,4,128,256]{5,4,3,2,1,0:T(8,128)(2,1)} custom-call(s32[4]{0:T(128)} %pad_add_fusion.place_ref, bf16[2560,4096]{1,0:T(8,128)(2,1)} %bitcast.166, bf16[2560,1024]{1,0:T(8,128)(2,1)} %bitcast.182, bf16[2560,1024]{1,0:T(8,128)(2,1)} %bitcast.183), custom_call_target="tpu_custom_call" | custom-call | flops 10681201413062656 | bytes 14054211977216 | tf_op jit(solution)/shard_map/reduce_other/pallas_call | solution.py:876
  393.7 17.8 %expand_other.1 = bf16[2,2,4,4,128,256]{5,4,3,2,1,0:T(8,128)(2,1)} custom-call(s32[4]{0:T(128)} %pad_add_fusion.place_ref, bf16[1,2560,1024]{2,1,0:T(8,128)(2,1)} %bitcast.180, bf16[1,2560,4096]{2,1,0:T(8,128)(2,1)} %bitcast.164), custom_call_target="tpu_custom_call" | custom-call | flops 10681201413062656 | bytes 14054211977216 | tf_op jit(solution)/shard_map/expand_other/pallas_call | solution.py:805
  412.0 19.3 %reduce_own.1 = (bf16[1,2,4,4,128,256]{5,4,3,2,1,0:T(8,128)(2,1)}, bf16[1,2,4,4,128,256]{5,4,3,2,1,0:T(8,128)(2,1)}) custom-call(s32[4]{0:T(128)} %pad_add_fusion.place_ref, bf16[2560,4096]{1,0:T(8,128)(2,1)} %bitcast.167, bf16[2560,1024]{1,0:T(8,128)(2,1)} %bitcast.184, bf16[2560,1024]{1,0:T(8,128)(2,1)} %bitcast.185, ...), custom_call_target="tpu_custom_call" | custom-call | flops 10681201413062656 | bytes 14054211977216 | tf_op jit(solution)/shard_map/reduce_own/pallas_call | solution.py:876
  431.3 19.4 %expand_own.1 = (bf16[1,2,4,4,128,256]{5,4,3,2,1,0:T(8,128)(2,1)}, bf16[1,2,4,4,128,256]{5,4,3,2,1,0:T(8,128)(2,1)}) custom-call(s32[4]{0:T(128)} %pad_add_fusion.place_ref, bf16[1,2560,1024]{2,1,0:T(8,128)(2,1)} %bitcast.181, bf16[1,2560,4096]{2,1,0:T(8,128)(2,1)} %bitcast.165, bf16[2,2,4,4,128,256]{5,4,3,2,1,0:T(8,128)(2,1)} %collective-permute-done.18.refs_1_), custom_call_target="tpu_custom_call" | custom-call | flops 10681201413062656 | bytes 14054211977216 | tf_op jit(solution)/shard_map/expand_own/pallas_call | solution.py:805
  452.7 56.5 %cross_back.1 = (bf16[3,4,8,320,256]{4,3,2,1,0:T(8,128)(2,1)}, f32[8,320,1024]{2,1,0:T(8,128)}, bf16[8,320,1024]{2,1,0:T(8,128)(2,1)}, f32[2,80,2048]{2,1,0:T(8,...) custom-call(s32[4]{0:T(128)} %pad_add_fusion.place_ref, bf16[2,5,8,4,8,1024]{5,4,3,2,1,0:T(8,128)(2,1)} %bitcast.132, ...), custom_call_target="tpu_custom_call" | custom-call | flops 47880001814528 | bytes 62999998464 | tf_op jit(solution)/shard_map/cross_back/pallas_call | solution.py:1198
  509.3 4.3 add_halves.11
  513.6 4.2 add_halves.10
  517.8 3.6 fusion.66
  521.4 17.7 %square_other.1 = bf16[2,2,4,3,128,256]{5,4,3,2,1,0:T(8,128)(2,1)} custom-call(s32[4]{0:T(128)} %pad_add_fusion.place_ref, bf16[3,2560,1024]{2,1,0:T(8,128)(2,1)} %bitcast.168, bf16[3,4,2560,256]{3,2,1,0:T(8,128)(2,1)} %bitcast.176), custom_call_target="tpu_custom_call" | custom-call | flops 8010901059796992 | bytes 10540659245056 | tf_op jit(solution)/shard_map/square_other/pallas_call | solution.py:805
  539.1 3.9 memory_other.1
  545.6 6.9 null_text.1
  552.5 4.5 memory_own.1
  557.0 18.3 %square_own.1 = (bf16[1,2,4,5,128,256]{5,4,3,2,1,0:T(8,128)(2,1)}, bf16[1,2,4,5,128,256]{5,4,3,2,1,0:T(8,128)(2,1)}) custom-call(s32[4]{0:T(128)} %pad_add_fusion.place_ref, bf16[3,2560,1024]{2,1,0:T(8,128)(2,1)} %bitcast.169, bf16[3,4,2560,256]{3,2,1,0:T(8,128)(2,1)} %bitcast.177, ...), custom_call_target="tpu_custom_call", output_to_operand_aliasing={{0}: (4, {}), {1}: (5, {})} | custom-call | flops 8010901059796992 | bytes 10540659245056 | tf_op jit(solution)/shard_map/square_own/pallas_call | solution.py:805
  575.3 3.4 add_halves.12
  583.6 48.0 %attend_back.1 = (bf16[3,4,8,320,256]{4,3,2,1,0:T(8,128)(2,1)}, f32[4,320,1280]{2,1,0:T(8,128)}) custom-call(bf16[8,320,3072]{2,1,0:T(8,128)(2,1)} %get-tuple-element.208.projected_ref, bf16[8,320,1024]{2,1,0:T(8,128)(2,1)} %get-tuple-element.273.grad_ref, bf16[8,4,320,1280]{3,2,1,0:T(8,128)(2,1)} %get-tuple-element.274.probs_ref), custom_call_target="tpu_custom_call" | custom-call | flops 36480000983040 | bytes 48000000000 | tf_op jit(solution)/shard_map/attend_back/pallas_call | solution.py:1275
  631.6 2.6 add_halves.14
  634.3 4.1 collective-permute-done.26
  638.4 4.6 add_halves.13
  643.0 15.1 %input_other.1 = bf16[2,2,4,3,128,256]{5,4,3,2,1,0:T(8,128)(2,1)} custom-call(s32[4]{0:T(128)} %pad_add_fusion.place_ref, bf16[1,2560,1024]{2,1,0:T(8,128)(2,1)} %bitcast.178, bf16[3,4,2560,256]{3,2,1,0:T(8,128)(2,1)} %bitcast.170, bf16[3,4,2560,256]{3,2,1,0:T(8,128)(2,1)} %bitcast.171, bf16[3,4,2560,256]{3,2,1,0:T(8,128)(2,1)} %bitcast.172), custom_call_target="tpu_custom_call" | custom-call | flops 8010901059796992 | bytes 10540659245056 | tf_op jit(solution)/shard_map/input_other/pallas_call | solution.py:805
  660.8 2.4 collective-permute-start.32
  665.7 16.4 %input_own.1 = (bf16[1,2,4,3,128,256]{5,4,3,2,1,0:T(8,128)(2,1)}, bf16[1,2,4,3,128,256]{5,4,3,2,1,0:T(8,128)(2,1)}) custom-call(s32[4]{0:T(128)} %pad_add_fusion.place_ref, bf16[1,2560,1024]{2,1,0:T(8,128)(2,1)} %bitcast.179, bf16[3,4,2560,256]{3,2,1,0:T(8,128)(2,1)} %bitcast.173, bf16[3,4,2560,256]{3,2,1,0:T(8,128)(2,1)} %bitcast.174, ...), custom_call_target="tpu_custom_call" | custom-call | flops 8010901059796992 | bytes 10540659245056 | tf_op jit(solution)/shard_map/input_own/pallas_call | solution.py:805
  682.1 6.1 bias_collect.1
  688.2 3.9 reshape.337
  692.1 2.3 collective-permute-done.31
  694.5 2.7 fusion.30
  698.0 2.1 add_bitcast_fusion
  700.1 2.6 add_halves.15
  703.9 29.6 %input_back.1 = (bf16[2,5,8,4,8,1024]{5,4,3,2,1,0:T(8,128)(2,1)}, bf16[2,1,8,4,8,1024]{5,4,3,2,1,0:T(8,128)(2,1)}, bf16[2,1,8,4,8,1024]{5,4,3,2,1,0:T(8,128)(2,1...) custom-call(bf16[2,5,8,4,8,1024]{5,4,3,2,1,0:T(8,128)(2,1)} %bitcast.134, ...), custom_call_target="tpu_custom_call" | custom-call | flops 22040000069632 | bytes 28999999488 | tf_op jit(solution)/shard_map/input_back/pallas_call | solution.py:1310
  733.7 5.1 collective-permute-done.35
  738.8 4.1 add_halves.16
  750.0 3.1 collective-permute-done.36
  755.2 2.2 add_halves.18
  758.3 2.3 constant_dynamic-update-slice_fusion.6
  760.6 6.6 collective-permute-done.41
  768.8 2.3 constant_dynamic-update-slice_fusion.5
  772.7 2.3 constant_dynamic-update-slice_fusion.4
  775.6 2.2 add_halves.17
  781.9 6.7 collective-permute-done.42
  789.4 1.9 add_halves.19
  791.3 2.3 collective-permute-done.40
  797.6 2.3 constant_dynamic-update-slice_fusion.2
  799.9 2.3 constant_dynamic-update-slice_fusion.1
  802.2 4.9 collective-permute-done.47
  809.1 2.2 collective-permute-done.46
  (224 shorter events, 69.5 us)
Async XLA Ops:
  7.2 14.8 %copy-start.10 = (bf16[128,1024]{1,0:T(8,128)(2,1)S(1)}, bf16[128,1024]{1,0:T(8,128)(2,1)}, u32[]{:S(2)}) copy-start(bf16[128,1024]{1,0:T(8,128)(2,1)} %param.28) | copy-start | bytes 786436
  7.2 14.8 %copy-start.11 = (bf16[512,256]{1,0:T(8,128)(2,1)S(1)}, bf16[512,256]{1,0:T(8,128)(2,1)}, u32[]{:S(2)}) copy-start(bf16[512,256]{1,0:T(8,128)(2,1)} %param.29) | copy-start | bytes 786436
  7.2 107.1 %all-gather.5.cloned.1.call-start = ((), (), s32[]{:S(2)}) async-start(), calls=%async_computation | async-start | bytes 6488064 | tf_op jit(solution)/shard_map/all_gather | solution.py:1019
  7.9 249.8 %all-gather.7.cloned.1.call-start = ((), (), s32[]{:S(2)}) async-start(), calls=%async_computation.1 | async-start | bytes 17301504 | tf_op jit(solution)/shard_map/all_gather | solution.py:1048
  9.0 20.9 %collective-permute-start.1 = (bf16[1,128,1280]{2,1,0:T(8,128)(2,1)S(1)}, bf16[1,128,1280]{2,1,0:T(8,128)(2,1)S(1)}, u32[]{:S(2)}, u32[]{:S(2)}) collective-permute-start(bf16[1,128,1280]{2,1,0:T(8,128)(2,1)S(1)} %maximum_bitcast_fusion), channel_id=1, source_target_pairs={{0,8},{4,12},{8,0},{12,4},{16,24},{20,28},{24,16},{28,20},{1,9},{5... | collective-permute-start | bytes 983048 | tf_op jit(solution)/shard_map/ppermute | solution.py:113
  14.6 15.3 %collective-permute-start = (f32[1,28068]{1,0:T(1,128)S(1)}, f32[1,28068]{1,0:T(1,128)S(1)}, u32[]{:S(2)}, u32[]{:S(2)}) collective-permute-start(f32[1,28068]{1,0:T(1,128)S(1)} %broadcast_in_dim.38), channel_id=1, source_target_pairs={{0,2},{1,3},{2,0},{3,1},{4,6},{5,7},{6,4},{7,5},{8,10},{9,11},{10,... | collective-permute-start | bytes 336824 | tf_op jit(solution)/shard_map/ppermute | solution.py:953
  16.1 18.3 %copy-start.20 = (f32[2,6,1024]{2,0,1:T(2,128)S(1)}, f32[2,6,1024]{2,0,1:T(2,128)}, u32[]{:S(2)}) copy-start(f32[2,6,1024]{2,0,1:T(2,128)} %param.17) | copy-start | bytes 147460
  16.1 18.9 %copy-start.32 = (s32[2]{0:T(128)S(1)}, s32[2]{0:T(128)}, u32[]{:S(2)}) copy-start(s32[2]{0:T(128)} %param.19) | copy-start | bytes 28
  19.7 91.3 %collective-permute-start.10 = (bf16[2,1,8,4,8,1024]{5,4,3,2,1,0:T(8,128)(2,1)}, bf16[2,1,8,4,8,1024]{5,4,3,2,1,0:T(8,128)(2,1)}, u32[]{:S(2)}, u32[]{:S(2)}) collective-permute-start(bf16[2,1,8,4,8,1024]{5,4,3,2,1,0:T(8,128)(2,1)} %get-tuple-element.396), channel_id=1, source_target_pairs={{0,1},{1,2},{2,3},{3,0},{4,5},{5,6},{6,7},{7,4},{8,9},{9,10},{10,1... | collective-permute-start | bytes 3145736 | tf_op jit(solution)/shard_map/ppermute | solution.py:902
  19.7 92.8 %collective-permute-start.8 = (bf16[2,1,8,4,8,1024]{5,4,3,2,1,0:T(8,128)(2,1)}, bf16[2,1,8,4,8,1024]{5,4,3,2,1,0:T(8,128)(2,1)}, u32[]{:S(2)}, u32[]{:S(2)}) collective-permute-start(bf16[2,1,8,4,8,1024]{5,4,3,2,1,0:T(8,128)(2,1)} %get-tuple-element.398), channel_id=1, source_target_pairs={{0,3},{1,0},{2,1},{3,2},{4,7},{5,4},{6,5},{7,6},{8,11},{9,8},{10,9... | collective-permute-start | bytes 3145736 | tf_op jit(solution)/shard_map/ppermute | solution.py:902
  21.4 91.3 %collective-permute-start.9 = (bf16[2,1,8,4,8,1024]{5,4,3,2,1,0:T(8,128)(2,1)}, bf16[2,1,8,4,8,1024]{5,4,3,2,1,0:T(8,128)(2,1)}, u32[]{:S(2)}, u32[]{:S(2)}) collective-permute-start(bf16[2,1,8,4,8,1024]{5,4,3,2,1,0:T(8,128)(2,1)} %get-tuple-element.397), channel_id=1, source_target_pairs={{0,2},{1,3},{2,0},{3,1},{4,6},{5,7},{6,4},{7,5},{8,10},{9,11},{10,... | collective-permute-start | bytes 3145736 | tf_op jit(solution)/shard_map/ppermute | solution.py:902
  30.0 37.3 %collective-permute-start.3 = (bf16[2,128,1280]{2,1,0:T(8,128)(2,1)S(1)}, bf16[2,128,1280]{2,1,0:T(8,128)(2,1)S(1)}, u32[]{:S(2)}, u32[]{:S(2)}) collective-permute-start(bf16[2,128,1280]{2,1,0:T(8,128)(2,1)S(1)} %pad_maximum_fusion.4), channel_id=1, source_target_pairs={{0,16},{4,20},{8,24},{12,28},{16,0},{20,4},{24,8},{28,12},{1,17},{... | collective-permute-start | bytes 1966088 | tf_op jit(solution)/shard_map/ppermute | solution.py:113
  33.7 1.8 collective-permute-start.2
  35.0 53.7 %copy-start.29 = (pred[2]{0:T(512)(128)(4,1)}, pred[2]{0:T(512)(128)(4,1)S(1)}, u32[]{:S(2)}) copy-start(pred[2]{0:T(512)(128)(4,1)S(1)} %broadcast_compare_fusion) | copy-start | bytes 10
  71.0 19.5 %collective-permute-start.4 = (bf16[4,128,512]{2,1,0:T(8,128)(2,1)S(1)}, bf16[4,128,512]{2,1,0:T(8,128)(2,1)}, u32[]{:S(2)}, u32[]{:S(2)}) collective-permute-start(bf16[4,128,512]{2,1,0:T(8,128)(2,1)S(1)} %copy-done.1), channel_id=1, source_target_pairs={{0,4},{4,0},{8,12},{12,8},{16,20},{20,16},{24,28},{28,24},{1,5},{5... | collective-permute-start | bytes 1572872 | tf_op jit(solution)/shard_map/ppermute | solution.py:113
  72.5 30.6 %collective-permute-start.5 = (bf16[4,128,768]{2,1,0:T(8,128)(2,1)S(1)}, bf16[4,128,768]{2,1,0:T(8,128)(2,1)}, u32[]{:S(2)}, u32[]{:S(2)}) collective-permute-start(bf16[4,128,768]{2,1,0:T(8,128)(2,1)S(1)} %pad_maximum_fusion.2), channel_id=1, source_target_pairs={{0,2},{1,3},{2,0},{3,1},{4,6},{5,7},{6,4},{7,5},{8,10},{9,11},{10,... | collective-permute-start | bytes 2359304 | tf_op jit(solution)/shard_map/ppermute | solution.py:113
  105.6 34.6 %collective-permute-start.7 = (bf16[8,128,512]{2,1,0:T(8,128)(2,1)}, bf16[8,128,512]{2,1,0:T(8,128)(2,1)}, u32[]{:S(2)}, u32[]{:S(2)}) collective-permute-start(bf16[8,128,512]{2,1,0:T(8,128)(2,1)} %pad_maximum_fusion.1.refs_0_), channel_id=1, source_target_pairs={{0,2},{1,3},{2,0},{3,1},{4,6},{5,7},{6,4},{7,5},{8,10},{9,11},{10,... | collective-permute-start | bytes 3145736 | tf_op jit(solution)/shard_map/ppermute | solution.py:113
  106.1 89.5 %collective-permute-start.14 = (bf16[8,128,512]{2,1,0:T(8,128)(2,1)}, bf16[8,128,512]{2,1,0:T(8,128)(2,1)}, u32[]{:S(2)}, u32[]{:S(2)}) collective-permute-start(bf16[8,128,512]{2,1,0:T(8,128)(2,1)} %pad_maximum_fusion.1.refs_0_), channel_id=1, source_target_pairs={{0,1},{1,0},{2,3},{3,2},{4,5},{5,4},{6,7},{7,6},{8,9},{9,8},{10,11... | collective-permute-start | bytes 3145736 | tf_op jit(solution)/shard_map/ppermute | solution.py:113
  111.0 42.6 %collective-permute-start.6 = (bf16[8,128,768]{2,1,0:T(8,128)(2,1)}, bf16[8,128,768]{2,1,0:T(8,128)(2,1)}, u32[]{:S(2)}, u32[]{:S(2)}) collective-permute-start(bf16[8,128,768]{2,1,0:T(8,128)(2,1)} %pad_maximum_fusion.refs_9_.refs_11_), channel_id=1, source_target_pairs={{0,4},{4,0},{8,12},{12,8},{16,20},{20,16},{24,28},{28,24},{1,5},{5... | collective-permute-start | bytes 4718600 | tf_op jit(solution)/shard_map/ppermute | solution.py:113
  112.5 89.5 %collective-permute-start.16 = (bf16[8,128,768]{2,1,0:T(8,128)(2,1)}, bf16[8,128,768]{2,1,0:T(8,128)(2,1)}, u32[]{:S(2)}, u32[]{:S(2)}) collective-permute-start(bf16[8,128,768]{2,1,0:T(8,128)(2,1)} %pad_maximum_fusion.refs_9_.refs_11_), channel_id=1, source_target_pairs={{0,1},{1,0},{2,3},{3,2},{4,5},{5,4},{6,7},{7,6},{8,9},{9,8},{10,11... | collective-permute-start | bytes 4718600 | tf_op jit(solution)/shard_map/ppermute | solution.py:113
  140.2 55.9 %collective-permute-start.15 = (bf16[8,128,512]{2,1,0:T(8,128)(2,1)}, bf16[8,128,512]{2,1,0:T(8,128)(2,1)}, u32[]{:S(2)}, u32[]{:S(2)}) collective-permute-start(bf16[8,128,512]{2,1,0:T(8,128)(2,1)} %collective-permute-done.7.refs_1_), channel_id=1, source_target_pairs={{0,1},{1,0},{2,3},{3,2},{4,5},{5,4},{6,7},{7,6},{8,9},{9,8},{10,11... | collective-permute-start | bytes 3145736 | tf_op jit(solution)/shard_map/ppermute | solution.py:113
  190.3 11.6 %collective-permute-start.17 = (bf16[8,128,768]{2,1,0:T(8,128)(2,1)}, bf16[8,128,768]{2,1,0:T(8,128)(2,1)}, u32[]{:S(2)}, u32[]{:S(2)}) collective-permute-start(bf16[8,128,768]{2,1,0:T(8,128)(2,1)} %collective-permute-done.6.refs_10_.refs_12_), channel_id=1, source_target_pairs={{0,1},{1,0},{2,3},{3,2},{4,5},{5,4},{6,7},{7,6},{8,9},{9,8},{10,11... | collective-permute-start | bytes 4718600 | tf_op jit(solution)/shard_map/ppermute | solution.py:113
  194.0 49.0 %collective-permute-start.11 = (bf16[2,1,8,4,8,1024]{5,4,3,2,1,0:T(8,128)(2,1)}, bf16[2,1,8,4,8,1024]{5,4,3,2,1,0:T(8,128)(2,1)}, u32[]{:S(2)}, u32[]{:S(2)}) collective-permute-start(bf16[2,1,8,4,8,1024]{5,4,3,2,1,0:T(8,128)(2,1)} %get-tuple-element.395), channel_id=1, source_target_pairs={{0,3},{1,0},{2,1},{3,2},{4,7},{5,4},{6,5},{7,6},{8,11},{9,8},{10,9... | collective-permute-start | bytes 3145736 | tf_op jit(solution)/shard_map/ppermute | solution.py:902
  195.6 62.2 %collective-permute-start.12 = (bf16[2,1,8,4,8,1024]{5,4,3,2,1,0:T(8,128)(2,1)}, bf16[2,1,8,4,8,1024]{5,4,3,2,1,0:T(8,128)(2,1)}, u32[]{:S(2)}, u32[]{:S(2)}) collective-permute-start(bf16[2,1,8,4,8,1024]{5,4,3,2,1,0:T(8,128)(2,1)} %get-tuple-element.394), channel_id=1, source_target_pairs={{0,2},{1,3},{2,0},{3,1},{4,6},{5,7},{6,4},{7,5},{8,10},{9,11},{10,... | collective-permute-start | bytes 3145736 | tf_op jit(solution)/shard_map/ppermute | solution.py:902
  196.1 61.7 %collective-permute-start.13 = (bf16[2,1,8,4,8,1024]{5,4,3,2,1,0:T(8,128)(2,1)}, bf16[2,1,8,4,8,1024]{5,4,3,2,1,0:T(8,128)(2,1)}, u32[]{:S(2)}, u32[]{:S(2)}) collective-permute-start(bf16[2,1,8,4,8,1024]{5,4,3,2,1,0:T(8,128)(2,1)} %get-tuple-element.393), channel_id=1, source_target_pairs={{0,1},{1,2},{2,3},{3,0},{4,5},{5,6},{6,7},{7,4},{8,9},{9,10},{10,1... | collective-permute-start | bytes 3145736 | tf_op jit(solution)/shard_map/ppermute | solution.py:902
  393.7 18.3 %collective-permute-start.19 = (bf16[2,2,4,4,128,256]{5,4,3,2,1,0:T(8,128)(2,1)}, bf16[2,2,4,4,128,256]{5,4,3,2,1,0:T(8,128)(2,1)}, u32[]{:S(2)}, u32[]{:S(2)}) collective-permute-start(bf16[2,2,4,4,128,256]{5,4,3,2,1,0:T(8,128)(2,1)} %reduce_other.1), channel_id=1, source_target_pairs={{0,1},{1,0},{2,3},{3,2},{4,5},{5,4},{6,7},{7,6},{8,9},{9,8},{10,11... | collective-permute-start | bytes 12582920 | tf_op jit(solution)/shard_map/ppermute | solution.py:113
  411.5 19.8 %collective-permute-start.18 = (bf16[2,2,4,4,128,256]{5,4,3,2,1,0:T(8,128)(2,1)}, bf16[2,2,4,4,128,256]{5,4,3,2,1,0:T(8,128)(2,1)}, u32[]{:S(2)}, u32[]{:S(2)}) collective-permute-start(bf16[2,2,4,4,128,256]{5,4,3,2,1,0:T(8,128)(2,1)} %expand_other.1), channel_id=1, source_target_pairs={{0,1},{1,0},{2,3},{3,2},{4,5},{5,4},{6,7},{7,6},{8,9},{9,8},{10,11... | collective-permute-start | bytes 12582920 | tf_op jit(solution)/shard_map/ppermute | solution.py:113
  450.7 58.5 %collective-permute-start.21 = (bf16[1,2,4,4,128,256]{5,4,3,2,1,0:T(8,128)(2,1)}, bf16[1,2,4,4,128,256]{5,4,3,2,1,0:T(8,128)(2,1)}, u32[]{:S(2)}, u32[]{:S(2)}) collective-permute-start(bf16[1,2,4,4,128,256]{5,4,3,2,1,0:T(8,128)(2,1)} %get-tuple-element.227), channel_id=1, source_target_pairs={{0,4},{4,0},{8,12},{12,8},{16,20},{20,16},{24,28},{28,24},{1,5},{5... | collective-permute-start | bytes 6291464 | tf_op jit(solution)/shard_map/ppermute | solution.py:113
  452.2 57.1 %collective-permute-start.20 = (bf16[1,2,4,4,128,256]{5,4,3,2,1,0:T(8,128)(2,1)}, bf16[1,2,4,4,128,256]{5,4,3,2,1,0:T(8,128)(2,1)}, u32[]{:S(2)}, u32[]{:S(2)}) collective-permute-start(bf16[1,2,4,4,128,256]{5,4,3,2,1,0:T(8,128)(2,1)} %get-tuple-element.226), channel_id=1, source_target_pairs={{0,2},{1,3},{2,0},{3,1},{4,6},{5,7},{6,4},{7,5},{8,10},{9,11},{10,... | collective-permute-start | bytes 6291464 | tf_op jit(solution)/shard_map/ppermute | solution.py:113
  452.7 65.0 %copy-start.30 = (pred[2]{0:T(512)(128)(4,1)S(1)}, pred[2]{0:T(512)(128)(4,1)}, u32[]{:S(2)}) copy-start(pred[2]{0:T(512)(128)(4,1)} %copy-done.29) | copy-start | bytes 10
  543.0 9.4 %collective-permute-start.25 = (bf16[2,2,4,2,128,256]{5,4,3,2,1,0:T(8,128)(2,1)}, bf16[2,2,4,2,128,256]{5,4,3,2,1,0:T(8,128)(2,1)}, u32[]{:S(2)}, u32[]{:S(2)}) collective-permute-start(bf16[2,2,4,2,128,256]{5,4,3,2,1,0:T(8,128)(2,1)} %memory_other.1), channel_id=1, source_target_pairs={{0,1},{1,0},{2,3},{3,2},{4,5},{5,4},{6,7},{7,6},{8,9},{9,8},{10,11... | collective-permute-start | bytes 6291464 | tf_op jit(solution)/shard_map/ppermute | solution.py:113
  543.0 13.9 %collective-permute-start.24 = (bf16[2,2,4,3,128,256]{5,4,3,2,1,0:T(8,128)(2,1)}, bf16[2,2,4,3,128,256]{5,4,3,2,1,0:T(8,128)(2,1)}, u32[]{:S(2)}, u32[]{:S(2)}) collective-permute-start(bf16[2,2,4,3,128,256]{5,4,3,2,1,0:T(8,128)(2,1)} %square_other.1), channel_id=1, source_target_pairs={{0,1},{1,0},{2,3},{3,2},{4,5},{5,4},{6,7},{7,6},{8,9},{9,8},{10,11... | collective-permute-start | bytes 9437192 | tf_op jit(solution)/shard_map/ppermute | solution.py:113
  543.5 31.8 %collective-permute-start.22 = (bf16[1,4,4,128,256]{4,3,2,1,0:T(8,128)(2,1)}, bf16[1,4,4,128,256]{4,3,2,1,0:T(8,128)(2,1)}, u32[]{:S(2)}, u32[]{:S(2)}) collective-permute-start(bf16[1,4,4,128,256]{4,3,2,1,0:T(8,128)(2,1)} %bitcast.31), channel_id=1, source_target_pairs={{0,4},{4,0},{8,12},{12,8},{16,20},{20,16},{24,28},{28,24},{1,5},{5... | collective-permute-start | bytes 3145736 | tf_op jit(solution)/shard_map/ppermute | solution.py:113
  543.9 31.4 %collective-permute-start.23 = (bf16[1,4,4,128,256]{4,3,2,1,0:T(8,128)(2,1)}, bf16[1,4,4,128,256]{4,3,2,1,0:T(8,128)(2,1)}, u32[]{:S(2)}, u32[]{:S(2)}) collective-permute-start(bf16[1,4,4,128,256]{4,3,2,1,0:T(8,128)(2,1)} %bitcast.27), channel_id=1, source_target_pairs={{0,2},{1,3},{2,0},{3,1},{4,6},{5,7},{6,4},{7,5},{8,10},{9,11},{10,... | collective-permute-start | bytes 3145736 | tf_op jit(solution)/shard_map/ppermute | solution.py:113
  578.7 53.0 %collective-permute-start.27 = (bf16[2,8,128,256]{3,2,1,0:T(8,128)(2,1)}, bf16[2,8,128,256]{3,2,1,0:T(8,128)(2,1)}, u32[]{:S(2)}, u32[]{:S(2)}) collective-permute-start(bf16[2,8,128,256]{3,2,1,0:T(8,128)(2,1)} %get-tuple-element.278), channel_id=1, source_target_pairs={{0,8},{4,12},{8,0},{12,4},{16,24},{20,28},{24,16},{28,20},{1,9},{5... | collective-permute-start | bytes 3145736 | tf_op jit(solution)/shard_map/ppermute | solution.py:113
  580.1 58.3 %collective-permute-start.26 = (bf16[1,2,4,5,128,256]{5,4,3,2,1,0:T(8,128)(2,1)}, bf16[1,2,4,5,128,256]{5,4,3,2,1,0:T(8,128)(2,1)}, u32[]{:S(2)}, u32[]{:S(2)}) collective-permute-start(bf16[1,2,4,5,128,256]{5,4,3,2,1,0:T(8,128)(2,1)} %get-tuple-element.277), channel_id=1, source_target_pairs={{0,4},{4,0},{8,12},{12,8},{16,20},{20,16},{24,28},{28,24},{1,5},{5... | collective-permute-start | bytes 7864328 | tf_op jit(solution)/shard_map/ppermute | solution.py:113
  581.6 56.8 %collective-permute-start.28 = (bf16[2,1,8,4,8,1024]{5,4,3,2,1,0:T(8,128)(2,1)}, bf16[2,1,8,4,8,1024]{5,4,3,2,1,0:T(8,128)(2,1)}, u32[]{:S(2)}, u32[]{:S(2)}) collective-permute-start(bf16[2,1,8,4,8,1024]{5,4,3,2,1,0:T(8,128)(2,1)} %get-tuple-element.288), channel_id=1, source_target_pairs={{3,0},{0,1},{1,2},{2,3},{7,4},{4,5},{5,6},{6,7},{11,8},{8,9},{9,10... | collective-permute-start | bytes 3145736 | tf_op jit(solution)/shard_map/ppermute | solution.py:925
  581.6 56.8 %collective-permute-start.29 = (bf16[2,1,8,4,8,1024]{5,4,3,2,1,0:T(8,128)(2,1)}, bf16[2,1,8,4,8,1024]{5,4,3,2,1,0:T(8,128)(2,1)}, u32[]{:S(2)}, u32[]{:S(2)}) collective-permute-start(bf16[2,1,8,4,8,1024]{5,4,3,2,1,0:T(8,128)(2,1)} %get-tuple-element.289), channel_id=1, source_target_pairs={{2,0},{3,1},{0,2},{1,3},{6,4},{7,5},{4,6},{5,7},{10,8},{11,9},{8,1... | collective-permute-start | bytes 3145736 | tf_op jit(solution)/shard_map/ppermute | solution.py:925
  582.2 56.2 %collective-permute-start.30 = (bf16[2,1,8,4,8,1024]{5,4,3,2,1,0:T(8,128)(2,1)}, bf16[2,1,8,4,8,1024]{5,4,3,2,1,0:T(8,128)(2,1)}, u32[]{:S(2)}, u32[]{:S(2)}) collective-permute-start(bf16[2,1,8,4,8,1024]{5,4,3,2,1,0:T(8,128)(2,1)} %get-tuple-element.290), channel_id=1, source_target_pairs={{1,0},{2,1},{3,2},{0,3},{5,4},{6,5},{7,6},{4,7},{9,8},{10,9},{11,1... | collective-permute-start | bytes 3145736 | tf_op jit(solution)/shard_map/ppermute | solution.py:925
  643.0 15.6 %copy-start.28 = (f32[1,1024]{1,0:T(1,128)S(1)}, f32[1,1024]{1,0:T(1,128)}, u32[]{:S(2)}) copy-start(f32[1,1024]{1,0:T(1,128)} %get-tuple-element.328) | copy-start | bytes 12292
  643.0 16.9 %copy-start.8 = (f32[80,1024]{1,0:T(8,128)S(1)}, f32[80,1024]{1,0:T(8,128)}, u32[]{:S(2)}) copy-start(f32[80,1024]{1,0:T(8,128)} %null_text.1) | copy-start | bytes 983044
  658.2 5.9 collective-permute-start.33
  660.8 31.3 %collective-permute-start.32 = (bf16[1,8,128,256]{3,2,1,0:T(8,128)(2,1)}, bf16[1,8,128,256]{3,2,1,0:T(8,128)(2,1)}, u32[]{:S(2)}, u32[]{:S(2)}) collective-permute-start(bf16[1,8,128,256]{3,2,1,0:T(8,128)(2,1)} %get-tuple-element.301), channel_id=1, source_target_pairs={{0,16},{4,20},{8,24},{12,28},{16,0},{20,4},{24,8},{28,12},{1,17},{... | collective-permute-start | bytes 1572872 | tf_op jit(solution)/shard_map/ppermute | solution.py:113
  663.2 31.2 %collective-permute-start.31 = (bf16[1,4,5,128,256]{4,3,2,1,0:T(8,128)(2,1)}, bf16[1,4,5,128,256]{4,3,2,1,0:T(8,128)(2,1)}, u32[]{:S(2)}, u32[]{:S(2)}) collective-permute-start(bf16[1,4,5,128,256]{4,3,2,1,0:T(8,128)(2,1)} %bitcast.162), channel_id=1, source_target_pairs={{0,2},{1,3},{2,0},{3,1},{4,6},{5,7},{6,4},{7,5},{8,10},{9,11},{10,... | collective-permute-start | bytes 3932168 | tf_op jit(solution)/shard_map/ppermute | solution.py:113
  702.7 36.0 %collective-permute-start.35 = (bf16[1,2,4,3,128,256]{5,4,3,2,1,0:T(8,128)(2,1)}, bf16[1,2,4,3,128,256]{5,4,3,2,1,0:T(8,128)(2,1)}, u32[]{:S(2)}, u32[]{:S(2)}) collective-permute-start(bf16[1,2,4,3,128,256]{5,4,3,2,1,0:T(8,128)(2,1)} %get-tuple-element.316), channel_id=1, source_target_pairs={{0,2},{1,3},{2,0},{3,1},{4,6},{5,7},{6,4},{7,5},{8,10},{9,11},{10,... | collective-permute-start | bytes 4718600 | tf_op jit(solution)/shard_map/ppermute | solution.py:113
  703.3 39.6 %collective-permute-start.34 = (bf16[2,5,128,256]{3,2,1,0:T(8,128)(2,1)}, bf16[2,5,128,256]{3,2,1,0:T(8,128)(2,1)}, u32[]{:S(2)}, u32[]{:S(2)}) collective-permute-start(bf16[2,5,128,256]{3,2,1,0:T(8,128)(2,1)} %get-tuple-element.314), channel_id=1, source_target_pairs={{0,8},{4,12},{8,0},{12,4},{16,24},{20,28},{24,16},{28,20},{1,9},{5... | collective-permute-start | bytes 1966088 | tf_op jit(solution)/shard_map/ppermute | solution.py:113
  703.8 29.7 %copy-start.5 = (f32[16,2025]{1,0:T(8,128)S(1)}, f32[16,2025]{1,0:T(8,128)}, u32[]{:S(2)}) copy-start(f32[16,2025]{1,0:T(8,128)} %reshape.338) | copy-start | bytes 388804
  703.8 39.1 %copy-start.21 = (f32[2,3,1024]{2,1,0:T(4,128)S(1)}, f32[2,3,1024]{2,1,0:T(4,128)}, u32[]{:S(2)}) copy-start(f32[2,3,1024]{2,1,0:T(4,128)} %get-tuple-element.327) | copy-start | bytes 73732
  703.8 39.1 %copy-start.27 = (f32[2,1,1024]{2,1,0:T(1,128)S(1)}, f32[2,1,1024]{2,1,0:T(1,128)}, u32[]{:S(2)}) copy-start(f32[2,1,1024]{2,1,0:T(1,128)} %get-tuple-element.326) | copy-start | bytes 24580
  703.8 39.9 %copy-start.2 = (f32[77,4,256]{2,1,0:T(4,128)S(1)}, f32[77,4,256]{2,1,0:T(4,128)}, u32[]{:S(2)}) copy-start(f32[77,4,256]{2,1,0:T(4,128)} %concatenate.57) | copy-start | bytes 946180
  703.8 39.9 %copy-start.26 = (f32[1,4,256]{2,1,0:T(4,128)S(1)}, f32[1,4,256]{2,1,0:T(4,128)}, u32[]{:S(2)}) copy-start(f32[1,4,256]{2,1,0:T(4,128)} %concatenate.56) | copy-start | bytes 12292
  703.8 43.7 %copy-start = (f32[8,128,256]{2,1,0:T(8,128)S(1)}, f32[8,128,256]{2,1,0:T(8,128)}, u32[]{:S(2)}) copy-start(f32[8,128,256]{2,1,0:T(8,128)} %add_bitcast_fusion) | copy-start | bytes 3145732
  744.0 9.0 %collective-permute-start.36 = (f32[2,31140]{1,0:T(2,128)S(1)}, f32[2,31140]{1,0:T(2,128)S(1)}, u32[]{:S(2)}, u32[]{:S(2)}) collective-permute-start(f32[2,31140]{1,0:T(2,128)S(1)} %broadcast_select_fusion), channel_id=1, source_target_pairs={{0,2},{1,3},{2,0},{3,1},{4,6},{5,7},{6,4},{7,5},{8,10},{9,11},{10,... | collective-permute-start | bytes 747368 | tf_op jit(solution)/shard_map/ppermute | solution.py:979
  744.6 46.7 %collective-permute-start.38 = (bf16[2,1,8,4,8,1024]{5,4,3,2,1,0:T(8,128)(2,1)}, bf16[2,1,8,4,8,1024]{5,4,3,2,1,0:T(8,128)(2,1)S(1)}, u32[]{:S(2)}, u32[]{:S(2)}) collective-permute-start(bf16[2,1,8,4,8,1024]{5,4,3,2,1,0:T(8,128)(2,1)} %get-tuple-element.336), channel_id=1, source_target_pairs={{3,0},{0,1},{1,2},{2,3},{7,4},{4,5},{5,6},{6,7},{11,8},{8,9},{9,10... | collective-permute-start | bytes 3145736 | tf_op jit(solution)/shard_map/ppermute | solution.py:925
  744.6 46.7 %collective-permute-start.39 = (bf16[2,1,8,4,8,1024]{5,4,3,2,1,0:T(8,128)(2,1)}, bf16[2,1,8,4,8,1024]{5,4,3,2,1,0:T(8,128)(2,1)}, u32[]{:S(2)}, u32[]{:S(2)}) collective-permute-start(bf16[2,1,8,4,8,1024]{5,4,3,2,1,0:T(8,128)(2,1)} %get-tuple-element.337), channel_id=1, source_target_pairs={{2,0},{3,1},{0,2},{1,3},{6,4},{7,5},{4,6},{5,7},{10,8},{11,9},{8,1... | collective-permute-start | bytes 3145736 | tf_op jit(solution)/shard_map/ppermute | solution.py:925
  746.1 47.5 %collective-permute-start.40 = (bf16[2,1,8,4,8,1024]{5,4,3,2,1,0:T(8,128)(2,1)}, bf16[2,1,8,4,8,1024]{5,4,3,2,1,0:T(8,128)(2,1)}, u32[]{:S(2)}, u32[]{:S(2)}) collective-permute-start(bf16[2,1,8,4,8,1024]{5,4,3,2,1,0:T(8,128)(2,1)} %get-tuple-element.338), channel_id=1, source_target_pairs={{1,0},{2,1},{3,2},{0,3},{5,4},{6,5},{7,6},{4,7},{9,8},{10,9},{11,1... | collective-permute-start | bytes 3145736 | tf_op jit(solution)/shard_map/ppermute | solution.py:925
  748.4 18.8 %collective-permute-start.41 = (bf16[1,4,3,128,256]{4,3,2,1,0:T(8,128)(2,1)}, bf16[1,4,3,128,256]{4,3,2,1,0:T(8,128)(2,1)S(1)}, u32[]{:S(2)}, u32[]{:S(2)}) collective-permute-start(bf16[1,4,3,128,256]{4,3,2,1,0:T(8,128)(2,1)} %bitcast.163), channel_id=1, source_target_pairs={{0,4},{4,0},{8,12},{12,8},{16,20},{20,16},{24,28},{28,24},{1,5},{5... | collective-permute-start | bytes 2359304 | tf_op jit(solution)/shard_map/ppermute | solution.py:113
  753.4 1.4 collective-permute-start.37
  757.5 21.9 %collective-permute-start.43 = (bf16[1,5,128,256]{3,2,1,0:T(8,128)(2,1)}, bf16[1,5,128,256]{3,2,1,0:T(8,128)(2,1)S(1)}, u32[]{:S(2)}, u32[]{:S(2)}) collective-permute-start(bf16[1,5,128,256]{3,2,1,0:T(8,128)(2,1)} %get-tuple-element.349), channel_id=1, source_target_pairs={{0,16},{4,20},{8,24},{12,28},{16,0},{20,4},{24,8},{28,12},{1,17},{... | collective-permute-start | bytes 983048 | tf_op jit(solution)/shard_map/ppermute | solution.py:113
  767.3 4.9 collective-permute-start.44
  772.1 5.7 collective-permute-start.45
  777.8 10.8 %collective-permute-start.42 = (bf16[2,3,128,256]{3,2,1,0:T(8,128)(2,1)}, bf16[2,3,128,256]{3,2,1,0:T(8,128)(2,1)S(1)}, u32[]{:S(2)}, u32[]{:S(2)}) collective-permute-start(bf16[2,3,128,256]{3,2,1,0:T(8,128)(2,1)} %get-tuple-element.346), channel_id=1, source_target_pairs={{0,8},{4,12},{8,0},{12,4},{16,24},{20,28},{24,16},{28,20},{1,9},{5... | collective-permute-start | bytes 1179656 | tf_op jit(solution)/shard_map/ppermute | solution.py:113
  793.6 13.5 %collective-permute-start.47 = (f32[28068]{0:T(1024)S(1)}, f32[28068]{0:T(1024)S(1)}, u32[]{:S(2)}, u32[]{:S(2)}) collective-permute-start(f32[28068]{0:T(1024)S(1)} %add.150), channel_id=1, source_target_pairs={{0,16},{4,20},{8,24},{12,28},{16,0},{20,4},{24,8},{28,12},{1,17},{... | collective-permute-start | bytes 336824 | tf_op jit(solution)/shard_map/ppermute | solution.py:987
  794.9 16.4 %collective-permute-start.46 = (bf16[1,3,128,256]{3,2,1,0:T(8,128)(2,1)}, bf16[1,3,128,256]{3,2,1,0:T(8,128)(2,1)S(1)}, u32[]{:S(2)}, u32[]{:S(2)}) collective-permute-start(bf16[1,3,128,256]{3,2,1,0:T(8,128)(2,1)} %get-tuple-element.361), channel_id=1, source_target_pairs={{0,16},{4,20},{8,24},{12,28},{16,0},{20,4},{24,8},{28,12},{1,17},{... | collective-permute-start | bytes 589832 | tf_op jit(solution)/shard_map/ppermute | solution.py:113
  (19 other events, 146.9 us)
Sparse Core Ops, SparseCore 0:
  10.9 103.3 all-gather.4
  117.7 131.2 all-gather.6
